TPU v7x, 32 devices: a whole 2x2x4 slice. The times are simulated.
32 devices in a mesh: ctx: 2 (over core), ep: 16 (over z, y, x).
Axes of the slice: x: 2, y: 2, z: 4, core: 2. Of those that a mesh axis runs over, the one named last changes fastest.
Arguments:
- queries: bfloat16 [4096, 2048], P(('ctx', 'ep')), may hold values from -40 to 40
- keys: bfloat16 [4096, 256], P(('ctx', 'ep')), may hold values from -40 to 40
- values: bfloat16 [4096, 256], P(('ctx', 'ep')), may hold values from -6 to 6
- prior_out: bfloat16 [4096, 2048], P(('ctx', 'ep')), may hold values from -6 to 6
- prior_lse: float32 [4096, 16], P(('ctx', 'ep')), may hold values from 4 to 8
- residual: bfloat16 [4096, 2048], P(('ctx', 'ep')), may hold values from -40 to 40
- out_proj: bfloat16 [2048, 2048], P(('ctx', 'ep')), may hold values from -0.25 to 0.25
- norm_gain: float32 [2048], replicated, may hold values from 0.5 to 1.5
- expert_in: bfloat16 [16, 2048, 1536], P('ep'), may hold values from -0.125 to 0.125
- expert_out: bfloat16 [16, 768, 2048], P('ep'), may hold values from -0.21875 to 0.21875
- expert_ids: int32 [4096, 8], P(('ctx', 'ep')), may hold values from 0 to 15, as said below
- route_weight: float32 [4096, 8], P(('ctx', 'ep')), may hold values from 0.05 to 0.6
Outputs:
- layer_out: bfloat16 [4096, 2048], P(('ctx', 'ep'))
- attended: bfloat16 [4096, 2048], P(('ctx', 'ep'))
Inputs may be any that keep to these rules, and one draw needn't show every extreme that they name: `expert_ids`: each row names 8 different experts. In the rows of one device no expert is named more than 72 times, and one expert is named exactly 72 times in the rows of every device.
All inputs are finite; a program needn't handle non-finite values.
Results may differ from a plain program's by a relative error of at most 0.0061.
Values may be sent and summed in bfloat16 or wider, within the bound.
No kernel may reach another device: no remote copies, remote signals or barrier semaphores. Data moves between devices by JAX's collectives and lax.ppermute only.
A program may use at most 128 MiB of HBM per device.

v0:
```python
import math

import jax
import jax.numpy as jnp
from jax import lax
from jax.sharding import PartitionSpec as P

HEADS = 16
KVH = 2
HD = 128
GROUP = 8


def passed_along(shard, axis, by):
    devices = lax.axis_size(axis)
    return lax.ppermute(shard, axis, [(i, (i + by) % devices) for i in range(devices)])


def run_expert(inputs, weight_in, weight_out, hidden_units):
    flat_in = inputs.reshape(-1, inputs.shape[-1])
    gate_up = jnp.dot(flat_in, weight_in, preferred_element_type=jnp.float32)
    activated = (jax.nn.silu(gate_up[:, :hidden_units]) * gate_up[:, hidden_units:]).astype(
        jnp.bfloat16
    )
    replies = jnp.dot(activated, weight_out, preferred_element_type=jnp.float32).astype(
        jnp.bfloat16
    )
    return replies.reshape(inputs.shape[:-1] + (weight_out.shape[-1],))


def shards(
    queries,
    keys,
    values,
    prior_out,
    prior_lse,
    residual,
    out_proj,
    norm_gain,
    expert_in,
    expert_out,
    expert_ids,
    route_weight,
):
    local_rows = queries.shape[0]
    ctx_count = lax.axis_size("ctx")
    ctx_here = lax.axis_index("ctx")
    ep_count = lax.axis_size("ep")
    reach_steps = min(2, ctx_count - 1)
    kv_pair = jnp.stack([keys, values])
    arrived = []
    current = kv_pair
    for stride in range(reach_steps):
        current = passed_along(current, "ctx", 1)
        arrived.append(current)
    window = jnp.concatenate(arrived, axis=1)
    width_kv = window.shape[1]
    key_win = window[0].reshape(width_kv, KVH, HD)
    value_win = window[1].reshape(width_kv, KVH, HD)
    query_blk = queries.reshape(local_rows, KVH, GROUP, HD)
    scores = jnp.einsum(
        "ighd,jgd->ghij", query_blk, key_win, preferred_element_type=jnp.float32
    ) / math.sqrt(HD)
    positions = jnp.arange(width_kv, dtype=jnp.int32)
    key_local = positions % local_rows
    key_ctx = (ctx_here - (positions // local_rows + 1)) % ctx_count
    query_local = jnp.arange(local_rows, dtype=jnp.int32)[:, None]
    visible = (key_local[None, :] < query_local) | (key_local[None, :] == query_local) & (
        key_ctx[None, :] <= ctx_here
    )
    scores = jnp.where(visible, scores, -jnp.inf)
    lse_prior = prior_lse.reshape(local_rows, KVH, GROUP).transpose(1, 2, 0)
    top_score = jnp.maximum(lse_prior, jnp.max(scores, axis=-1))
    weights = jnp.exp(scores - top_score[..., None])
    prior_weight = jnp.exp(lse_prior - top_score)
    totals = prior_weight + jnp.sum(weights, axis=-1)
    gathered = jnp.einsum(
        "ghij,jgd->ighd",
        weights.astype(jnp.bfloat16),
        value_win,
        preferred_element_type=jnp.float32,
    )
    prior_part = (
        prior_out.reshape(local_rows, KVH, GROUP, HD).astype(jnp.float32)
        * prior_weight.transpose(2, 0, 1)[..., None]
    )
    attended = ((prior_part + gathered) / totals.transpose(2, 0, 1)[..., None]).astype(jnp.bfloat16)
    attended = attended.reshape(local_rows, HEADS * HD)
    model_width = out_proj.shape[1]
    projected = jnp.dot(
        attended,
        lax.all_gather(out_proj, ("ctx", "ep"), axis=0, tiled=True),
        preferred_element_type=jnp.float32,
    )
    mixed_state = (residual.astype(jnp.float32) + projected).astype(jnp.bfloat16)
    state_f = lax.optimization_barrier(mixed_state).astype(jnp.float32)
    normed = (
        state_f * lax.rsqrt(jnp.mean(state_f * state_f, axis=-1, keepdims=True) + 1e-06) * norm_gain
    ).astype(jnp.bfloat16)
    experts_all = ep_count * expert_in.shape[0]
    top_count = expert_ids.shape[1]
    capacity = max(
        local_rows // 4, top_count * ((local_rows + experts_all - 2) // (experts_all - 1))
    )
    flat_ids = expert_ids.reshape(-1)
    one_hot = (flat_ids[:, None] == jnp.arange(experts_all, dtype=jnp.int32)[None, :]).astype(
        jnp.int32
    )
    earlier = jnp.cumsum(one_hot, axis=0) - one_hot
    slot_ids = flat_ids * capacity + jnp.sum(earlier * one_hot, axis=1)
    outgoing = jnp.zeros((experts_all * capacity, model_width), jnp.bfloat16)
    outgoing = (
        outgoing.at[slot_ids]
        .set(jnp.repeat(normed, top_count, axis=0))
        .reshape(experts_all, capacity, model_width)
    )
    weight_in = expert_in[0]
    weight_out = expert_out[0]
    hidden_units = weight_out.shape[0]
    replies = run_expert(
        lax.all_to_all(outgoing, "ep", split_axis=0, concat_axis=0, tiled=True),
        weight_in,
        weight_out,
        hidden_units,
    )
    returned = lax.all_to_all(replies, "ep", split_axis=0, concat_axis=0, tiled=True)
    picked = returned.reshape(experts_all * capacity, model_width)[slot_ids].reshape(
        local_rows, top_count, model_width
    )
    combined = jnp.sum(route_weight[:, :, None] * picked.astype(jnp.float32), axis=1)
    layer_out = (state_f + combined).astype(jnp.bfloat16)
    return (layer_out, attended)


def solution(mesh):
    return jax.shard_map(
        shards,
        mesh=mesh,
        in_specs=(
            P(("ctx", "ep"), None),
            P(("ctx", "ep"), None),
            P(("ctx", "ep"), None),
            P(("ctx", "ep"), None),
            P(("ctx", "ep"), None),
            P(("ctx", "ep"), None),
            P(("ctx", "ep"), None),
            P(),
            P("ep", None, None),
            P("ep", None, None),
            P(("ctx", "ep"), None),
            P(("ctx", "ep"), None),
        ),
        out_specs=(P(("ctx", "ep"), None), P(("ctx", "ep"), None)),
        check_vma=False,
    )
```

profile of v0, /device:TPU:14, one launch (start us, length us, event | category | flops | bytes accessed | tf_op | source)
XLA Modules:
  0.0 365.4 jit_solution(8171588519915162645)
XLA Ops:
  7.2 0.0 copy-start
  7.2 0.0 copy-start.3
  7.2 0.0 all-gather.2.cloned.1.call-start
  7.2 0.7 all-gather.2.cloned.1.call-update
  7.9 1.1 copy.23
  9.0 1.0 copy.24
  10.0 0.1 collective-permute-start
  10.1 0.8 copy.30
  10.9 0.1 eq.42
  11.0 0.7 eq.38
  11.6 1.9 copy.40
  13.6 2.3 copy.22
  15.9 4.5 %reduce-window.6 = s32[16,8,128]{2,1,0:T(8,128)S(1)} reduce-window(s32[16,8,128]{2,1,0:T(8,128)S(1)} %fusion.31, s32[]{:T(128)} %constant.58.clone.1), window={size=1x1x128 pad=0_0x0_0x127_0}, to_apply=%region_2.3 | reduce-window | flops 2080768 | bytes 131076 | tf_op jit(solution)/shard_map/reduce-window
  20.4 0.1 slice.28
  20.5 0.1 copy.32
  20.7 0.1 copy.33
  20.8 1.3 broadcast_multiply_fusion
  22.0 0.8 copy.29
  22.8 0.7 mul.66
  23.5 0.1 broadcast_add_fusion
  23.6 0.7 fusion.28
  24.3 0.1 fusion.29
  24.4 0.7 compare_select_fusion
  25.1 0.0 collective-permute-done
  25.2 1.4 fusion.40
  26.6 0.0 copy-done.3
  26.6 0.2 fusion.21
  26.8 2.4 fusion.16
  29.1 59.4 %all-gather.2.cloned.1.call-done = bf16[2048,2048]{1,0:T(8,128)(2,1)} async-done(((bf16[64,2048]{1,0:T(8,128)(2,1)}), bf16[2048,2048]{1,0:T(8,128)(2,1)}) %all-gather.2.cloned.1.call-update) | async-done | bytes 8388624 | tf_op jit(solution)/shard_map/all_gather | solution.py:92
  88.6 4.9 %fusion.7 = bf16[128,2048]{1,0:T(8,128)(2,1)S(1)} fusion(bf16[128,2048]{0,1:T(8,128)(2,1)} %bitcast.84, bf16[2048,2048]{1,0:T(8,128)(2,1)} %all-gather.2.cloned.1.call-done, bf16[128,2048]{1,0:T(8,128)(2,1)} %param.17), kind=kOutput, calls=%fused_computation.13 | convolution fusion | flops 1074528256 | bytes 9961472 | tf_op jit(solution)/shard_map/dot_general | solution.py:90
  93.5 0.0 copy-start.1
  93.5 0.2 fusion.17
  93.7 0.6 copy-done.1
  94.3 0.0 copy-done.4
  94.3 1.0 fusion.19
  95.2 9.8 %scatter_custom_fusion = bf16[1152,2048]{1,0:T(8,128)(2,1)} fusion(s32[1024]{0:T(1024)S(1)} %bitcast.96, bf16[]{:T(256)} %constant.69.clone.1, bf16[128,2048]{1,0:T(8,128)(2,1)} %fusion.19), kind=kCustom, calls=%fused_computation.7 | custom fusion | bytes 5242882 | tf_op jit(solution)/shard_map/scatter | solution.py:114
  105.0 108.8 %all_to_all.10 = bf16[16,72,2048]{2,1,0:T(8,128)(2,1)S(1)} all-to-all(bf16[16,72,2048]{2,1,0:T(8,128)(2,1)} %bitcast.81), channel_id=1, replica_groups=mesh['ctx'=2,'ep'=16] {'ep'}, dimensions={0} | all-to-all | bytes 9437184 | tf_op jit(solution)/shard_map/all_to_all | solution.py:121
  213.9 9.7 %fusion.1 = f32[1152,1536]{1,0:T(8,128)S(1)} fusion(bf16[1152,2048]{1,0:T(8,128)(2,1)S(1)} %bitcast.83, bf16[1,2048,1536]{2,1,0:T(8,128)(2,1)} %param.20), kind=kOutput, calls=%fused_computation.5 | convolution fusion | flops 7247757312 | bytes 18087936 | tf_op jit(solution)/shard_map/dot_general | solution.py:21
  223.5 0.0 copy-done
  223.5 5.6 %convolution_convert_fusion = bf16[1152,2048]{1,0:T(8,128)(2,1)} fusion(bf16[1,768,2048]{2,1,0:T(8,128)(2,1)S(1)} %copy-done, f32[1152,1536]{1,0:T(8,128)S(1)} %fusion.1), kind=kOutput, calls=%fused_computation.4 | convolution fusion | flops 3631546368 | bytes 14942208 | tf_op jit(solution)/shard_map/dot_general | solution.py:25
  229.2 6.6 %all-to-all-start.1 = ((bf16[16,72,2048]{2,1,0:T(8,128)(2,1)}), bf16[16,72,2048]{2,1,0:T(8,128)(2,1)}, u32[]{:S(2)}, u32[]{:S(2)}) async-start(bf16[16,72,2048]{2,1,0:T(8,128)(2,1)} %bitcast.82), calls=%async_computation.1 | async-start | bytes 9437184 | tf_op jit(solution)/shard_map/all_to_all | solution.py:126
  235.8 0.0 copy-done.5
  235.8 0.1 copy.28
  235.9 2.0 copy.34
  237.9 101.3 %all-to-all-done.1 = bf16[16,72,2048]{2,1,0:T(8,128)(2,1)} async-done(((bf16[16,72,2048]{2,1,0:T(8,128)(2,1)}), bf16[16,72,2048]{2,1,0:T(8,128)(2,1)}, u32[]{:S(2)}, u32[]{:S(2)}) %all-to-all-start.1) | async-done | bytes 4718624 | tf_op jit(solution)/shard_map/all_to_all | solution.py:126
  339.2 11.8 %gather_fusion = bf16[1024,2048]{1,0:T(8,128)(2,1)} fusion(bf16[1152,2048]{1,0:T(8,128)(2,1)} %bitcast.25, s32[1024]{0:T(1024)S(1)} %broadcast_clamp_fusion), kind=kCustom, calls=%fused_computation | custom fusion | bytes 8392704 | tf_op jit(solution)/shard_map/gather | solution.py:127
  351.0 6.6 %fusion = f32[128,2048]{1,0:T(8,128)S(1)} fusion(bf16[1024,2048]{1,0:T(8,128)(2,1)} %gather_fusion, f32[128,8]{1,0:T(8,128)S(1)} %copy.28), kind=kLoop, calls=%fused_computation.3 | loop fusion | flops 6029312 | bytes 5246976 | tf_op jit(solution)/shard_map/reduce_sum | solution.py:130
  357.6 0.9 fusion.20
  (15 shorter events, 0.1 us)
Async XLA Ops:
  7.2 216.4 %copy-start = (bf16[1,768,2048]{2,1,0:T(8,128)(2,1)S(1)}, bf16[1,768,2048]{2,1,0:T(8,128)(2,1)}, u32[]{:S(2)}) copy-start(bf16[1,768,2048]{2,1,0:T(8,128)(2,1)} %param.21) | copy-start | bytes 9437188
  7.2 19.4 %copy-start.3 = (f32[128,16]{0,1:T(8,128)S(1)}, f32[128,16]{0,1:T(8,128)}, u32[]{:S(2)}) copy-start(f32[128,16]{0,1:T(8,128)} %param.16) | copy-start | bytes 24580
  7.2 81.4 %all-gather.2.cloned.1.call-start = ((), (), s32[]{:S(2)}) async-start(), calls=%async_computation.2 | async-start | bytes 8650752 | tf_op jit(solution)/shard_map/all_gather | solution.py:92
  10.0 15.1 %collective-permute-start = (bf16[2,128,256]{1,2,0:T(8,128)(2,1)S(1)}, bf16[2,128,256]{1,2,0:T(8,128)(2,1)S(1)}, u32[]{:S(2)}, u32[]{:S(2)}) collective-permute-start(bf16[2,128,256]{1,2,0:T(8,128)(2,1)S(1)} %pad_maximum_fusion), channel_id=1, source_target_pairs={{0,16},{16,0},{1,17},{17,1},{2,18},{18,2},{3,19},{19,3},{4,20},{20... | collective-permute-start | bytes 393224 | tf_op jit(solution)/shard_map/ppermute | solution.py:16
  88.6 5.7 %copy-start.4 = (f32[2048]{0:T(1024)S(1)}, f32[2048]{0:T(1024)}, u32[]{:S(2)}) copy-start(f32[2048]{0:T(1024)} %param.19) | copy-start | bytes 24580
  93.5 0.8 copy-start.1
  229.2 6.6 %copy-start.5 = (f32[128,8]{0,1:T(8,128)S(1)}, f32[128,8]{0,1:T(8,128)}, u32[]{:S(2)}) copy-start(f32[128,8]{0,1:T(8,128)} %param.23) | copy-start | bytes 12292
  229.2 110.1 %all-to-all-start.1 = ((bf16[16,72,2048]{2,1,0:T(8,128)(2,1)}), bf16[16,72,2048]{2,1,0:T(8,128)(2,1)}, u32[]{:S(2)}, u32[]{:S(2)}) async-start(bf16[16,72,2048]{2,1,0:T(8,128)(2,1)} %bitcast.82), calls=%async_computation.1 | async-start | bytes 9437184 | tf_op jit(solution)/shard_map/all_to_all | solution.py:126
  351.0 6.6 %copy-start.2 = (bf16[128,2048]{1,0:T(8,128)(2,1)S(1)}, bf16[128,2048]{1,0:T(8,128)(2,1)}, u32[]{:S(2)}) copy-start(bf16[128,2048]{1,0:T(8,128)(2,1)} %copy-done.1) | copy-start | bytes 1572868
Sparse Core Ops, SparseCore 0:
  10.9 77.6 all-gather.1
where the time goes:
time: 366 us; the launch traced here: 365 us
  waiting for transfers between devices  161 us (44%)
  blocking collectives  109 us (30%)
  local copies, waits for them, and re-layouts  34 us (9%)
  matrix products  23.9 us (7%)
  other arithmetic  16.3 us (4%)
  between operations  14.2 us (4%)
  starting transfers between devices  6.7 us (2%)
    all_to_all x1, blocking collectives, shards(): lax.all_to_all(outgoing, 'ep', split_axis=0, concat_axis=0, tiled=True)  109 us
    all_to_all x1, waiting for transfers between devices, shards(): lax.all_to_all(replies, 'ep', split_axis=0, concat_axis=0, tiled=True)  101 us
    all_gather x1, waiting for transfers between devices, shards(): lax.all_gather(out_proj, ('ctx', 'ep'), axis=0, tiled=True)  59.4 us
    gather x1, local copies, waits for them, and re-layouts, shards(): returned.reshape(experts_all * capacity, model_width)[slot_ids]  11.8 us
    scatter x1, local copies, waits for them, and re-layouts, shards(): outgoing = outgoing.at[slot_ids].set(jnp.repeat(normed, top_count, axis=0...  9.76 us
    dot_general x1, matrix products, run_expert(): gate_up = jnp.dot(flat_in, weight_in, preferred_element_type=jnp.float32)  9.66 us
    unnamed x18, local copies, waits for them, and re-layouts  7.54 us
  transfers between devices with their start and end apart: 3, of which 2 were waited for; matrix products, arithmetic and copies ran while one was open for 6% of the time, Pallas kernels for 0%

commit v1 on v0

v1 whole, which is shorter than its diff:
```python
import functools
import math

import jax
import jax.numpy as jnp
from jax import lax
from jax.experimental import pallas as pl
from jax.experimental.pallas import tpu as pltpu
from jax.sharding import PartitionSpec as P

HEADS = 16
KVH = 2
HD = 128
GROUP = 8


def passed_along(shard, axis, by):
    devices = lax.axis_size(axis)
    return lax.ppermute(shard, axis, [(i, (i + by) % devices) for i in range(devices)])


def swapped(shard, axis, mask):
    devices = lax.axis_size(axis)
    return lax.ppermute(shard, axis, [(i, i ^ mask) for i in range(devices)])


def after(array, *others):
    return lax.optimization_barrier((array,) + others)[0]


WHOLE = pl.BlockSpec(memory_space=pltpu.VMEM)
ANYWHERE = pl.BlockSpec(memory_space=pl.ANY)
SCALARS = pl.BlockSpec(memory_space=pltpu.SMEM)
ROOM = pltpu.CompilerParams(vmem_limit_bytes=16 * 1024 * 1024)
LARGE = pltpu.CompilerParams(vmem_limit_bytes=30 * 1024 * 1024)
BRIEF = pl.CostEstimate(flops=0, bytes_accessed=0, transcendentals=0)


def local(kernel, out_shape, *operands, room=ROOM):
    return pl.pallas_call(
        kernel,
        out_shape=out_shape,
        in_specs=[WHOLE] * len(operands),
        out_specs=jax.tree.map(lambda _: WHOLE, out_shape),
        compiler_params=room,
        cost_estimate=BRIEF,
    )(*operands)


def attention_kernel(here, queries, keys, values, prior_out, prior_lse, mask, *outs, count):
    halves = HEADS // 2
    hidden = mask[...]
    scale = 1.0 / math.sqrt(HD)
    relative = len(outs) > 1
    turn = (here[1] & 1) != 0
    flip = here[1] // (count // halves) if relative else 0
    for side in range(2):
        group = here[0] ^ (1 - side) if relative else side
        shared = pl.ds(pl.multiple_of(group * HD, HD), HD)
        lse_rows = prior_lse[pl.ds(pl.multiple_of(group * halves, halves), halves), :]
        spans, weights, prior_rows, total_rows = [], [], [], []
        for i in range(halves):
            head = group * halves + (i ^ flip)
            span = pl.ds(pl.multiple_of(head * HD, HD), HD)
            scores = lax.dot_general(
                keys[:, shared],
                queries[:, span],
                (((1,), (1,)), ((), ())),
                preferred_element_type=jnp.float32,
            )
            scores = scores * scale + hidden
            lse = prior_lse[pl.ds(head, 1), :]
            top = jnp.maximum(lse, jnp.max(scores, axis=0, keepdims=True))
            part = jnp.exp(scores - top)
            prior_weight = jnp.exp(lse - top)
            inverse = 1.0 / (prior_weight + jnp.sum(part, axis=0, keepdims=True))
            spans.append(span)
            weights.append(part.astype(jnp.bfloat16))
            prior_rows.append(prior_weight * inverse)
            total_rows.append(inverse)
        rows = jnp.concatenate(prior_rows + total_rows, axis=0)
        fill = jnp.zeros((HD - rows.shape[0], rows.shape[1]), jnp.float32)
        rows = jnp.concatenate([rows, fill], axis=0).T
        for i in range(halves):
            gathered = lax.dot_general(
                weights[i],
                values[:, shared],
                (((0,), (0,)), ((), ())),
                preferred_element_type=jnp.float32,
            )
            prior_part = rows[:, i : i + 1] * prior_out[:, spans[i]].astype(jnp.float32)
            result = prior_part + rows[:, halves + i : halves + i + 1] * gathered
            outs[0][:, spans[i]] = result.astype(jnp.bfloat16)
            if relative:
                turned = pltpu.roll(result, HD // 2, 1)
                outs[1 + side][:, i * HD : (i + 1) * HD] = jnp.where(turn, turned, result).astype(
                    jnp.bfloat16
                )


def attention(queries, keys, values, prior_out, prior_lse, split):
    rows, width = queries.shape
    ctx_count = lax.axis_size("ctx")
    ctx_here = lax.axis_index("ctx")
    reach_steps = min(2, ctx_count - 1)
    windows = []
    for array in (keys, values):
        arrived = []
        for stride in range(reach_steps):
            array = passed_along(array, "ctx", 1)
            arrived.append(array)
        windows.append(arrived[0] if reach_steps == 1 else jnp.concatenate(arrived, axis=0))
    positions = jnp.arange(reach_steps * rows, dtype=jnp.int32)[:, None]
    key_local = positions % rows
    key_ctx = (ctx_here - (positions // rows + 1)) % ctx_count
    query_local = jnp.arange(rows, dtype=jnp.int32)[None, :]
    visible = (key_local < query_local) | (key_local == query_local) & (key_ctx <= ctx_here)
    mask = jnp.where(visible, 0.0, -jnp.inf).astype(jnp.float32)
    here = jnp.stack([ctx_here, lax.axis_index("ep")]).astype(jnp.int32)
    shapes = [jax.ShapeDtypeStruct((rows, width), jnp.bfloat16)]
    if split:
        shapes += [jax.ShapeDtypeStruct((rows, width // 2), jnp.bfloat16)] * 2
    return pl.pallas_call(
        functools.partial(attention_kernel, count=lax.axis_size("ep")),
        out_shape=shapes,
        in_specs=[SCALARS] + [WHOLE] * 6,
        out_specs=[WHOLE] * len(shapes),
        compiler_params=ROOM,
        cost_estimate=BRIEF,
    )(here, queries, *windows, prior_out, prior_lse.T, mask)


WEIGHT_STEPS = (
    (8, 8),
    (2, 2),
    (1, 1),
    (4, 4),
    (12, 4),
    (None, 4),
    (10, 2),
    (9, 1),
    (None, 8),
    (3, 2),
    (5, 1),
    (None, 1),
    (14, 2),
    (6, 2),
    (None, 2),
    (13, 1),
    (11, 1),
    (7, 2),
    (15, 1),
)


def weight_planes(shard, picks, token):
    blocks = {0: shard}
    masks = [0]
    for mask, bit in WEIGHT_STEPS:
        if mask is None:
            token = after(swapped(picks, "ep", bit), token)
            picks = jnp.concatenate([picks, token], axis=0)
            masks = masks + [m | bit for m in masks]
        else:
            token = after(swapped(blocks[mask ^ bit], "ep", bit), token)
            blocks[mask] = token
    return [(m, [blocks[m + i] for i in range(4)]) for m in range(0, 16, 4)], picks, masks


def product_kernel(*refs, spans):
    lhs, blocks = refs[:2], refs[2 : 2 + 4 * len(spans)]
    outs, weight, sems = refs[2 + 4 * len(spans) : -2], refs[-2], refs[-1]
    rows, width = blocks[0].shape
    copies = []
    for i, block in enumerate(blocks):
        place = weight.at[pl.ds(i * rows, rows), :]
        copies.append(pltpu.make_async_copy(block, place, sems.at[i]))
        copies[-1].start()
    tile = min(width, 512)
    for i, span in enumerate(spans):
        for copy in copies[4 * i : 4 * i + 4]:
            copy.wait()
        left = jnp.concatenate([side[:, span] for side in lhs], axis=0)
        half = left.shape[0] // 2
        for start in range(0, width, tile):
            columns = slice(start, start + tile)
            term = jnp.dot(
                left,
                weight[4 * i * rows : 4 * (i + 1) * rows, columns],
                preferred_element_type=jnp.float32,
            )
            for out, part in zip(outs, (term[:half], term[half:])):
                out[:, columns] = part if i == 0 else out[:, columns] + part


def product(lhs, planes, rows):
    spans = [slice(mask * rows, (mask + 4) * rows) for mask, _ in planes]
    blocks = [block for _, plane in planes for block in plane]
    width = blocks[0].shape[1]
    shape = jax.ShapeDtypeStruct((lhs[0].shape[0], width), jnp.float32)
    return pl.pallas_call(
        functools.partial(product_kernel, spans=spans),
        out_shape=[shape] * 2,
        in_specs=[WHOLE] * 2 + [ANYWHERE] * len(blocks),
        out_specs=[WHOLE] * 2,
        scratch_shapes=[
            pltpu.VMEM((len(blocks) * rows, width), jnp.bfloat16),
            pltpu.SemaphoreType.DMA((len(blocks),)),
        ],
        compiler_params=ROOM,
        cost_estimate=BRIEF,
    )(*lhs, *blocks)


def norm_kernel(own, heard, residual, gain, pack, state, left, right, packed):
    mixed = (residual[...].astype(jnp.float32) + (own[...] + heard[...])).astype(jnp.bfloat16)
    state[...] = mixed
    mixed = mixed.astype(jnp.float32)
    scale = lax.rsqrt(jnp.mean(mixed * mixed, axis=1, keepdims=True) + 1e-06)
    rows = (mixed * scale * gain[...]).astype(jnp.bfloat16)
    middle = left.shape[1]
    left[...] = rows[:, :middle]
    right[...] = rows[:, middle:]
    packed[...] = jnp.dot(pack[0], rows, preferred_element_type=jnp.float32).astype(jnp.bfloat16)


def norm(own, heard, residual, gain, pack):
    rows, width = residual.shape
    half = jax.ShapeDtypeStruct((rows, width // 2), jnp.bfloat16)
    packed = jax.ShapeDtypeStruct((pack.shape[1], width), jnp.bfloat16)
    return local(
        norm_kernel,
        [jax.ShapeDtypeStruct(residual.shape, jnp.bfloat16), half, half, packed],
        own,
        heard,
        residual,
        gain.reshape(1, -1),
        pack,
    )


def routing_kernel(here, picks, pack, row_weight, *, masks):
    blocks, capacity, rows = pack.shape
    count, twice, _ = picks.shape
    ids, weights = picks[:, : twice // 2, :], picks[:, twice // 2 :, :]
    before = lax.broadcasted_iota(jnp.int32, (rows, rows), 0)
    behind = lax.broadcasted_iota(jnp.int32, (rows, rows), 1)
    earlier = jnp.where(before < behind, 1.0, 0.0).astype(jnp.bfloat16)
    places = lax.broadcasted_iota(jnp.int32, (capacity, rows), 0).astype(jnp.float32)

    def chosen(expert):
        hits = ids == expert.astype(jnp.float32)
        named = jnp.sum(jnp.where(hits, 1.0, 0.0), axis=1)
        slot = jnp.dot(named.astype(jnp.bfloat16), earlier, preferred_element_type=jnp.float32)
        return jnp.where(named > 0.0, slot, -1.0), jnp.sum(jnp.where(hits, weights, 0.0), axis=1)

    own_slot, own_weight = chosen(here[0])
    other_slot, _ = chosen(here[0] ^ 1)
    for m in range(blocks):
        same, other = masks.index(2 * m), masks.index(2 * m + 1)
        pack[m] = jnp.where(other_slot[same : same + 1] == places, 1.0, 0.0).astype(jnp.bfloat16)
        row = (m % 2) * rows
        row_weight[m // 2, row : row + rows, :] = jnp.sum(
            jnp.where(before == behind, own_weight[same : same + 1], 0.0), axis=1, keepdims=True
        )
        row = 2 * rows + (m % 2) * capacity
        row_weight[m // 2, row : row + capacity, :] = jnp.sum(
            jnp.where(
                own_slot[other : other + 1] == places, own_weight[other : other + 1], 0.0
            ),
            axis=1,
            keepdims=True,
        )


def own_picks(expert_ids, route_weight):
    return jnp.concatenate([expert_ids.T.astype(jnp.float32), route_weight.T], axis=0)[None]


def all_picks(picks):
    ep_count = lax.axis_size("ep")
    masks, bit = [0], 1
    while bit < ep_count:
        picks = jnp.concatenate([picks, swapped(picks, "ep", bit)], axis=0)
        masks = masks + [mask | bit for mask in masks]
        bit *= 2
    return picks, masks


def routing(picks, masks, capacity):
    count, _, rows = picks.shape
    return pl.pallas_call(
        functools.partial(routing_kernel, masks=masks),
        out_shape=[
            jax.ShapeDtypeStruct((count // 2, capacity, rows), jnp.bfloat16),
            jax.ShapeDtypeStruct((count // 4, 2 * rows + 2 * capacity, 1), jnp.float32),
        ],
        in_specs=[SCALARS, WHOLE],
        out_specs=[WHOLE] * 2,
        compiler_params=ROOM,
        cost_estimate=BRIEF,
    )(lax.axis_index("ep").astype(jnp.int32).reshape(1), picks)


def pack_kernel(index, pack, left, right, out):
    chosen = pack[index]
    middle = left.shape[1]
    for start, half in ((0, left), (middle, right)):
        rows = jnp.dot(chosen, half[...], preferred_element_type=jnp.float32)
        out[:, start : start + middle] = rows.astype(jnp.bfloat16)


def expert_kernel(*refs):
    near_left, near_right, far_left, far_right, near_packed, far_packed = refs[:6]
    row_weight, weight_in, weight_out, whole, near_out, far_out = refs[6:]
    near = jnp.concatenate([near_left[...], near_right[...]], axis=1)
    far = jnp.concatenate([far_left[...], far_right[...]], axis=1)
    packed = jnp.concatenate(
        [near_packed[...].astype(jnp.float32), far_packed[...].astype(jnp.float32)], axis=0
    ).astype(jnp.bfloat16)
    rows = jnp.concatenate([near, far, packed], axis=0)
    hidden_units, width = weight_out.shape
    tile = 256
    activated = []
    for start in range(0, hidden_units, tile):
        gate = jnp.dot(
            rows, weight_in[:, start : start + tile], preferred_element_type=jnp.float32
        )
        start += hidden_units
        up = jnp.dot(rows, weight_in[:, start : start + tile], preferred_element_type=jnp.float32)
        scaled = gate / (1.0 + jnp.exp(-gate)) * up * row_weight[...]
        activated.append(scaled.astype(jnp.bfloat16))
    activated = jnp.concatenate(activated, axis=1)
    count, capacity = whole.shape[0], near_out.shape[0]
    for start in range(0, width, tile):
        columns = slice(start, start + tile)
        reply = jnp.dot(activated, weight_out[:, columns], preferred_element_type=jnp.float32)
        whole[:, columns] = reply[:count]
        near_out[:, columns] = reply[count : count + capacity].astype(jnp.bfloat16)
        far_out[:, columns] = reply[count + capacity :].astype(jnp.bfloat16)


def unpack_kernel(index, far, pack, whole, returned, *outs):
    rows = pack.shape[2]
    total = lax.dot_general(
        pack[index],
        returned[...],
        (((0,), (0,)), ((), ())),
        preferred_element_type=jnp.float32,
    )
    total = total + whole[rows * far : rows * (far + 1), :]
    middle = outs[0].shape[1]
    for i, out in enumerate(outs):
        out[...] = total[:, i * middle : (i + 1) * middle].astype(out.dtype)


def final_kernel(state, *refs):
    parts, out = refs[:-1], refs[-1]
    middle = parts[0].shape[1]
    for i in range(2):
        columns = slice(i * middle, (i + 1) * middle)
        total = parts[i][...].astype(jnp.float32)
        for part in parts[2 + i :: 2]:
            total = total + part[...].astype(jnp.float32)
        out[:, columns] = (state[:, columns].astype(jnp.float32) + total).astype(jnp.bfloat16)


STEPS = (
    ("block", 2, 0),
    ("packed", 0),
    ("block", 2, 1),
    ("pack", 2),
    ("block", 4, 0),
    ("block", 8, 0),
    ("block", 4, 1),
    ("pack", 4),
    ("block", 8, 1),
    ("pack", 8),
    ("packed", 2),
    ("block", 6, 0),
    ("block", 12, 0),
    ("block", 10, 0),
    ("block", 6, 1),
    ("block", 12, 1),
    ("pack", 12),
    ("block", 14, 0),
    ("block", 10, 1),
    ("pack", 10),
    ("packed", 4),
    ("packed", 8),
    ("block", 14, 1),
    ("pack", 14),
    ("pack", 6),
    ("packed", 12),
    ("packed", 10),
    ("reply", 0),
    ("packed", 14),
)


def plain_steps(count):
    steps = []
    for mask in sorted(range(2, count, 2), key=lambda m: (m.bit_count(), m & 2, m)):
        steps += [("block", mask, 0), ("block", mask, 1), ("pack", mask)]
    return steps


def experts_sum(state, halves, packed, pack, row_weight, weight_in, weight_out):
    ep_count = lax.axis_size("ep")
    rows, width = state.shape
    capacity = pack.shape[1]
    half = (rows, width // 2)
    packed_shape = jax.ShapeDtypeStruct((capacity, width), jnp.bfloat16)
    blocks, arrived = {0: halves}, {0: swapped(packed, "ep", 1)}
    replies, returned = {}, {}
    token = packed

    def receive(mask, side):
        nonlocal token
        bit = mask & -mask
        token = after(swapped(blocks[mask ^ bit][side], "ep", bit), token)
        blocks.setdefault(mask, [None, None])[side] = token

    def send_packed(mask):
        nonlocal token
        token = local(
            functools.partial(pack_kernel, mask // 2),
            packed_shape,
            pack,
            blocks[mask][0],
            after(blocks[mask][1], token),
        )
        arrived[mask] = swapped(token, "ep", 1)

    def reply_to(mask):
        nonlocal token
        whole = jax.ShapeDtypeStruct((2 * rows, width), jnp.float32)
        replies[mask] = local(
            expert_kernel,
            [whole, packed_shape, packed_shape],
            after(blocks[mask][0], token),
            blocks[mask][1],
            *blocks[mask | 2],
            arrived[mask],
            arrived[mask | 2],
            row_weight[mask // 4],
            weight_in,
            weight_out,
            room=LARGE,
        )
        token = replies[mask][1]

    steps = STEPS if ep_count == 16 else plain_steps(ep_count)
    for kind, mask, *side in steps:
        if kind == "block":
            receive(mask, *side)
        elif kind == "pack":
            send_packed(mask)
        elif kind == "reply":
            reply_to(mask)
        else:
            token = arrived[mask] = after(arrived[mask], token)
    far = sorted(mask for mask in blocks if mask and not mask & 2)
    backward = [far[-1], far[-2]] + far[:-2][::-1] + [0]
    received = {mask: ([], []) for mask in backward}
    sums = {}

    def send_replies(mask):
        nonlocal token
        if mask not in replies:
            reply_to(mask)
        for far_side in (1, 0):
            token = after(replies[mask][1 + far_side], token)
            returned[mask | 2 * far_side] = swapped(token, "ep", 1)

    def unpack(mask):
        nonlocal token
        far_side = mask // 2 % 2
        kind = jnp.bfloat16 if far_side else jnp.float32
        outs = local(
            functools.partial(unpack_kernel, mask // 2, far_side),
            [jax.ShapeDtypeStruct(half, kind)] * 2,
            pack,
            replies[mask & ~2][0],
            after(returned[mask], token),
        )
        token = outs[0]
        if far_side:
            for side, out in enumerate(outs):
                received[mask & ~2][side].append(swapped(out, "ep", 2))
        else:
            sums[mask] = outs

    def pass_on(mask, side):
        nonlocal token
        total = sums[mask][side]
        for part in received[mask][side]:
            total = total + after(part, token).astype(jnp.float32)
        token = total.astype(jnp.bfloat16)
        bit = mask & -mask
        received[mask ^ bit][side].append(swapped(token, "ep", bit))

    for mask in backward[:2]:
        send_replies(mask)
    unpack(backward[0] | 2)
    for mask in backward[2:]:
        send_replies(mask)
    for k, mask in enumerate(backward):
        if k:
            unpack(mask | 2)
            pass_on(backward[k - 1], 0)
        if mask:
            unpack(mask)
        if k:
            pass_on(backward[k - 1], 1)
    unpack(0)
    parts = [part for pair in zip(*received[0]) for part in pair]
    shape = jax.ShapeDtypeStruct(state.shape, jnp.bfloat16)
    return local(final_kernel, shape, state, *sums[0], *parts)


def shards(
    queries,
    keys,
    values,
    prior_out,
    prior_lse,
    residual,
    out_proj,
    norm_gain,
    expert_in,
    expert_out,
    expert_ids,
    route_weight,
):
    local_rows = queries.shape[0]
    experts_all = lax.axis_size("ep") * expert_in.shape[0]
    top_count = expert_ids.shape[1]
    capacity = max(
        local_rows // 4, top_count * ((local_rows + experts_all - 2) // (experts_all - 1))
    )
    ep_count = lax.axis_size("ep")
    split = (
        lax.axis_size("ctx") == 2
        and out_proj.shape[0] * ep_count == HEADS // 2 * HD
        and 2 * out_proj.shape[0] == HD
    )
    picks = own_picks(expert_ids, route_weight)
    results = attention(queries, keys, values, prior_out, prior_lse, split)
    attended = results[0]
    if split:
        rows = out_proj.shape[0]
        given, kept = results[1:]
        sibling = swapped(given, "ctx", 1)
        planes, picks, masks = weight_planes(out_proj, picks, given)
        given_sum, own_sum = product([sibling, kept], planes, rows)
        heard_sum = swapped(given_sum, "ctx", 1)
    else:
        picks, masks = all_picks(picks)
        full = lax.all_gather(out_proj, ("ctx", "ep"), axis=0, tiled=True)
        own_sum = jnp.dot(attended, full, preferred_element_type=jnp.float32)
        heard_sum = jnp.zeros_like(own_sum)
    pack, row_weight = routing(picks, masks, capacity)
    state, left, right, packed = norm(own_sum, heard_sum, residual, norm_gain, pack)
    layer_out = experts_sum(
        state, [left, right], packed, pack, row_weight, expert_in[0], expert_out[0]
    )
    return (layer_out, attended)


def solution(mesh):
    return jax.shard_map(
        shards,
        mesh=mesh,
        in_specs=(
            P(("ctx", "ep"), None),
            P(("ctx", "ep"), None),
            P(("ctx", "ep"), None),
            P(("ctx", "ep"), None),
            P(("ctx", "ep"), None),
            P(("ctx", "ep"), None),
            P(("ctx", "ep"), None),
            P(),
            P("ep", None, None),
            P("ep", None, None),
            P(("ctx", "ep"), None),
            P(("ctx", "ep"), None),
        ),
        out_specs=(P(("ctx", "ep"), None), P(("ctx", "ep"), None)),
        check_vma=False,
    )
```

time: 366 us -> 208 us (0.57)
  the two profiles are of different devices: /device:TPU:14 before, /device:TPU:0 now
where the time goes in v1:
time: 208 us
  waiting for transfers between devices  96.3 us (46%)
  starting transfers between devices  76.6 us (37%)
  Pallas kernels  27.9 us (13%)
  local copies, waits for them, and re-layouts  3.83 us (2%)
    ppermute x65, waiting for transfers between devices, swapped(): return lax.ppermute(shard, axis, [(i, i ^ mask) for i in range(devices)])  95.5 us
    ppermute x65, starting transfers between devices, swapped(): return lax.ppermute(shard, axis, [(i, i ^ mask) for i in range(devices)])  76.1 us
    pallas_call x21, Pallas kernels, local(): pl.pallas_call(kernel, out_shape=out_shape, in_specs=[WHOLE] * len(operan...  22.1 us
  transfers between devices with their start and end apart: 67, of which 33 were waited for; matrix products, arithmetic and copies ran while one was open for 1% of the time, Pallas kernels for 10%

profile of v1, /device:TPU:0, one launch (start us, length us, event | category | flops | bytes accessed | tf_op | source)
XLA Modules:
  0.0 207.6 jit_solution(9583337885900266517)
XLA Ops:
  0.6 4.1 %collective-permute-start.5 = (bf16[64,2048]{1,0:T(8,128)(2,1)}, bf16[64,2048]{1,0:T(8,128)(2,1)S(1)}, u32[]{:S(2)}, u32[]{:S(2)}) collective-permute-start(bf16[64,2048]{1,0:T(8,128)(2,1)} %refs_2_.1), channel_id=1, source_target_pairs={{0,8},{1,9},{2,10},{3,11},{4,12},{5,13},{6,14},{7,15},{8,0},{9,1},... | collective-permute-start | bytes 786440 | tf_op jit(solution)/shard_map/ppermute | solution.py:24
  4.7 1.5 collective-permute-start.4
  6.3 1.5 collective-permute-start.3
  9.2 1.6 collective-permute-start.9
  13.6 3.4 %shard_map.131 = (bf16[128,2048]{1,0:T(8,128)(2,1)}, bf16[128,1024]{1,0:T(8,128)(2,1)S(1)}, bf16[128,1024]{1,0:T(8,128)(2,1)S(1)}) custom-call(s32[2]{0:T(128)S(1)} %pad_add_fusion.here, bf16[128,2048]{1,0:T(8,128)(2,1)S(1)} %copy-done.1, bf16[128,256]{1,0:T(8,128)(2,1)S(1)} %collective-permute-done.keys, ...), custom_call_target="tpu_custom_call" | custom-call | tf_op jit(solution)/shard_map/pallas_call | solution.py:123
  17.0 1.6 collective-permute-start.12
  18.5 1.5 collective-permute-start.11
  24.0 4.0 %collective-permute-done.8.refs_14_ = bf16[64,2048]{1,0:T(8,128)(2,1)S(1)} collective-permute-done((bf16[64,2048]{1,0:T(8,128)(2,1)S(1)}, bf16[64,2048]{1,0:T(8,128)(2,1)S(1)}, u32[]{:S(2)}, u32[]{:S(2)}) %collective-permute-start.8) | collective-permute-done | bytes 262176 | tf_op jit(solution)/shard_map/ppermute | solution.py:24
  28.5 2.0 collective-permute-start.10
  31.1 1.5 collective-permute-start.15
  33.2 1.4 collective-permute-start.16
  35.1 2.3 %collective-permute-done.16 = f32[4,16,128]{2,1,0:T(8,128)S(1)} collective-permute-done((f32[4,16,128]{2,1,0:T(8,128)S(1)}, f32[4,16,128]{2,1,0:T(8,128)S(1)}, u32[]{:S(2)}, u32[]{:S(2)}) %collective-permute-start.16) | collective-permute-done | bytes 32800 | tf_op jit(solution)/shard_map/ppermute | solution.py:24
  37.7 1.5 collective-permute-start.19
  39.7 4.4 %collective-permute-done.15.refs_16_ = bf16[64,2048]{1,0:T(8,128)(2,1)S(1)} collective-permute-done((bf16[64,2048]{1,0:T(8,128)(2,1)S(1)}, bf16[64,2048]{1,0:T(8,128)(2,1)S(1)}, u32[]{:S(2)}, u32[]{:S(2)}) %collective-permute-start.15) | collective-permute-done | bytes 262176 | tf_op jit(solution)/shard_map/ppermute | solution.py:24
  44.6 1.5 collective-permute-start.21
  46.9 4.2 %collective-permute-done.18.refs_13_ = bf16[64,2048]{1,0:T(8,128)(2,1)S(1)} collective-permute-done((bf16[64,2048]{1,0:T(8,128)(2,1)S(1)}, bf16[64,2048]{1,0:T(8,128)(2,1)S(1)}, u32[]{:S(2)}, u32[]{:S(2)}) %collective-permute-start.18) | collective-permute-done | bytes 262176 | tf_op jit(solution)/shard_map/ppermute | solution.py:24
  51.1 2.8 %collective-permute-done.21.refs_17_ = bf16[64,2048]{1,0:T(8,128)(2,1)S(1)} collective-permute-done((bf16[64,2048]{1,0:T(8,128)(2,1)S(1)}, bf16[64,2048]{1,0:T(8,128)(2,1)S(1)}, u32[]{:S(2)}, u32[]{:S(2)}) %collective-permute-start.21) | collective-permute-done | bytes 262176 | tf_op jit(solution)/shard_map/ppermute | solution.py:24
  54.9 2.0 shard_map.132
  57.5 2.2 %collective-permute-done.22.heard = f32[128,2048]{1,0:T(8,128)S(1)} collective-permute-done((f32[128,2048]{1,0:T(8,128)S(1)}, f32[128,2048]{1,0:T(8,128)S(1)}, u32[]{:S(2)}, u32[]{:S(2)}) %collective-permute-start.22) | collective-permute-done | bytes 1048608 | tf_op jit(solution)/shard_map/ppermute | solution.py:24
  60.2 1.5 collective-permute-start.27
  64.4 3.2 %collective-permute-start.23 = (bf16[128,1024]{1,0:T(8,128)(2,1)S(1)}, bf16[128,1024]{1,0:T(8,128)(2,1)S(1)}, u32[]{:S(2)}, u32[]{:S(2)}) collective-permute-start(bf16[128,1024]{1,0:T(8,128)(2,1)S(1)} %get-tuple-element.171.refs_0_), channel_id=1, source_target_pairs={{0,8},{1,9},{2,10},{3,11},{4,12},{5,13},{6,14},{7,15},{8,0},{9,1},... | collective-permute-start | bytes 786440 | tf_op jit(solution)/shard_map/ppermute | solution.py:24
  67.6 3.4 %collective-permute-done.25.left.refs_2_ = bf16[128,1024]{1,0:T(8,128)(2,1)S(1)} collective-permute-done((bf16[128,1024]{1,0:T(8,128)(2,1)S(1)}, bf16[128,1024]{1,0:T(8,128)(2,1)S(1)}, u32[]{:S(2)}, u32[]{:S(2)}) %collective-permute-start.25) | collective-permute-done | bytes 262176 | tf_op jit(solution)/shard_map/ppermute | solution.py:24
  71.5 3.2 %collective-permute-start.32 = (bf16[128,1024]{1,0:T(8,128)(2,1)S(1)}, bf16[128,1024]{1,0:T(8,128)(2,1)S(1)}, u32[]{:S(2)}, u32[]{:S(2)}) collective-permute-start(bf16[128,1024]{1,0:T(8,128)(2,1)S(1)} %get-tuple-element.144.refs_1_), channel_id=1, source_target_pairs={{0,8},{1,9},{2,10},{3,11},{4,12},{5,13},{6,14},{7,15},{8,0},{9,1},... | collective-permute-start | bytes 786440 | tf_op jit(solution)/shard_map/ppermute | solution.py:24
  75.7 4.4 %collective-permute-done.24.left.refs_0_ = bf16[128,1024]{1,0:T(8,128)(2,1)S(1)} collective-permute-done((bf16[128,1024]{1,0:T(8,128)(2,1)S(1)}, bf16[128,1024]{1,0:T(8,128)(2,1)S(1)}, u32[]{:S(2)}, u32[]{:S(2)}) %collective-permute-start.24) | collective-permute-done | bytes 262176 | tf_op jit(solution)/shard_map/ppermute | solution.py:24
  82.7 7.2 %collective-permute-done.33.right.refs_1_ = bf16[128,1024]{1,0:T(8,128)(2,1)S(1)} collective-permute-done((bf16[128,1024]{1,0:T(8,128)(2,1)S(1)}, bf16[128,1024]{1,0:T(8,128)(2,1)S(1)}, u32[]{:S(2)}, u32[]{:S(2)}) %collective-permute-start.33) | collective-permute-done | bytes 262176 | tf_op jit(solution)/shard_map/ppermute | solution.py:24
  92.1 1.6 collective-permute-done.29.left.refs_0_
  99.1 4.2 %collective-permute-done.28.left.refs_2_ = bf16[128,1024]{1,0:T(8,128)(2,1)S(1)} collective-permute-done((bf16[128,1024]{1,0:T(8,128)(2,1)S(1)}, bf16[128,1024]{1,0:T(8,128)(2,1)S(1)}, u32[]{:S(2)}, u32[]{:S(2)}) %collective-permute-start.28) | collective-permute-done | bytes 262176 | tf_op jit(solution)/shard_map/ppermute | solution.py:24
  105.6 3.3 %collective-permute-done.35.left.refs_2_ = bf16[128,1024]{1,0:T(8,128)(2,1)S(1)} collective-permute-done((bf16[128,1024]{1,0:T(8,128)(2,1)S(1)}, bf16[128,1024]{1,0:T(8,128)(2,1)S(1)}, u32[]{:S(2)}, u32[]{:S(2)}) %collective-permute-start.35) | collective-permute-done | bytes 262176 | tf_op jit(solution)/shard_map/ppermute | solution.py:24
  108.9 5.3 %collective-permute-done.34.right.refs_3_ = bf16[128,1024]{1,0:T(8,128)(2,1)S(1)} collective-permute-done((bf16[128,1024]{1,0:T(8,128)(2,1)S(1)}, bf16[128,1024]{1,0:T(8,128)(2,1)S(1)}, u32[]{:S(2)}, u32[]{:S(2)}) %collective-permute-start.34) | collective-permute-done | bytes 262176 | tf_op jit(solution)/shard_map/ppermute | solution.py:24
  114.8 2.2 %collective-permute-done.40.right.refs_3_ = bf16[128,1024]{1,0:T(8,128)(2,1)S(1)} collective-permute-done((bf16[128,1024]{1,0:T(8,128)(2,1)S(1)}, bf16[128,1024]{1,0:T(8,128)(2,1)S(1)}, u32[]{:S(2)}, u32[]{:S(2)}) %collective-permute-start.40) | collective-permute-done | bytes 262176 | tf_op jit(solution)/shard_map/ppermute | solution.py:24
  118.2 5.7 %collective-permute-done.38.refs_5_ = bf16[72,2048]{1,0:T(8,128)(2,1)S(1)} collective-permute-done((bf16[72,2048]{1,0:T(8,128)(2,1)S(1)}, bf16[72,2048]{1,0:T(8,128)(2,1)S(1)}, u32[]{:S(2)}, u32[]{:S(2)}) %collective-permute-start.38) | collective-permute-done | bytes 294944 | tf_op jit(solution)/shard_map/ppermute | solution.py:24
  123.9 4.0 %shard_map.142 = (f32[256,2048]{1,0:T(8,128)S(1)}, bf16[72,2048]{1,0:T(8,128)(2,1)S(1)}, bf16[72,2048]{1,0:T(8,128)(2,1)S(1)}) custom-call(bf16[128,1024]{1,0:T(8,128)(2,1)S(1)} %get-tuple-element.171.refs_0_, bf16[128,1024]{1,0:T(8,128)(2,1)S(1)} %get-tuple-element.144.refs_1_, bf16[128,1024]{1,0:T(8,128)(2,1)S(1)} %collective-permute-done.25.left.refs_2_, ...), custom_call_target="tpu_custom_call" | custom-call | tf_op jit(solution)/shard_map/pallas_call | solution.py:40
  127.9 4.0 %shard_map.143 = (f32[256,2048]{1,0:T(8,128)S(1)}, bf16[72,2048]{1,0:T(8,128)(2,1)S(1)}, bf16[72,2048]{1,0:T(8,128)(2,1)S(1)}) custom-call(bf16[128,1024]{1,0:T(8,128)(2,1)S(1)} %collective-permute-done.29.left.refs_0_, bf16[128,1024]{1,0:T(8,128)(2,1)S(1)} %collective-permute-done.36.right.refs_1_, ...), custom_call_target="tpu_custom_call" | custom-call | tf_op jit(solution)/shard_map/pallas_call | solution.py:40
  135.2 4.2 %shard_map.144 = (f32[256,2048]{1,0:T(8,128)S(1)}, bf16[72,2048]{1,0:T(8,128)(2,1)S(1)}, bf16[72,2048]{1,0:T(8,128)(2,1)S(1)}) custom-call(bf16[128,1024]{1,0:T(8,128)(2,1)S(1)} %collective-permute-done.23.left.refs_0_, bf16[128,1024]{1,0:T(8,128)(2,1)S(1)} %collective-permute-done.32.right.refs_1_, ...), custom_call_target="tpu_custom_call" | custom-call | tf_op jit(solution)/shard_map/pallas_call | solution.py:40
  140.4 1.6 collective-permute-done.44.returned
  144.7 3.5 %collective-permute-done.45.refs_5_ = bf16[72,2048]{1,0:T(8,128)(2,1)S(1)} collective-permute-done((bf16[72,2048]{1,0:T(8,128)(2,1)S(1)}, bf16[72,2048]{1,0:T(8,128)(2,1)S(1)}, u32[]{:S(2)}, u32[]{:S(2)}) %collective-permute-start.45) | collective-permute-done | bytes 294944 | tf_op jit(solution)/shard_map/ppermute | solution.py:24
  149.4 4.0 %shard_map.146 = (f32[256,2048]{1,0:T(8,128)S(1)}, bf16[72,2048]{1,0:T(8,128)(2,1)S(1)}, bf16[72,2048]{1,0:T(8,128)(2,1)S(1)}) custom-call(bf16[128,1024]{1,0:T(8,128)(2,1)S(1)} %collective-permute-done.24.left.refs_0_, bf16[128,1024]{1,0:T(8,128)(2,1)S(1)} %collective-permute-done.33.right.refs_1_, ...), custom_call_target="tpu_custom_call" | custom-call | tf_op jit(solution)/shard_map/pallas_call | solution.py:40
  156.1 4.8 %collective-permute-done.51.returned = bf16[72,2048]{1,0:T(8,128)(2,1)S(1)} collective-permute-done((bf16[72,2048]{1,0:T(8,128)(2,1)S(1)}, bf16[72,2048]{1,0:T(8,128)(2,1)S(1)}, u32[]{:S(2)}, u32[]{:S(2)}) %collective-permute-start.51) | collective-permute-done | bytes 294944 | tf_op jit(solution)/shard_map/ppermute | solution.py:24
  163.2 4.0 %collective-permute-done.48.returned = bf16[72,2048]{1,0:T(8,128)(2,1)S(1)} collective-permute-done((bf16[72,2048]{1,0:T(8,128)(2,1)S(1)}, bf16[72,2048]{1,0:T(8,128)(2,1)S(1)}, u32[]{:S(2)}, u32[]{:S(2)}) %collective-permute-start.48) | collective-permute-done | bytes 294944 | tf_op jit(solution)/shard_map/ppermute | solution.py:24
  169.7 3.9 %collective-permute-done.53.returned = bf16[72,2048]{1,0:T(8,128)(2,1)S(1)} collective-permute-done((bf16[72,2048]{1,0:T(8,128)(2,1)S(1)}, bf16[72,2048]{1,0:T(8,128)(2,1)S(1)}, u32[]{:S(2)}, u32[]{:S(2)}) %collective-permute-start.53) | collective-permute-done | bytes 294944 | tf_op jit(solution)/shard_map/ppermute | solution.py:24
  177.3 2.6 %collective-permute-done.47.returned = bf16[72,2048]{1,0:T(8,128)(2,1)S(1)} collective-permute-done((bf16[72,2048]{1,0:T(8,128)(2,1)S(1)}, bf16[72,2048]{1,0:T(8,128)(2,1)S(1)}, u32[]{:S(2)}, u32[]{:S(2)}) %collective-permute-start.47) | collective-permute-done | bytes 294944 | tf_op jit(solution)/shard_map/ppermute | solution.py:24
  182.8 2.5 %collective-permute-start.62 = (bf16[128,1024]{1,0:T(8,128)(2,1)S(1)}, bf16[128,1024]{1,0:T(8,128)(2,1)S(1)}, u32[]{:S(2)}, u32[]{:S(2)}) collective-permute-start(bf16[128,1024]{1,0:T(8,128)(2,1)S(1)} %add_convert_fusion.2), channel_id=1, source_target_pairs={{0,8},{1,9},{2,10},{3,11},{4,12},{5,13},{6,14},{7,15},{8,0},{9,1},... | collective-permute-start | bytes 786440 | tf_op jit(solution)/shard_map/ppermute | solution.py:24
  187.8 3.4 %collective-permute-done.56 = bf16[128,1024]{1,0:T(8,128)(2,1)S(1)} collective-permute-done((bf16[128,1024]{1,0:T(8,128)(2,1)S(1)}, bf16[128,1024]{1,0:T(8,128)(2,1)S(1)}, u32[]{:S(2)}, u32[]{:S(2)}) %collective-permute-start.56) | collective-permute-done | bytes 262176 | tf_op jit(solution)/shard_map/ppermute | solution.py:24
  191.2 3.3 %collective-permute-start.61 = (bf16[128,1024]{1,0:T(8,128)(2,1)S(1)}, bf16[128,1024]{1,0:T(8,128)(2,1)S(1)}, u32[]{:S(2)}, u32[]{:S(2)}) collective-permute-start(bf16[128,1024]{1,0:T(8,128)(2,1)S(1)} %add_convert_fusion.3), channel_id=1, source_target_pairs={{0,8},{1,9},{2,10},{3,11},{4,12},{5,13},{6,14},{7,15},{8,0},{9,1},... | collective-permute-start | bytes 786440 | tf_op jit(solution)/shard_map/ppermute | solution.py:24
  194.9 1.8 collective-permute-start.65
  197.0 4.6 %collective-permute-done.61.refs_2_ = bf16[128,1024]{1,0:T(8,128)(2,1)S(1)} collective-permute-done((bf16[128,1024]{1,0:T(8,128)(2,1)S(1)}, bf16[128,1024]{1,0:T(8,128)(2,1)S(1)}, u32[]{:S(2)}, u32[]{:S(2)}) %collective-permute-start.61) | collective-permute-done | bytes 262176 | tf_op jit(solution)/shard_map/ppermute | solution.py:24
  201.6 2.1 %collective-permute-done.66.refs_7_ = bf16[128,1024]{1,0:T(8,128)(2,1)S(1)} collective-permute-done((bf16[128,1024]{1,0:T(8,128)(2,1)S(1)}, bf16[128,1024]{1,0:T(8,128)(2,1)S(1)}, u32[]{:S(2)}, u32[]{:S(2)}) %collective-permute-start.66) | collective-permute-done | bytes 262176 | tf_op jit(solution)/shard_map/ppermute | solution.py:24
  203.7 2.8 %collective-permute-done.65.refs_6_ = bf16[128,1024]{1,0:T(8,128)(2,1)S(1)} collective-permute-done((bf16[128,1024]{1,0:T(8,128)(2,1)S(1)}, bf16[128,1024]{1,0:T(8,128)(2,1)S(1)}, u32[]{:S(2)}, u32[]{:S(2)}) %collective-permute-start.65) | collective-permute-done | bytes 262176 | tf_op jit(solution)/shard_map/ppermute | solution.py:24
  (152 shorter events, 59.1 us)
Async XLA Ops:
  0.6 16.4 %collective-permute-start.5 = (bf16[64,2048]{1,0:T(8,128)(2,1)}, bf16[64,2048]{1,0:T(8,128)(2,1)S(1)}, u32[]{:S(2)}, u32[]{:S(2)}) collective-permute-start(bf16[64,2048]{1,0:T(8,128)(2,1)} %refs_2_.1), channel_id=1, source_target_pairs={{0,8},{1,9},{2,10},{3,11},{4,12},{5,13},{6,14},{7,15},{8,0},{9,1},... | collective-permute-start | bytes 786440 | tf_op jit(solution)/shard_map/ppermute | solution.py:24
  4.7 15.3 %collective-permute-start.4 = (bf16[64,2048]{1,0:T(8,128)(2,1)}, bf16[64,2048]{1,0:T(8,128)(2,1)S(1)}, u32[]{:S(2)}, u32[]{:S(2)}) collective-permute-start(bf16[64,2048]{1,0:T(8,128)(2,1)} %refs_2_.1), channel_id=1, source_target_pairs={{0,2},{1,3},{2,0},{3,1},{4,6},{5,7},{6,4},{7,5},{8,10},{9,11},{10,... | collective-permute-start | bytes 786440 | tf_op jit(solution)/shard_map/ppermute | solution.py:24
  6.3 15.9 %collective-permute-start.3 = (bf16[64,2048]{1,0:T(8,128)(2,1)}, bf16[64,2048]{1,0:T(8,128)(2,1)S(1)}, u32[]{:S(2)}, u32[]{:S(2)}) collective-permute-start(bf16[64,2048]{1,0:T(8,128)(2,1)} %refs_2_.1), channel_id=1, source_target_pairs={{0,1},{1,0},{2,3},{3,2},{4,5},{5,4},{6,7},{7,6},{8,9},{9,8},{10,11... | collective-permute-start | bytes 786440 | tf_op jit(solution)/shard_map/ppermute | solution.py:24
  9.2 14.2 %collective-permute-start.9 = (bf16[64,2048]{1,0:T(8,128)(2,1)}, bf16[64,2048]{1,0:T(8,128)(2,1)S(1)}, u32[]{:S(2)}, u32[]{:S(2)}) collective-permute-start(bf16[64,2048]{1,0:T(8,128)(2,1)} %refs_2_.1), channel_id=1, source_target_pairs={{0,4},{1,5},{2,6},{3,7},{4,0},{5,1},{6,2},{7,3},{8,12},{9,13},{10,... | collective-permute-start | bytes 786440 | tf_op jit(solution)/shard_map/ppermute | solution.py:24
  17.0 13.6 %collective-permute-start.12 = (bf16[64,2048]{1,0:T(8,128)(2,1)S(1)}, bf16[64,2048]{1,0:T(8,128)(2,1)S(1)}, u32[]{:S(2)}, u32[]{:S(2)}) collective-permute-start(bf16[64,2048]{1,0:T(8,128)(2,1)S(1)} %collective-permute-done.5.refs_10_), channel_id=1, source_target_pairs={{0,2},{1,3},{2,0},{3,1},{4,6},{5,7},{6,4},{7,5},{8,10},{9,11},{10,... | collective-permute-start | bytes 786440 | tf_op jit(solution)/shard_map/ppermute | solution.py:24
  18.5 12.6 %collective-permute-start.11 = (bf16[64,2048]{1,0:T(8,128)(2,1)S(1)}, bf16[64,2048]{1,0:T(8,128)(2,1)S(1)}, u32[]{:S(2)}, u32[]{:S(2)}) collective-permute-start(bf16[64,2048]{1,0:T(8,128)(2,1)S(1)} %collective-permute-done.5.refs_10_), channel_id=1, source_target_pairs={{0,1},{1,0},{2,3},{3,2},{4,5},{5,4},{6,7},{7,6},{8,9},{9,8},{10,11... | collective-permute-start | bytes 786440 | tf_op jit(solution)/shard_map/ppermute | solution.py:24
  23.4 11.2 %collective-permute-start.6 = (bf16[64,2048]{1,0:T(8,128)(2,1)S(1)}, bf16[64,2048]{1,0:T(8,128)(2,1)S(1)}, u32[]{:S(2)}, u32[]{:S(2)}) collective-permute-start(bf16[64,2048]{1,0:T(8,128)(2,1)S(1)} %collective-permute-done.3.refs_3_), channel_id=1, source_target_pairs={{0,2},{1,3},{2,0},{3,1},{4,6},{5,7},{6,4},{7,5},{8,10},{9,11},{10,... | collective-permute-start | bytes 786440 | tf_op jit(solution)/shard_map/ppermute | solution.py:24
  30.6 14.0 %collective-permute-start.14 = (bf16[64,2048]{1,0:T(8,128)(2,1)S(1)}, bf16[64,2048]{1,0:T(8,128)(2,1)S(1)}, u32[]{:S(2)}, u32[]{:S(2)}) collective-permute-start(bf16[64,2048]{1,0:T(8,128)(2,1)S(1)} %collective-permute-done.9.refs_6_), channel_id=1, source_target_pairs={{0,2},{1,3},{2,0},{3,1},{4,6},{5,7},{6,4},{7,5},{8,10},{9,11},{10,... | collective-permute-start | bytes 786440 | tf_op jit(solution)/shard_map/ppermute | solution.py:24
  31.1 13.0 %collective-permute-start.15 = (bf16[64,2048]{1,0:T(8,128)(2,1)S(1)}, bf16[64,2048]{1,0:T(8,128)(2,1)S(1)}, u32[]{:S(2)}, u32[]{:S(2)}) collective-permute-start(bf16[64,2048]{1,0:T(8,128)(2,1)S(1)} %collective-permute-done.8.refs_14_), channel_id=1, source_target_pairs={{0,2},{1,3},{2,0},{3,1},{4,6},{5,7},{6,4},{7,5},{8,10},{9,11},{10,... | collective-permute-start | bytes 786440 | tf_op jit(solution)/shard_map/ppermute | solution.py:24
  39.2 12.0 %collective-permute-start.18 = (bf16[64,2048]{1,0:T(8,128)(2,1)S(1)}, bf16[64,2048]{1,0:T(8,128)(2,1)S(1)}, u32[]{:S(2)}, u32[]{:S(2)}) collective-permute-start(bf16[64,2048]{1,0:T(8,128)(2,1)S(1)} %collective-permute-done.12.refs_12_), channel_id=1, source_target_pairs={{0,1},{1,0},{2,3},{3,2},{4,5},{5,4},{6,7},{7,6},{8,9},{9,8},{10,11... | collective-permute-start | bytes 786440 | tf_op jit(solution)/shard_map/ppermute | solution.py:24
  60.2 11.3 %collective-permute-start.27 = (bf16[72,2048]{1,0:T(8,128)(2,1)S(1)}, bf16[72,2048]{1,0:T(8,128)(2,1)S(1)}, u32[]{:S(2)}, u32[]{:S(2)}) collective-permute-start(bf16[72,2048]{1,0:T(8,128)(2,1)S(1)} %get-tuple-element.142), channel_id=1, source_target_pairs={{0,1},{1,0},{2,3},{3,2},{4,5},{5,4},{6,7},{7,6},{8,9},{9,8},{10,11... | collective-permute-start | bytes 884744 | tf_op jit(solution)/shard_map/ppermute | solution.py:24
  62.8 12.6 %collective-permute-start.26 = (bf16[128,1024]{1,0:T(8,128)(2,1)S(1)}, bf16[128,1024]{1,0:T(8,128)(2,1)S(1)}, u32[]{:S(2)}, u32[]{:S(2)}) collective-permute-start(bf16[128,1024]{1,0:T(8,128)(2,1)S(1)} %get-tuple-element.144.refs_1_), channel_id=1, source_target_pairs={{0,2},{1,3},{2,0},{3,1},{4,6},{5,7},{6,4},{7,5},{8,10},{9,11},{10,... | collective-permute-start | bytes 786440 | tf_op jit(solution)/shard_map/ppermute | solution.py:24
  63.8 16.3 %collective-permute-start.24 = (bf16[128,1024]{1,0:T(8,128)(2,1)S(1)}, bf16[128,1024]{1,0:T(8,128)(2,1)S(1)}, u32[]{:S(2)}, u32[]{:S(2)}) collective-permute-start(bf16[128,1024]{1,0:T(8,128)(2,1)S(1)} %get-tuple-element.171.refs_0_), channel_id=1, source_target_pairs={{0,4},{1,5},{2,6},{3,7},{4,0},{5,1},{6,2},{7,3},{8,12},{9,13},{10,... | collective-permute-start | bytes 786440 | tf_op jit(solution)/shard_map/ppermute | solution.py:24
  64.4 15.7 %collective-permute-start.23 = (bf16[128,1024]{1,0:T(8,128)(2,1)S(1)}, bf16[128,1024]{1,0:T(8,128)(2,1)S(1)}, u32[]{:S(2)}, u32[]{:S(2)}) collective-permute-start(bf16[128,1024]{1,0:T(8,128)(2,1)S(1)} %get-tuple-element.171.refs_0_), channel_id=1, source_target_pairs={{0,8},{1,9},{2,10},{3,11},{4,12},{5,13},{6,14},{7,15},{8,0},{9,1},... | collective-permute-start | bytes 786440 | tf_op jit(solution)/shard_map/ppermute | solution.py:24
  70.9 18.9 %collective-permute-start.33 = (bf16[128,1024]{1,0:T(8,128)(2,1)S(1)}, bf16[128,1024]{1,0:T(8,128)(2,1)S(1)}, u32[]{:S(2)}, u32[]{:S(2)}) collective-permute-start(bf16[128,1024]{1,0:T(8,128)(2,1)S(1)} %get-tuple-element.144.refs_1_), channel_id=1, source_target_pairs={{0,4},{1,5},{2,6},{3,7},{4,0},{5,1},{6,2},{7,3},{8,12},{9,13},{10,... | collective-permute-start | bytes 786440 | tf_op jit(solution)/shard_map/ppermute | solution.py:24
  71.5 19.4 %collective-permute-start.32 = (bf16[128,1024]{1,0:T(8,128)(2,1)S(1)}, bf16[128,1024]{1,0:T(8,128)(2,1)S(1)}, u32[]{:S(2)}, u32[]{:S(2)}) collective-permute-start(bf16[128,1024]{1,0:T(8,128)(2,1)S(1)} %get-tuple-element.144.refs_1_), channel_id=1, source_target_pairs={{0,8},{1,9},{2,10},{3,11},{4,12},{5,13},{6,14},{7,15},{8,0},{9,1},... | collective-permute-start | bytes 786440 | tf_op jit(solution)/shard_map/ppermute | solution.py:24
  80.0 13.7 %collective-permute-start.29 = (bf16[128,1024]{1,0:T(8,128)(2,1)S(1)}, bf16[128,1024]{1,0:T(8,128)(2,1)S(1)}, u32[]{:S(2)}, u32[]{:S(2)}) collective-permute-start(bf16[128,1024]{1,0:T(8,128)(2,1)S(1)} %collective-permute-done.23.left.refs_0_), channel_id=1, source_target_pairs={{0,4},{1,5},{2,6},{3,7},{4,0},{5,1},{6,2},{7,3},{8,12},{9,13},{10,... | collective-permute-start | bytes 786440 | tf_op jit(solution)/shard_map/ppermute | solution.py:24
  80.8 15.1 %collective-permute-start.31 = (bf16[72,2048]{1,0:T(8,128)(2,1)S(1)}, bf16[72,2048]{1,0:T(8,128)(2,1)S(1)}, u32[]{:S(2)}, u32[]{:S(2)}) collective-permute-start(bf16[72,2048]{1,0:T(8,128)(2,1)S(1)} %shard_map.135), channel_id=1, source_target_pairs={{0,1},{1,0},{2,3},{3,2},{4,5},{5,4},{6,7},{7,6},{8,9},{9,8},{10,11... | collective-permute-start | bytes 884744 | tf_op jit(solution)/shard_map/ppermute | solution.py:24
  81.3 13.1 %collective-permute-start.30 = (bf16[128,1024]{1,0:T(8,128)(2,1)S(1)}, bf16[128,1024]{1,0:T(8,128)(2,1)S(1)}, u32[]{:S(2)}, u32[]{:S(2)}) collective-permute-start(bf16[128,1024]{1,0:T(8,128)(2,1)S(1)} %collective-permute-done.24.left.refs_0_), channel_id=1, source_target_pairs={{0,2},{1,3},{2,0},{3,1},{4,6},{5,7},{6,4},{7,5},{8,10},{9,11},{10,... | collective-permute-start | bytes 786440 | tf_op jit(solution)/shard_map/ppermute | solution.py:24
  91.0 12.3 %collective-permute-start.28 = (bf16[128,1024]{1,0:T(8,128)(2,1)S(1)}, bf16[128,1024]{1,0:T(8,128)(2,1)S(1)}, u32[]{:S(2)}, u32[]{:S(2)}) collective-permute-start(bf16[128,1024]{1,0:T(8,128)(2,1)S(1)} %collective-permute-done.23.left.refs_0_), channel_id=1, source_target_pairs={{0,2},{1,3},{2,0},{3,1},{4,6},{5,7},{6,4},{7,5},{8,10},{9,11},{10,... | collective-permute-start | bytes 786440 | tf_op jit(solution)/shard_map/ppermute | solution.py:24
  93.7 11.0 %collective-permute-start.36 = (bf16[128,1024]{1,0:T(8,128)(2,1)S(1)}, bf16[128,1024]{1,0:T(8,128)(2,1)S(1)}, u32[]{:S(2)}, u32[]{:S(2)}) collective-permute-start(bf16[128,1024]{1,0:T(8,128)(2,1)S(1)} %collective-permute-done.32.right.refs_1_), channel_id=1, source_target_pairs={{0,4},{1,5},{2,6},{3,7},{4,0},{5,1},{6,2},{7,3},{8,12},{9,13},{10,... | collective-permute-start | bytes 786440 | tf_op jit(solution)/shard_map/ppermute | solution.py:24
  94.4 20.3 %collective-permute-start.42 = (bf16[72,2048]{1,0:T(8,128)(2,1)S(1)}, bf16[72,2048]{1,0:T(8,128)(2,1)S(1)}, u32[]{:S(2)}, u32[]{:S(2)}) collective-permute-start(bf16[72,2048]{1,0:T(8,128)(2,1)S(1)} %shard_map.136), channel_id=1, source_target_pairs={{0,1},{1,0},{2,3},{3,2},{4,5},{5,4},{6,7},{7,6},{8,9},{9,8},{10,11... | collective-permute-start | bytes 884744 | tf_op jit(solution)/shard_map/ppermute | solution.py:24
  95.9 18.9 %collective-permute-start.41 = (bf16[72,2048]{1,0:T(8,128)(2,1)S(1)}, bf16[72,2048]{1,0:T(8,128)(2,1)S(1)}, u32[]{:S(2)}, u32[]{:S(2)}) collective-permute-start(bf16[72,2048]{1,0:T(8,128)(2,1)S(1)} %shard_map.137), channel_id=1, source_target_pairs={{0,1},{1,0},{2,3},{3,2},{4,5},{5,4},{6,7},{7,6},{8,9},{9,8},{10,11... | collective-permute-start | bytes 884744 | tf_op jit(solution)/shard_map/ppermute | solution.py:24
  97.7 11.2 %collective-permute-start.35 = (bf16[128,1024]{1,0:T(8,128)(2,1)S(1)}, bf16[128,1024]{1,0:T(8,128)(2,1)S(1)}, u32[]{:S(2)}, u32[]{:S(2)}) collective-permute-start(bf16[128,1024]{1,0:T(8,128)(2,1)S(1)} %collective-permute-done.29.left.refs_0_), channel_id=1, source_target_pairs={{0,2},{1,3},{2,0},{3,1},{4,6},{5,7},{6,4},{7,5},{8,10},{9,11},{10,... | collective-permute-start | bytes 786440 | tf_op jit(solution)/shard_map/ppermute | solution.py:24
  103.3 10.9 %collective-permute-start.34 = (bf16[128,1024]{1,0:T(8,128)(2,1)S(1)}, bf16[128,1024]{1,0:T(8,128)(2,1)S(1)}, u32[]{:S(2)}, u32[]{:S(2)}) collective-permute-start(bf16[128,1024]{1,0:T(8,128)(2,1)S(1)} %collective-permute-done.32.right.refs_1_), channel_id=1, source_target_pairs={{0,2},{1,3},{2,0},{3,1},{4,6},{5,7},{6,4},{7,5},{8,10},{9,11},{10,... | collective-permute-start | bytes 786440 | tf_op jit(solution)/shard_map/ppermute | solution.py:24
  104.7 12.3 %collective-permute-start.40 = (bf16[128,1024]{1,0:T(8,128)(2,1)S(1)}, bf16[128,1024]{1,0:T(8,128)(2,1)S(1)}, u32[]{:S(2)}, u32[]{:S(2)}) collective-permute-start(bf16[128,1024]{1,0:T(8,128)(2,1)S(1)} %collective-permute-done.36.right.refs_1_), channel_id=1, source_target_pairs={{0,2},{1,3},{2,0},{3,1},{4,6},{5,7},{6,4},{7,5},{8,10},{9,11},{10,... | collective-permute-start | bytes 786440 | tf_op jit(solution)/shard_map/ppermute | solution.py:24
  114.4 9.4 %collective-permute-start.38 = (bf16[72,2048]{1,0:T(8,128)(2,1)S(1)}, bf16[72,2048]{1,0:T(8,128)(2,1)S(1)}, u32[]{:S(2)}, u32[]{:S(2)}) collective-permute-start(bf16[72,2048]{1,0:T(8,128)(2,1)S(1)} %shard_map.139), channel_id=1, source_target_pairs={{0,1},{1,0},{2,3},{3,2},{4,5},{5,4},{6,7},{7,6},{8,9},{9,8},{10,11... | collective-permute-start | bytes 884744 | tf_op jit(solution)/shard_map/ppermute | solution.py:24
  117.2 10.7 %collective-permute-start.43 = (bf16[72,2048]{1,0:T(8,128)(2,1)S(1)}, bf16[72,2048]{1,0:T(8,128)(2,1)S(1)}, u32[]{:S(2)}, u32[]{:S(2)}) collective-permute-start(bf16[72,2048]{1,0:T(8,128)(2,1)S(1)} %shard_map.140), channel_id=1, source_target_pairs={{0,1},{1,0},{2,3},{3,2},{4,5},{5,4},{6,7},{7,6},{8,9},{9,8},{10,11... | collective-permute-start | bytes 884744 | tf_op jit(solution)/shard_map/ppermute | solution.py:24
  131.9 10.0 %collective-permute-start.44 = (bf16[72,2048]{1,0:T(8,128)(2,1)S(1)}, bf16[72,2048]{1,0:T(8,128)(2,1)S(1)}, u32[]{:S(2)}, u32[]{:S(2)}) collective-permute-start(bf16[72,2048]{1,0:T(8,128)(2,1)S(1)} %get-tuple-element.181), channel_id=1, source_target_pairs={{0,1},{1,0},{2,3},{3,2},{4,5},{5,4},{6,7},{7,6},{8,9},{9,8},{10,11... | collective-permute-start | bytes 884744 | tf_op jit(solution)/shard_map/ppermute | solution.py:24
  133.2 15.1 %collective-permute-start.45 = (bf16[72,2048]{1,0:T(8,128)(2,1)S(1)}, bf16[72,2048]{1,0:T(8,128)(2,1)S(1)}, u32[]{:S(2)}, u32[]{:S(2)}) collective-permute-start(bf16[72,2048]{1,0:T(8,128)(2,1)S(1)} %shard_map.141), channel_id=1, source_target_pairs={{0,1},{1,0},{2,3},{3,2},{4,5},{5,4},{6,7},{7,6},{8,9},{9,8},{10,11... | collective-permute-start | bytes 884744 | tf_op jit(solution)/shard_map/ppermute | solution.py:24
  134.0 20.6 %collective-permute-start.49 = (bf16[72,2048]{1,0:T(8,128)(2,1)S(1)}, bf16[72,2048]{1,0:T(8,128)(2,1)S(1)}, u32[]{:S(2)}, u32[]{:S(2)}) collective-permute-start(bf16[72,2048]{1,0:T(8,128)(2,1)S(1)} %get-tuple-element.182), channel_id=1, source_target_pairs={{0,1},{1,0},{2,3},{3,2},{4,5},{5,4},{6,7},{7,6},{8,9},{9,8},{10,11... | collective-permute-start | bytes 884744 | tf_op jit(solution)/shard_map/ppermute | solution.py:24
  139.4 21.5 %collective-permute-start.51 = (bf16[72,2048]{1,0:T(8,128)(2,1)S(1)}, bf16[72,2048]{1,0:T(8,128)(2,1)S(1)}, u32[]{:S(2)}, u32[]{:S(2)}) collective-permute-start(bf16[72,2048]{1,0:T(8,128)(2,1)S(1)} %get-tuple-element.186), channel_id=1, source_target_pairs={{0,1},{1,0},{2,3},{3,2},{4,5},{5,4},{6,7},{7,6},{8,9},{9,8},{10,11... | collective-permute-start | bytes 884744 | tf_op jit(solution)/shard_map/ppermute | solution.py:24
  142.3 20.2 %collective-permute-start.50 = (bf16[128,1024]{1,0:T(8,128)(2,1)S(1)}, bf16[128,1024]{1,0:T(8,128)(2,1)S(1)}, u32[]{:S(2)}, u32[]{:S(2)}) collective-permute-start(bf16[128,1024]{1,0:T(8,128)(2,1)S(1)} %get-tuple-element.189), channel_id=1, source_target_pairs={{0,2},{1,3},{2,0},{3,1},{4,6},{5,7},{6,4},{7,5},{8,10},{9,11},{10,... | collective-permute-start | bytes 786440 | tf_op jit(solution)/shard_map/ppermute | solution.py:24
  143.5 23.7 %collective-permute-start.48 = (bf16[72,2048]{1,0:T(8,128)(2,1)S(1)}, bf16[72,2048]{1,0:T(8,128)(2,1)S(1)}, u32[]{:S(2)}, u32[]{:S(2)}) collective-permute-start(bf16[72,2048]{1,0:T(8,128)(2,1)S(1)} %get-tuple-element.187), channel_id=1, source_target_pairs={{0,1},{1,0},{2,3},{3,2},{4,5},{5,4},{6,7},{7,6},{8,9},{9,8},{10,11... | collective-permute-start | bytes 884744 | tf_op jit(solution)/shard_map/ppermute | solution.py:24
  148.3 20.5 %collective-permute-start.54 = (bf16[128,1024]{1,0:T(8,128)(2,1)S(1)}, bf16[128,1024]{1,0:T(8,128)(2,1)S(1)}, u32[]{:S(2)}, u32[]{:S(2)}) collective-permute-start(bf16[128,1024]{1,0:T(8,128)(2,1)S(1)} %get-tuple-element.207), channel_id=1, source_target_pairs={{0,2},{1,3},{2,0},{3,1},{4,6},{5,7},{6,4},{7,5},{8,10},{9,11},{10,... | collective-permute-start | bytes 786440 | tf_op jit(solution)/shard_map/ppermute | solution.py:24
  154.6 19.0 %collective-permute-start.53 = (bf16[72,2048]{1,0:T(8,128)(2,1)S(1)}, bf16[72,2048]{1,0:T(8,128)(2,1)S(1)}, u32[]{:S(2)}, u32[]{:S(2)}) collective-permute-start(bf16[72,2048]{1,0:T(8,128)(2,1)S(1)} %get-tuple-element.193), channel_id=1, source_target_pairs={{0,1},{1,0},{2,3},{3,2},{4,5},{5,4},{6,7},{7,6},{8,9},{9,8},{10,11... | collective-permute-start | bytes 884744 | tf_op jit(solution)/shard_map/ppermute | solution.py:24
  161.2 13.8 %collective-permute-start.52 = (bf16[128,1024]{1,0:T(8,128)(2,1)S(1)}, bf16[128,1024]{1,0:T(8,128)(2,1)S(1)}, u32[]{:S(2)}, u32[]{:S(2)}) collective-permute-start(bf16[128,1024]{1,0:T(8,128)(2,1)S(1)} %get-tuple-element.202), channel_id=1, source_target_pairs={{0,2},{1,3},{2,0},{3,1},{4,6},{5,7},{6,4},{7,5},{8,10},{9,11},{10,... | collective-permute-start | bytes 786440 | tf_op jit(solution)/shard_map/ppermute | solution.py:24
  162.5 13.8 %collective-permute-start.55 = (bf16[128,1024]{1,0:T(8,128)(2,1)S(1)}, bf16[128,1024]{1,0:T(8,128)(2,1)S(1)}, u32[]{:S(2)}, u32[]{:S(2)}) collective-permute-start(bf16[128,1024]{1,0:T(8,128)(2,1)S(1)} %add_convert_fusion.5), channel_id=1, source_target_pairs={{0,4},{1,5},{2,6},{3,7},{4,0},{5,1},{6,2},{7,3},{8,12},{9,13},{10,... | collective-permute-start | bytes 786440 | tf_op jit(solution)/shard_map/ppermute | solution.py:24
  167.2 12.6 %collective-permute-start.47 = (bf16[72,2048]{1,0:T(8,128)(2,1)S(1)}, bf16[72,2048]{1,0:T(8,128)(2,1)S(1)}, u32[]{:S(2)}, u32[]{:S(2)}) collective-permute-start(bf16[72,2048]{1,0:T(8,128)(2,1)S(1)} %get-tuple-element.194), channel_id=1, source_target_pairs={{0,1},{1,0},{2,3},{3,2},{4,5},{5,4},{6,7},{7,6},{8,9},{9,8},{10,11... | collective-permute-start | bytes 884744 | tf_op jit(solution)/shard_map/ppermute | solution.py:24
  168.8 12.6 %collective-permute-start.60 = (bf16[128,1024]{1,0:T(8,128)(2,1)S(1)}, bf16[128,1024]{1,0:T(8,128)(2,1)S(1)}, u32[]{:S(2)}, u32[]{:S(2)}) collective-permute-start(bf16[128,1024]{1,0:T(8,128)(2,1)S(1)} %add_convert_fusion.4), channel_id=1, source_target_pairs={{0,4},{1,5},{2,6},{3,7},{4,0},{5,1},{6,2},{7,3},{8,12},{9,13},{10,... | collective-permute-start | bytes 786440 | tf_op jit(solution)/shard_map/ppermute | solution.py:24
  175.0 10.3 %collective-permute-start.58 = (bf16[72,2048]{1,0:T(8,128)(2,1)S(1)}, bf16[72,2048]{1,0:T(8,128)(2,1)S(1)}, u32[]{:S(2)}, u32[]{:S(2)}) collective-permute-start(bf16[72,2048]{1,0:T(8,128)(2,1)S(1)} %get-tuple-element.195), channel_id=1, source_target_pairs={{0,1},{1,0},{2,3},{3,2},{4,5},{5,4},{6,7},{7,6},{8,9},{9,8},{10,11... | collective-permute-start | bytes 884744 | tf_op jit(solution)/shard_map/ppermute | solution.py:24
  176.4 10.3 %collective-permute-start.57 = (bf16[128,1024]{1,0:T(8,128)(2,1)S(1)}, bf16[128,1024]{1,0:T(8,128)(2,1)S(1)}, u32[]{:S(2)}, u32[]{:S(2)}) collective-permute-start(bf16[128,1024]{1,0:T(8,128)(2,1)S(1)} %get-tuple-element.210), channel_id=1, source_target_pairs={{0,2},{1,3},{2,0},{3,1},{4,6},{5,7},{6,4},{7,5},{8,10},{9,11},{10,... | collective-permute-start | bytes 786440 | tf_op jit(solution)/shard_map/ppermute | solution.py:24
  179.9 14.7 %collective-permute-start.46 = (bf16[72,2048]{1,0:T(8,128)(2,1)S(1)}, bf16[72,2048]{1,0:T(8,128)(2,1)S(1)}, u32[]{:S(2)}, u32[]{:S(2)}) collective-permute-start(bf16[72,2048]{1,0:T(8,128)(2,1)S(1)} %get-tuple-element.196), channel_id=1, source_target_pairs={{0,1},{1,0},{2,3},{3,2},{4,5},{5,4},{6,7},{7,6},{8,9},{9,8},{10,11... | collective-permute-start | bytes 884744 | tf_op jit(solution)/shard_map/ppermute | solution.py:24
  181.4 9.8 %collective-permute-start.56 = (bf16[128,1024]{1,0:T(8,128)(2,1)S(1)}, bf16[128,1024]{1,0:T(8,128)(2,1)S(1)}, u32[]{:S(2)}, u32[]{:S(2)}) collective-permute-start(bf16[128,1024]{1,0:T(8,128)(2,1)S(1)} %get-tuple-element.215), channel_id=1, source_target_pairs={{0,2},{1,3},{2,0},{3,1},{4,6},{5,7},{6,4},{7,5},{8,10},{9,11},{10,... | collective-permute-start | bytes 786440 | tf_op jit(solution)/shard_map/ppermute | solution.py:24
  182.8 14.2 %collective-permute-start.62 = (bf16[128,1024]{1,0:T(8,128)(2,1)S(1)}, bf16[128,1024]{1,0:T(8,128)(2,1)S(1)}, u32[]{:S(2)}, u32[]{:S(2)}) collective-permute-start(bf16[128,1024]{1,0:T(8,128)(2,1)S(1)} %add_convert_fusion.2), channel_id=1, source_target_pairs={{0,8},{1,9},{2,10},{3,11},{4,12},{5,13},{6,14},{7,15},{8,0},{9,1},... | collective-permute-start | bytes 786440 | tf_op jit(solution)/shard_map/ppermute | solution.py:24
  186.7 10.3 %collective-permute-start.63 = (bf16[128,1024]{1,0:T(8,128)(2,1)S(1)}, bf16[128,1024]{1,0:T(8,128)(2,1)S(1)}, u32[]{:S(2)}, u32[]{:S(2)}) collective-permute-start(bf16[128,1024]{1,0:T(8,128)(2,1)S(1)} %get-tuple-element.222), channel_id=1, source_target_pairs={{0,2},{1,3},{2,0},{3,1},{4,6},{5,7},{6,4},{7,5},{8,10},{9,11},{10,... | collective-permute-start | bytes 786440 | tf_op jit(solution)/shard_map/ppermute | solution.py:24
  191.2 10.5 %collective-permute-start.61 = (bf16[128,1024]{1,0:T(8,128)(2,1)S(1)}, bf16[128,1024]{1,0:T(8,128)(2,1)S(1)}, u32[]{:S(2)}, u32[]{:S(2)}) collective-permute-start(bf16[128,1024]{1,0:T(8,128)(2,1)S(1)} %add_convert_fusion.3), channel_id=1, source_target_pairs={{0,8},{1,9},{2,10},{3,11},{4,12},{5,13},{6,14},{7,15},{8,0},{9,1},... | collective-permute-start | bytes 786440 | tf_op jit(solution)/shard_map/ppermute | solution.py:24
  194.9 11.7 %collective-permute-start.65 = (bf16[128,1024]{1,0:T(8,128)(2,1)S(1)}, bf16[128,1024]{1,0:T(8,128)(2,1)S(1)}, u32[]{:S(2)}, u32[]{:S(2)}) collective-permute-start(bf16[128,1024]{1,0:T(8,128)(2,1)S(1)} %add_convert_fusion.1), channel_id=1, source_target_pairs={{0,4},{1,5},{2,6},{3,7},{4,0},{5,1},{6,2},{7,3},{8,12},{9,13},{10,... | collective-permute-start | bytes 786440 | tf_op jit(solution)/shard_map/ppermute | solution.py:24
  (29 other events, 314.8 us)

commit v2 on v1

--- a/solution.py
+++ b/solution.py
@@ -135,34 +135,39 @@
     (2, 2),
     (1, 1),
     (4, 4),
+    (9, 1),
     (12, 4),
+    (10, 2),
+    (5, 1),
+    (3, 2),
     (None, 4),
-    (10, 2),
-    (9, 1),
+    (14, 2),
+    (13, 1),
     (None, 8),
-    (3, 2),
-    (5, 1),
-    (None, 1),
-    (14, 2),
     (6, 2),
-    (None, 2),
-    (13, 1),
+    (15, 1),
     (11, 1),
     (7, 2),
-    (15, 1),
 )
 
 
-def weight_planes(shard, picks, token):
+def doubled(picks, masks, bit):
+    picks = jnp.concatenate([picks, swapped(picks, "ep", bit)], axis=0)
+    return picks, masks + [mask | bit for mask in masks]
+
+
+def weight_planes(shard, picks, masks, token):
     blocks = {0: shard}
-    masks = [0]
     for mask, bit in WEIGHT_STEPS:
         if mask is None:
-            token = after(swapped(picks, "ep", bit), token)
-            picks = jnp.concatenate([picks, token], axis=0)
-            masks = masks + [m | bit for m in masks]
+            picks, masks = doubled(picks, masks, bit)
+            token = after(picks, token)
+            picks = token
         else:
-            token = after(swapped(blocks[mask ^ bit], "ep", bit), token)
+            source = blocks[mask ^ bit]
+            if mask == 6:
+                source = after(source, blocks[12])
+            token = after(swapped(source, "ep", bit), token)
             blocks[mask] = token
     return [(m, [blocks[m + i] for i in range(4)]) for m in range(0, 16, 4)], picks, masks
 
@@ -212,7 +217,7 @@
     )(*lhs, *blocks)
 
 
-def norm_kernel(own, heard, residual, gain, pack, state, left, right, packed):
+def norm_kernel(own, heard, residual, gain, state, left, right):
     mixed = (residual[...].astype(jnp.float32) + (own[...] + heard[...])).astype(jnp.bfloat16)
     state[...] = mixed
     mixed = mixed.astype(jnp.float32)
@@ -221,21 +226,18 @@
     middle = left.shape[1]
     left[...] = rows[:, :middle]
     right[...] = rows[:, middle:]
-    packed[...] = jnp.dot(pack[0], rows, preferred_element_type=jnp.float32).astype(jnp.bfloat16)
-
-
-def norm(own, heard, residual, gain, pack):
+
+
+def norm(own, heard, residual, gain):
     rows, width = residual.shape
     half = jax.ShapeDtypeStruct((rows, width // 2), jnp.bfloat16)
-    packed = jax.ShapeDtypeStruct((pack.shape[1], width), jnp.bfloat16)
     return local(
         norm_kernel,
-        [jax.ShapeDtypeStruct(residual.shape, jnp.bfloat16), half, half, packed],
+        [jax.ShapeDtypeStruct(residual.shape, jnp.bfloat16), half, half],
         own,
         heard,
         residual,
         gain.reshape(1, -1),
-        pack,
     )
 
 
@@ -277,13 +279,9 @@
     return jnp.concatenate([expert_ids.T.astype(jnp.float32), route_weight.T], axis=0)[None]
 
 
-def all_picks(picks):
-    ep_count = lax.axis_size("ep")
-    masks, bit = [0], 1
-    while bit < ep_count:
-        picks = jnp.concatenate([picks, swapped(picks, "ep", bit)], axis=0)
-        masks = masks + [mask | bit for mask in masks]
-        bit *= 2
+def all_picks(picks, masks, bits):
+    for bit in bits:
+        picks, masks = doubled(picks, masks, bit)
     return picks, masks
 
 
@@ -367,7 +365,7 @@
 
 STEPS = (
     ("block", 2, 0),
-    ("packed", 0),
+    ("pack", 0),
     ("block", 2, 1),
     ("pack", 2),
     ("block", 4, 0),
@@ -376,6 +374,7 @@
     ("pack", 4),
     ("block", 8, 1),
     ("pack", 8),
+    ("packed", 0),
     ("packed", 2),
     ("block", 6, 0),
     ("block", 12, 0),
@@ -395,30 +394,35 @@
     ("packed", 10),
     ("reply", 0),
     ("packed", 14),
+    ("reply", 12),
+    ("packed", 6),
 )
 
 
 def plain_steps(count):
-    steps = []
+    steps = [("pack", 0)]
     for mask in sorted(range(2, count, 2), key=lambda m: (m.bit_count(), m & 2, m)):
         steps += [("block", mask, 0), ("block", mask, 1), ("pack", mask)]
     return steps
 
 
-def experts_sum(state, halves, packed, pack, row_weight, weight_in, weight_out):
+def experts_sum(state, halves, pack, row_weight, weight_in, weight_out):
     ep_count = lax.axis_size("ep")
     rows, width = state.shape
     capacity = pack.shape[1]
     half = (rows, width // 2)
     packed_shape = jax.ShapeDtypeStruct((capacity, width), jnp.bfloat16)
-    blocks, arrived = {0: halves}, {0: swapped(packed, "ep", 1)}
+    blocks, arrived = {0: halves}, {}
     replies, returned = {}, {}
-    token = packed
+    token = state
 
     def receive(mask, side):
         nonlocal token
         bit = mask & -mask
-        token = after(swapped(blocks[mask ^ bit][side], "ep", bit), token)
+        source = blocks[mask ^ bit][side]
+        if mask == 2:
+            source = after(source, pack)
+        token = after(swapped(source, "ep", bit), token)
         blocks.setdefault(mask, [None, None])[side] = token
 
     def send_packed(mask):
@@ -465,13 +469,13 @@
     received = {mask: ([], []) for mask in backward}
     sums = {}
 
-    def send_replies(mask):
+    def send_reply(mask):
         nonlocal token
-        if mask not in replies:
-            reply_to(mask)
-        for far_side in (1, 0):
-            token = after(replies[mask][1 + far_side], token)
-            returned[mask | 2 * far_side] = swapped(token, "ep", 1)
+        group, far_side = mask & ~2, mask // 2 % 2
+        if group not in replies:
+            reply_to(group)
+        token = after(replies[group][1 + far_side], token)
+        returned[mask] = swapped(token, "ep", 1)
 
     def unpack(mask):
         nonlocal token
@@ -501,18 +505,35 @@
         received[mask ^ bit][side].append(swapped(token, "ep", bit))
 
     for mask in backward[:2]:
-        send_replies(mask)
+        send_reply(mask | 2)
+        send_reply(mask)
     unpack(backward[0] | 2)
-    for mask in backward[2:]:
-        send_replies(mask)
-    for k, mask in enumerate(backward):
-        if k:
+    for mask in backward[2:-1]:
+        send_reply(mask | 2)
+        send_reply(mask)
+    unpack(backward[0])
+    for k, mask in enumerate(backward[1:-1]):
+        if k == 0:
             unpack(mask | 2)
-            pass_on(backward[k - 1], 0)
-        if mask:
+        pass_on(backward[k], 0)
+        if k == 1:
+            send_reply(2)
+        pass_on(backward[k], 1)
+        if k == 0:
             unpack(mask)
-        if k:
-            pass_on(backward[k - 1], 1)
+            unpack(backward[2] | 2)
+        else:
+            if k > 1:
+                unpack(mask | 2)
+            unpack(mask)
+    send_reply(0)
+    pass_on(backward[-2], 0)
+    pass_on(backward[-2], 1)
+    near, far = received[0]
+    token = near[0] = after(near[0], token)
+    unpack(2)
+    token = far[0] = after(far[0], token)
+    token = near[1] = after(near[1], token)
     unpack(0)
     parts = [part for pair in zip(*received[0]) for part in pair]
     shape = jax.ShapeDtypeStruct(state.shape, jnp.bfloat16)
@@ -546,24 +567,27 @@
         and 2 * out_proj.shape[0] == HD
     )
     picks = own_picks(expert_ids, route_weight)
+    masks = [0]
     results = attention(queries, keys, values, prior_out, prior_lse, split)
     attended = results[0]
     if split:
         rows = out_proj.shape[0]
         given, kept = results[1:]
         sibling = swapped(given, "ctx", 1)
-        planes, picks, masks = weight_planes(out_proj, picks, given)
+        planes, picks, masks = weight_planes(out_proj, picks, masks, given)
         given_sum, own_sum = product([sibling, kept], planes, rows)
-        heard_sum = swapped(given_sum, "ctx", 1)
+        picks, masks = doubled(picks, masks, 1)
+        heard_sum = after(swapped(given_sum, "ctx", 1), picks)
+        picks, masks = doubled(picks, masks, 2)
     else:
-        picks, masks = all_picks(picks)
+        picks, masks = all_picks(picks, masks, [1 << k for k in range(ep_count.bit_length() - 1)])
         full = lax.all_gather(out_proj, ("ctx", "ep"), axis=0, tiled=True)
         own_sum = jnp.dot(attended, full, preferred_element_type=jnp.float32)
         heard_sum = jnp.zeros_like(own_sum)
     pack, row_weight = routing(picks, masks, capacity)
-    state, left, right, packed = norm(own_sum, heard_sum, residual, norm_gain, pack)
+    state, left, right = norm(own_sum, heard_sum, residual, norm_gain)
     layer_out = experts_sum(
-        state, [left, right], packed, pack, row_weight, expert_in[0], expert_out[0]
+        state, [left, right], pack, row_weight, expert_in[0], expert_out[0]
     )
     return (layer_out, attended)
 

time: 208 us -> 201 us (0.966)
  waiting for transfers between devices: 96.3 us -> 89.1 us
    ppermute x65, waiting for transfers between devices: 95.5 us -> 86.5 us  [swapped(): return lax.ppermute(shard, axis, [(i, i ^ mask) for i in range(devices)])]
    pallas_call x21 -> x22, Pallas kernels: 22.1 us -> 22.1 us  [local(): pl.pallas_call(kernel, out_shape=out_shape, in_specs=[WHOLE] * len(operan...]
  transfers between devices with their start and end apart: 67 -> 67, of which waited for: 33 -> 37; matrix products, arithmetic and copies ran while one was open for 1% -> 1% of each run, Pallas kernels for 10% -> 12%
where the time goes in v2:
time: 201 us; the launch traced here: 200 us
  waiting for transfers between devices  89.1 us (44%)
  starting transfers between devices  76.4 us (38%)
  Pallas kernels  27.9 us (14%)
  local copies, waits for them, and re-layouts  3.81 us (2%)
  other arithmetic  2.05 us (1%)
    ppermute x65, waiting for transfers between devices, swapped(): return lax.ppermute(shard, axis, [(i, i ^ mask) for i in range(devices)])  86.5 us
    ppermute x65, starting transfers between devices, swapped(): return lax.ppermute(shard, axis, [(i, i ^ mask) for i in range(devices)])  76.3 us
    pallas_call x22, Pallas kernels, local(): pl.pallas_call(kernel, out_shape=out_shape, in_specs=[WHOLE] * len(operan...  22.1 us
  transfers between devices with their start and end apart: 67, of which 37 were waited for; matrix products, arithmetic and copies ran while one was open for 1% of the time, Pallas kernels for 12%

profile of v2, /device:TPU:0, one launch (start us, length us, event | category | flops | bytes accessed | tf_op | source)
XLA Modules:
  0.0 200.3 jit_solution(6474613112976903924)
XLA Ops:
  0.6 4.1 %collective-permute-start.5 = (bf16[64,2048]{1,0:T(8,128)(2,1)}, bf16[64,2048]{1,0:T(8,128)(2,1)S(1)}, u32[]{:S(2)}, u32[]{:S(2)}) collective-permute-start(bf16[64,2048]{1,0:T(8,128)(2,1)} %refs_2_.1), channel_id=1, source_target_pairs={{0,8},{1,9},{2,10},{3,11},{4,12},{5,13},{6,14},{7,15},{8,0},{9,1},... | collective-permute-start | bytes 786440 | tf_op jit(solution)/shard_map/ppermute | solution.py:24
  7.7 1.6 collective-permute-start.7
  15.0 3.4 %shard_map.131 = (bf16[128,2048]{1,0:T(8,128)(2,1)}, bf16[128,1024]{1,0:T(8,128)(2,1)S(1)}, bf16[128,1024]{1,0:T(8,128)(2,1)S(1)}) custom-call(s32[2]{0:T(128)S(1)} %pad_add_fusion.here, bf16[128,2048]{1,0:T(8,128)(2,1)S(1)} %copy-done.2, bf16[128,256]{1,0:T(8,128)(2,1)S(1)} %collective-permute-done.keys, ...), custom_call_target="tpu_custom_call" | custom-call | tf_op jit(solution)/shard_map/pallas_call | solution.py:123
  24.4 3.2 %collective-permute-done.11.refs_11_ = bf16[64,2048]{1,0:T(8,128)(2,1)S(1)} collective-permute-done((bf16[64,2048]{1,0:T(8,128)(2,1)S(1)}, bf16[64,2048]{1,0:T(8,128)(2,1)S(1)}, u32[]{:S(2)}, u32[]{:S(2)}) %collective-permute-start.11) | collective-permute-done | bytes 262176 | tf_op jit(solution)/shard_map/ppermute | solution.py:24
  28.6 2.7 %collective-permute-done.13 = f32[1,16,128]{2,1,0:T(8,128)S(1)} collective-permute-done((f32[1,16,128]{2,1,0:T(8,128)S(1)}, f32[1,16,128]{2,1,0:T(8,128)S(1)}, u32[]{:S(2)}, u32[]{:S(2)}) %collective-permute-start.13) | collective-permute-done | bytes 8224 | tf_op jit(solution)/shard_map/ppermute | solution.py:24
  33.2 1.8 collective-permute-done.6.refs_5_
  35.0 3.1 %collective-permute-start.14 = (f32[2,16,128]{2,1,0:T(8,128)S(1)}, f32[2,16,128]{2,1,0:T(8,128)S(1)}, u32[]{:S(2)}, u32[]{:S(2)}) collective-permute-start(f32[2,16,128]{2,1,0:T(8,128)S(1)} %pad_maximum_fusion.2), channel_id=1, source_target_pairs={{0,8},{1,9},{2,10},{3,11},{4,12},{5,13},{6,14},{7,15},{8,0},{9,1},... | collective-permute-start | bytes 49160 | tf_op jit(solution)/shard_map/ppermute | solution.py:24
  43.8 3.6 %collective-permute-done.12.refs_8_ = bf16[64,2048]{1,0:T(8,128)(2,1)S(1)} collective-permute-done((bf16[64,2048]{1,0:T(8,128)(2,1)S(1)}, bf16[64,2048]{1,0:T(8,128)(2,1)S(1)}, u32[]{:S(2)}, u32[]{:S(2)}) %collective-permute-start.12) | collective-permute-done | bytes 262176 | tf_op jit(solution)/shard_map/ppermute | solution.py:24
  48.9 2.8 %collective-permute-done.18.refs_13_ = bf16[64,2048]{1,0:T(8,128)(2,1)S(1)} collective-permute-done((bf16[64,2048]{1,0:T(8,128)(2,1)S(1)}, bf16[64,2048]{1,0:T(8,128)(2,1)S(1)}, u32[]{:S(2)}, u32[]{:S(2)}) %collective-permute-start.18) | collective-permute-done | bytes 262176 | tf_op jit(solution)/shard_map/ppermute | solution.py:24
  52.7 2.0 %shard_map.132 = (f32[128,2048]{1,0:T(8,128)S(1)}, f32[128,2048]{1,0:T(8,128)S(1)}) custom-call(bf16[128,1024]{1,0:T(8,128)(2,1)S(1)} %collective-permute-done.2.refs_0_, bf16[128,1024]{1,0:T(8,128)(2,1)S(1)} %get-tuple-element.123.refs_1_, bf16[64,2048]{1,0:T(8,128)(2,1)S(1)} %copy-done.4, bf16[64,2048]{1,0:T(8,128)(2,1)S(1)} %collective-permute-done.3.refs_3_, ...), custom_call_target="tpu_custom_call" | custom-call | tf_op jit(solution)/shard_map/pallas_call | solution.py:206
  56.4 2.4 %collective-permute-done.21 = f32[4,16,128]{2,1,0:T(8,128)S(1)} collective-permute-done((f32[4,16,128]{2,1,0:T(8,128)S(1)}, f32[4,16,128]{2,1,0:T(8,128)S(1)}, u32[]{:S(2)}, u32[]{:S(2)}) %collective-permute-start.21) | collective-permute-done | bytes 32800 | tf_op jit(solution)/shard_map/ppermute | solution.py:24
  59.7 3.3 %collective-permute-done.22 = f32[8,16,128]{2,1,0:T(8,128)S(1)} collective-permute-done((f32[8,16,128]{2,1,0:T(8,128)S(1)}, f32[8,16,128]{2,1,0:T(8,128)S(1)}, u32[]{:S(2)}, u32[]{:S(2)}) %collective-permute-start.22) | collective-permute-done | bytes 65568 | tf_op jit(solution)/shard_map/ppermute | solution.py:24
  65.9 1.6 collective-permute-start.24
  67.5 1.7 collective-permute-start.23
  70.6 2.4 %collective-permute-done.25.left.refs_2_ = bf16[128,1024]{1,0:T(8,128)(2,1)S(1)} collective-permute-done((bf16[128,1024]{1,0:T(8,128)(2,1)S(1)}, bf16[128,1024]{1,0:T(8,128)(2,1)S(1)}, u32[]{:S(2)}, u32[]{:S(2)}) %collective-permute-start.25) | collective-permute-done | bytes 262176 | tf_op jit(solution)/shard_map/ppermute | solution.py:24
  73.0 2.7 %collective-permute-start.32 = (bf16[128,1024]{1,0:T(8,128)(2,1)S(1)}, bf16[128,1024]{1,0:T(8,128)(2,1)S(1)}, u32[]{:S(2)}, u32[]{:S(2)}) collective-permute-start(bf16[128,1024]{1,0:T(8,128)(2,1)S(1)} %get-tuple-element.152.right.refs_1_), channel_id=1, source_target_pairs={{0,8},{1,9},{2,10},{3,11},{4,12},{5,13},{6,14},{7,15},{8,0},{9,1},... | collective-permute-start | bytes 786440 | tf_op jit(solution)/shard_map/ppermute | solution.py:24
  76.2 6.2 %collective-permute-done.24.left.refs_0_ = bf16[128,1024]{1,0:T(8,128)(2,1)S(1)} collective-permute-done((bf16[128,1024]{1,0:T(8,128)(2,1)S(1)}, bf16[128,1024]{1,0:T(8,128)(2,1)S(1)}, u32[]{:S(2)}, u32[]{:S(2)}) %collective-permute-start.24) | collective-permute-done | bytes 262176 | tf_op jit(solution)/shard_map/ppermute | solution.py:24
  85.6 5.3 %collective-permute-done.33.right.refs_1_ = bf16[128,1024]{1,0:T(8,128)(2,1)S(1)} collective-permute-done((bf16[128,1024]{1,0:T(8,128)(2,1)S(1)}, bf16[128,1024]{1,0:T(8,128)(2,1)S(1)}, u32[]{:S(2)}, u32[]{:S(2)}) %collective-permute-start.33) | collective-permute-done | bytes 262176 | tf_op jit(solution)/shard_map/ppermute | solution.py:24
  96.5 1.6 collective-permute-start.42
  99.2 2.2 %collective-permute-start.41 = (bf16[72,2048]{1,0:T(8,128)(2,1)S(1)}, bf16[72,2048]{1,0:T(8,128)(2,1)S(1)}, u32[]{:S(2)}, u32[]{:S(2)}) collective-permute-start(bf16[72,2048]{1,0:T(8,128)(2,1)S(1)} %shard_map.138), channel_id=1, source_target_pairs={{0,1},{1,0},{2,3},{3,2},{4,5},{5,4},{6,7},{7,6},{8,9},{9,8},{10,11... | collective-permute-start | bytes 884744 | tf_op jit(solution)/shard_map/ppermute | solution.py:24
  102.0 5.2 %collective-permute-done.27.left.refs_2_ = bf16[128,1024]{1,0:T(8,128)(2,1)S(1)} collective-permute-done((bf16[128,1024]{1,0:T(8,128)(2,1)S(1)}, bf16[128,1024]{1,0:T(8,128)(2,1)S(1)}, u32[]{:S(2)}, u32[]{:S(2)}) %collective-permute-start.27) | collective-permute-done | bytes 262176 | tf_op jit(solution)/shard_map/ppermute | solution.py:24
  107.6 1.6 collective-permute-start.40
  109.5 3.3 %collective-permute-done.35.left.refs_2_ = bf16[128,1024]{1,0:T(8,128)(2,1)S(1)} collective-permute-done((bf16[128,1024]{1,0:T(8,128)(2,1)S(1)}, bf16[128,1024]{1,0:T(8,128)(2,1)S(1)}, u32[]{:S(2)}, u32[]{:S(2)}) %collective-permute-start.35) | collective-permute-done | bytes 262176 | tf_op jit(solution)/shard_map/ppermute | solution.py:24
  113.3 3.7 %collective-permute-done.34.right.refs_3_ = bf16[128,1024]{1,0:T(8,128)(2,1)S(1)} collective-permute-done((bf16[128,1024]{1,0:T(8,128)(2,1)S(1)}, bf16[128,1024]{1,0:T(8,128)(2,1)S(1)}, u32[]{:S(2)}, u32[]{:S(2)}) %collective-permute-start.34) | collective-permute-done | bytes 262176 | tf_op jit(solution)/shard_map/ppermute | solution.py:24
  120.0 1.6 collective-permute-start.43
  122.5 4.7 %collective-permute-done.38.refs_5_ = bf16[72,2048]{1,0:T(8,128)(2,1)S(1)} collective-permute-done((bf16[72,2048]{1,0:T(8,128)(2,1)S(1)}, bf16[72,2048]{1,0:T(8,128)(2,1)S(1)}, u32[]{:S(2)}, u32[]{:S(2)}) %collective-permute-start.38) | collective-permute-done | bytes 294944 | tf_op jit(solution)/shard_map/ppermute | solution.py:24
  127.3 4.0 %shard_map.143 = (f32[256,2048]{1,0:T(8,128)S(1)}, bf16[72,2048]{1,0:T(8,128)(2,1)S(1)}, bf16[72,2048]{1,0:T(8,128)(2,1)S(1)}) custom-call(bf16[128,1024]{1,0:T(8,128)(2,1)S(1)} %get-tuple-element.179.left.refs_0_, bf16[128,1024]{1,0:T(8,128)(2,1)S(1)} %get-tuple-element.152.right.refs_1_, bf16[128,1024]{1,0:T(8,128)(2,1)S(1)} %collective-permute-done.25.left.refs_2_, ...), custom_call_target="tpu_custom_call" | custom-call | tf_op jit(solution)/shard_map/pallas_call | solution.py:40
  132.7 4.0 %shard_map.144 = (f32[256,2048]{1,0:T(8,128)S(1)}, bf16[72,2048]{1,0:T(8,128)(2,1)S(1)}, bf16[72,2048]{1,0:T(8,128)(2,1)S(1)}) custom-call(bf16[128,1024]{1,0:T(8,128)(2,1)S(1)} %collective-permute-done.28.left.refs_0_, bf16[128,1024]{1,0:T(8,128)(2,1)S(1)} %collective-permute-done.36.right.refs_1_, ...), custom_call_target="tpu_custom_call" | custom-call | tf_op jit(solution)/shard_map/pallas_call | solution.py:40
  136.9 1.7 collective-permute-start.45
  138.9 4.2 %shard_map.145 = (f32[256,2048]{1,0:T(8,128)S(1)}, bf16[72,2048]{1,0:T(8,128)(2,1)S(1)}, bf16[72,2048]{1,0:T(8,128)(2,1)S(1)}) custom-call(bf16[128,1024]{1,0:T(8,128)(2,1)S(1)} %collective-permute-done.23.left.refs_0_, bf16[128,1024]{1,0:T(8,128)(2,1)S(1)} %collective-permute-done.32.right.refs_1_, ...), custom_call_target="tpu_custom_call" | custom-call | tf_op jit(solution)/shard_map/pallas_call | solution.py:40
  143.1 1.8 collective-permute-start.51
  144.9 1.9 collective-permute-done.45.returned
  147.1 1.6 collective-permute-start.50
  149.2 1.7 collective-permute-start.47
  151.0 4.0 %shard_map.147 = (f32[256,2048]{1,0:T(8,128)S(1)}, bf16[72,2048]{1,0:T(8,128)(2,1)S(1)}, bf16[72,2048]{1,0:T(8,128)(2,1)S(1)}) custom-call(bf16[128,1024]{1,0:T(8,128)(2,1)S(1)} %collective-permute-done.24.left.refs_0_, bf16[128,1024]{1,0:T(8,128)(2,1)S(1)} %collective-permute-done.33.right.refs_1_, ...), custom_call_target="tpu_custom_call" | custom-call | tf_op jit(solution)/shard_map/pallas_call | solution.py:40
  155.7 3.8 %collective-permute-done.51.returned = bf16[72,2048]{1,0:T(8,128)(2,1)S(1)} collective-permute-done((bf16[72,2048]{1,0:T(8,128)(2,1)S(1)}, bf16[72,2048]{1,0:T(8,128)(2,1)S(1)}, u32[]{:S(2)}, u32[]{:S(2)}) %collective-permute-start.51) | collective-permute-done | bytes 294944 | tf_op jit(solution)/shard_map/ppermute | solution.py:24
  159.8 1.6 collective-permute-start.53
  161.5 1.6 collective-permute-start.55
  166.0 3.3 %collective-permute-done.54.returned = bf16[72,2048]{1,0:T(8,128)(2,1)S(1)} collective-permute-done((bf16[72,2048]{1,0:T(8,128)(2,1)S(1)}, bf16[72,2048]{1,0:T(8,128)(2,1)S(1)}, u32[]{:S(2)}, u32[]{:S(2)}) %collective-permute-start.54) | collective-permute-done | bytes 294944 | tf_op jit(solution)/shard_map/ppermute | solution.py:24
  169.3 1.7 collective-permute-start.46
  171.9 1.6 collective-permute-start.63
  173.6 2.7 %collective-permute-start.62 = (bf16[128,1024]{1,0:T(8,128)(2,1)S(1)}, bf16[128,1024]{1,0:T(8,128)(2,1)S(1)}, u32[]{:S(2)}, u32[]{:S(2)}) collective-permute-start(bf16[128,1024]{1,0:T(8,128)(2,1)S(1)} %add_convert_fusion.3), channel_id=1, source_target_pairs={{0,8},{1,9},{2,10},{3,11},{4,12},{5,13},{6,14},{7,15},{8,0},{9,1},... | collective-permute-start | bytes 786440 | tf_op jit(solution)/shard_map/ppermute | solution.py:24
  176.4 2.1 %collective-permute-done.46.returned = bf16[72,2048]{1,0:T(8,128)(2,1)S(1)} collective-permute-done((bf16[72,2048]{1,0:T(8,128)(2,1)S(1)}, bf16[72,2048]{1,0:T(8,128)(2,1)S(1)}, u32[]{:S(2)}, u32[]{:S(2)}) %collective-permute-start.46) | collective-permute-done | bytes 294944 | tf_op jit(solution)/shard_map/ppermute | solution.py:24
  181.6 2.1 %collective-permute-start.59 = (bf16[128,1024]{1,0:T(8,128)(2,1)S(1)}, bf16[128,1024]{1,0:T(8,128)(2,1)S(1)}, u32[]{:S(2)}, u32[]{:S(2)}) collective-permute-start(bf16[128,1024]{1,0:T(8,128)(2,1)S(1)} %add_convert_fusion.1), channel_id=1, source_target_pairs={{0,4},{1,5},{2,6},{3,7},{4,0},{5,1},{6,2},{7,3},{8,12},{9,13},{10,... | collective-permute-start | bytes 786440 | tf_op jit(solution)/shard_map/ppermute | solution.py:24
  183.8 5.0 %collective-permute-done.62.refs_2_ = bf16[128,1024]{1,0:T(8,128)(2,1)S(1)} collective-permute-done((bf16[128,1024]{1,0:T(8,128)(2,1)S(1)}, bf16[128,1024]{1,0:T(8,128)(2,1)S(1)}, u32[]{:S(2)}, u32[]{:S(2)}) %collective-permute-start.62) | collective-permute-done | bytes 262176 | tf_op jit(solution)/shard_map/ppermute | solution.py:24
  189.1 3.0 %collective-permute-done.60.refs_3_ = bf16[128,1024]{1,0:T(8,128)(2,1)S(1)} collective-permute-done((bf16[128,1024]{1,0:T(8,128)(2,1)S(1)}, bf16[128,1024]{1,0:T(8,128)(2,1)S(1)}, u32[]{:S(2)}, u32[]{:S(2)}) %collective-permute-start.60) | collective-permute-done | bytes 262176 | tf_op jit(solution)/shard_map/ppermute | solution.py:24
  192.6 2.8 %collective-permute-done.59.refs_4_ = bf16[128,1024]{1,0:T(8,128)(2,1)S(1)} collective-permute-done((bf16[128,1024]{1,0:T(8,128)(2,1)S(1)}, bf16[128,1024]{1,0:T(8,128)(2,1)S(1)}, u32[]{:S(2)}, u32[]{:S(2)}) %collective-permute-start.59) | collective-permute-done | bytes 262176 | tf_op jit(solution)/shard_map/ppermute | solution.py:24
  195.7 2.5 %collective-permute-done.64.refs_5_ = bf16[128,1024]{1,0:T(8,128)(2,1)S(1)} collective-permute-done((bf16[128,1024]{1,0:T(8,128)(2,1)S(1)}, bf16[128,1024]{1,0:T(8,128)(2,1)S(1)}, u32[]{:S(2)}, u32[]{:S(2)}) %collective-permute-start.64) | collective-permute-done | bytes 262176 | tf_op jit(solution)/shard_map/ppermute | solution.py:24
  (148 shorter events, 62.5 us)
Async XLA Ops:
  0.6 17.8 %collective-permute-start.5 = (bf16[64,2048]{1,0:T(8,128)(2,1)}, bf16[64,2048]{1,0:T(8,128)(2,1)S(1)}, u32[]{:S(2)}, u32[]{:S(2)}) collective-permute-start(bf16[64,2048]{1,0:T(8,128)(2,1)} %refs_2_.1), channel_id=1, source_target_pairs={{0,8},{1,9},{2,10},{3,11},{4,12},{5,13},{6,14},{7,15},{8,0},{9,1},... | collective-permute-start | bytes 786440 | tf_op jit(solution)/shard_map/ppermute | solution.py:24
  4.7 15.4 %collective-permute-start.4 = (bf16[64,2048]{1,0:T(8,128)(2,1)}, bf16[64,2048]{1,0:T(8,128)(2,1)S(1)}, u32[]{:S(2)}, u32[]{:S(2)}) collective-permute-start(bf16[64,2048]{1,0:T(8,128)(2,1)} %refs_2_.1), channel_id=1, source_target_pairs={{0,2},{1,3},{2,0},{3,1},{4,6},{5,7},{6,4},{7,5},{8,10},{9,11},{10,... | collective-permute-start | bytes 786440 | tf_op jit(solution)/shard_map/ppermute | solution.py:24
  6.3 15.1 %collective-permute-start.3 = (bf16[64,2048]{1,0:T(8,128)(2,1)}, bf16[64,2048]{1,0:T(8,128)(2,1)S(1)}, u32[]{:S(2)}, u32[]{:S(2)}) collective-permute-start(bf16[64,2048]{1,0:T(8,128)(2,1)} %refs_2_.1), channel_id=1, source_target_pairs={{0,1},{1,0},{2,3},{3,2},{4,5},{5,4},{6,7},{7,6},{8,9},{9,8},{10,11... | collective-permute-start | bytes 786440 | tf_op jit(solution)/shard_map/ppermute | solution.py:24
  7.7 14.4 %collective-permute-start.7 = (bf16[64,2048]{1,0:T(8,128)(2,1)}, bf16[64,2048]{1,0:T(8,128)(2,1)S(1)}, u32[]{:S(2)}, u32[]{:S(2)}) collective-permute-start(bf16[64,2048]{1,0:T(8,128)(2,1)} %refs_2_.1), channel_id=1, source_target_pairs={{0,4},{1,5},{2,6},{3,7},{4,0},{5,1},{6,2},{7,3},{8,12},{9,13},{10,... | collective-permute-start | bytes 786440 | tf_op jit(solution)/shard_map/ppermute | solution.py:24
  20.1 11.7 %collective-permute-start.9 = (bf16[64,2048]{1,0:T(8,128)(2,1)S(1)}, bf16[64,2048]{1,0:T(8,128)(2,1)S(1)}, u32[]{:S(2)}, u32[]{:S(2)}) collective-permute-start(bf16[64,2048]{1,0:T(8,128)(2,1)S(1)} %collective-permute-done.5.refs_10_), channel_id=1, source_target_pairs={{0,2},{1,3},{2,0},{3,1},{4,6},{5,7},{6,4},{7,5},{8,10},{9,11},{10,... | collective-permute-start | bytes 786440 | tf_op jit(solution)/shard_map/ppermute | solution.py:24
  21.4 13.6 %collective-permute-start.6 = (bf16[64,2048]{1,0:T(8,128)(2,1)S(1)}, bf16[64,2048]{1,0:T(8,128)(2,1)S(1)}, u32[]{:S(2)}, u32[]{:S(2)}) collective-permute-start(bf16[64,2048]{1,0:T(8,128)(2,1)S(1)} %collective-permute-done.3.refs_3_), channel_id=1, source_target_pairs={{0,2},{1,3},{2,0},{3,1},{4,6},{5,7},{6,4},{7,5},{8,10},{9,11},{10,... | collective-permute-start | bytes 786440 | tf_op jit(solution)/shard_map/ppermute | solution.py:24
  22.2 11.1 %collective-permute-start.8 = (bf16[64,2048]{1,0:T(8,128)(2,1)S(1)}, bf16[64,2048]{1,0:T(8,128)(2,1)S(1)}, u32[]{:S(2)}, u32[]{:S(2)}) collective-permute-start(bf16[64,2048]{1,0:T(8,128)(2,1)S(1)} %collective-permute-done.7.refs_6_), channel_id=1, source_target_pairs={{0,1},{1,0},{2,3},{3,2},{4,5},{5,4},{6,7},{7,6},{8,9},{9,8},{10,11... | collective-permute-start | bytes 786440 | tf_op jit(solution)/shard_map/ppermute | solution.py:24
  28.1 12.5 %collective-permute-start.16 = (bf16[64,2048]{1,0:T(8,128)(2,1)S(1)}, bf16[64,2048]{1,0:T(8,128)(2,1)S(1)}, u32[]{:S(2)}, u32[]{:S(2)}) collective-permute-start(bf16[64,2048]{1,0:T(8,128)(2,1)S(1)} %collective-permute-done.10.refs_14_), channel_id=1, source_target_pairs={{0,2},{1,3},{2,0},{3,1},{4,6},{5,7},{6,4},{7,5},{8,10},{9,11},{10,... | collective-permute-start | bytes 786440 | tf_op jit(solution)/shard_map/ppermute | solution.py:24
  31.3 12.5 %collective-permute-start.15 = (bf16[64,2048]{1,0:T(8,128)(2,1)S(1)}, bf16[64,2048]{1,0:T(8,128)(2,1)S(1)}, u32[]{:S(2)}, u32[]{:S(2)}) collective-permute-start(bf16[64,2048]{1,0:T(8,128)(2,1)S(1)} %collective-permute-done.10.refs_14_), channel_id=1, source_target_pairs={{0,1},{1,0},{2,3},{3,2},{4,5},{5,4},{6,7},{7,6},{8,9},{9,8},{10,11... | collective-permute-start | bytes 786440 | tf_op jit(solution)/shard_map/ppermute | solution.py:24
  38.1 9.2 %collective-permute-start.12 = (bf16[64,2048]{1,0:T(8,128)(2,1)S(1)}, bf16[64,2048]{1,0:T(8,128)(2,1)S(1)}, u32[]{:S(2)}, u32[]{:S(2)}) collective-permute-start(bf16[64,2048]{1,0:T(8,128)(2,1)S(1)} %collective-permute-done.7.refs_6_), channel_id=1, source_target_pairs={{0,2},{1,3},{2,0},{3,1},{4,6},{5,7},{6,4},{7,5},{8,10},{9,11},{10,... | collective-permute-start | bytes 786440 | tf_op jit(solution)/shard_map/ppermute | solution.py:24
  42.1 9.6 %collective-permute-start.18 = (bf16[64,2048]{1,0:T(8,128)(2,1)S(1)}, bf16[64,2048]{1,0:T(8,128)(2,1)S(1)}, u32[]{:S(2)}, u32[]{:S(2)}) collective-permute-start(bf16[64,2048]{1,0:T(8,128)(2,1)S(1)} %collective-permute-done.9.refs_12_), channel_id=1, source_target_pairs={{0,1},{1,0},{2,3},{3,2},{4,5},{5,4},{6,7},{7,6},{8,9},{9,8},{10,11... | collective-permute-start | bytes 786440 | tf_op jit(solution)/shard_map/ppermute | solution.py:24
  64.8 11.1 %collective-permute-start.26 = (bf16[128,1024]{1,0:T(8,128)(2,1)S(1)}, bf16[128,1024]{1,0:T(8,128)(2,1)S(1)}, u32[]{:S(2)}, u32[]{:S(2)}) collective-permute-start(bf16[128,1024]{1,0:T(8,128)(2,1)S(1)} %get-tuple-element.152.right.refs_1_), channel_id=1, source_target_pairs={{0,2},{1,3},{2,0},{3,1},{4,6},{5,7},{6,4},{7,5},{8,10},{9,11},{10,... | collective-permute-start | bytes 786440 | tf_op jit(solution)/shard_map/ppermute | solution.py:24
  65.9 16.5 %collective-permute-start.24 = (bf16[128,1024]{1,0:T(8,128)(2,1)S(1)}, bf16[128,1024]{1,0:T(8,128)(2,1)S(1)}, u32[]{:S(2)}, u32[]{:S(2)}) collective-permute-start(bf16[128,1024]{1,0:T(8,128)(2,1)S(1)} %get-tuple-element.179.left.refs_0_), channel_id=1, source_target_pairs={{0,4},{1,5},{2,6},{3,7},{4,0},{5,1},{6,2},{7,3},{8,12},{9,13},{10,... | collective-permute-start | bytes 786440 | tf_op jit(solution)/shard_map/ppermute | solution.py:24
  67.5 15.7 %collective-permute-start.23 = (bf16[128,1024]{1,0:T(8,128)(2,1)S(1)}, bf16[128,1024]{1,0:T(8,128)(2,1)S(1)}, u32[]{:S(2)}, u32[]{:S(2)}) collective-permute-start(bf16[128,1024]{1,0:T(8,128)(2,1)S(1)} %get-tuple-element.179.left.refs_0_), channel_id=1, source_target_pairs={{0,8},{1,9},{2,10},{3,11},{4,12},{5,13},{6,14},{7,15},{8,0},{9,1},... | collective-permute-start | bytes 786440 | tf_op jit(solution)/shard_map/ppermute | solution.py:24
  69.2 21.7 %collective-permute-start.33 = (bf16[128,1024]{1,0:T(8,128)(2,1)S(1)}, bf16[128,1024]{1,0:T(8,128)(2,1)S(1)}, u32[]{:S(2)}, u32[]{:S(2)}) collective-permute-start(bf16[128,1024]{1,0:T(8,128)(2,1)S(1)} %get-tuple-element.152.right.refs_1_), channel_id=1, source_target_pairs={{0,4},{1,5},{2,6},{3,7},{4,0},{5,1},{6,2},{7,3},{8,12},{9,13},{10,... | collective-permute-start | bytes 786440 | tf_op jit(solution)/shard_map/ppermute | solution.py:24
  73.0 19.3 %collective-permute-start.32 = (bf16[128,1024]{1,0:T(8,128)(2,1)S(1)}, bf16[128,1024]{1,0:T(8,128)(2,1)S(1)}, u32[]{:S(2)}, u32[]{:S(2)}) collective-permute-start(bf16[128,1024]{1,0:T(8,128)(2,1)S(1)} %get-tuple-element.152.right.refs_1_), channel_id=1, source_target_pairs={{0,8},{1,9},{2,10},{3,11},{4,12},{5,13},{6,14},{7,15},{8,0},{9,1},... | collective-permute-start | bytes 786440 | tf_op jit(solution)/shard_map/ppermute | solution.py:24
  83.1 11.0 %collective-permute-start.28 = (bf16[128,1024]{1,0:T(8,128)(2,1)S(1)}, bf16[128,1024]{1,0:T(8,128)(2,1)S(1)}, u32[]{:S(2)}, u32[]{:S(2)}) collective-permute-start(bf16[128,1024]{1,0:T(8,128)(2,1)S(1)} %collective-permute-done.23.left.refs_0_), channel_id=1, source_target_pairs={{0,4},{1,5},{2,6},{3,7},{4,0},{5,1},{6,2},{7,3},{8,12},{9,13},{10,... | collective-permute-start | bytes 786440 | tf_op jit(solution)/shard_map/ppermute | solution.py:24
  83.6 11.8 %collective-permute-start.29 = (bf16[128,1024]{1,0:T(8,128)(2,1)S(1)}, bf16[128,1024]{1,0:T(8,128)(2,1)S(1)}, u32[]{:S(2)}, u32[]{:S(2)}) collective-permute-start(bf16[128,1024]{1,0:T(8,128)(2,1)S(1)} %collective-permute-done.24.left.refs_0_), channel_id=1, source_target_pairs={{0,2},{1,3},{2,0},{3,1},{4,6},{5,7},{6,4},{7,5},{8,10},{9,11},{10,... | collective-permute-start | bytes 786440 | tf_op jit(solution)/shard_map/ppermute | solution.py:24
  85.1 11.4 %collective-permute-start.30 = (bf16[72,2048]{1,0:T(8,128)(2,1)S(1)}, bf16[72,2048]{1,0:T(8,128)(2,1)S(1)}, u32[]{:S(2)}, u32[]{:S(2)}) collective-permute-start(bf16[72,2048]{1,0:T(8,128)(2,1)S(1)} %shard_map.136), channel_id=1, source_target_pairs={{0,1},{1,0},{2,3},{3,2},{4,5},{5,4},{6,7},{7,6},{8,9},{9,8},{10,11... | collective-permute-start | bytes 884744 | tf_op jit(solution)/shard_map/ppermute | solution.py:24
  94.2 13.1 %collective-permute-start.27 = (bf16[128,1024]{1,0:T(8,128)(2,1)S(1)}, bf16[128,1024]{1,0:T(8,128)(2,1)S(1)}, u32[]{:S(2)}, u32[]{:S(2)}) collective-permute-start(bf16[128,1024]{1,0:T(8,128)(2,1)S(1)} %collective-permute-done.23.left.refs_0_), channel_id=1, source_target_pairs={{0,2},{1,3},{2,0},{3,1},{4,6},{5,7},{6,4},{7,5},{8,10},{9,11},{10,... | collective-permute-start | bytes 786440 | tf_op jit(solution)/shard_map/ppermute | solution.py:24
  95.4 12.3 %collective-permute-start.36 = (bf16[128,1024]{1,0:T(8,128)(2,1)S(1)}, bf16[128,1024]{1,0:T(8,128)(2,1)S(1)}, u32[]{:S(2)}, u32[]{:S(2)}) collective-permute-start(bf16[128,1024]{1,0:T(8,128)(2,1)S(1)} %collective-permute-done.32.right.refs_1_), channel_id=1, source_target_pairs={{0,4},{1,5},{2,6},{3,7},{4,0},{5,1},{6,2},{7,3},{8,12},{9,13},{10,... | collective-permute-start | bytes 786440 | tf_op jit(solution)/shard_map/ppermute | solution.py:24
  96.5 22.3 %collective-permute-start.42 = (bf16[72,2048]{1,0:T(8,128)(2,1)S(1)}, bf16[72,2048]{1,0:T(8,128)(2,1)S(1)}, u32[]{:S(2)}, u32[]{:S(2)}) collective-permute-start(bf16[72,2048]{1,0:T(8,128)(2,1)S(1)} %shard_map.137), channel_id=1, source_target_pairs={{0,1},{1,0},{2,3},{3,2},{4,5},{5,4},{6,7},{7,6},{8,9},{9,8},{10,11... | collective-permute-start | bytes 884744 | tf_op jit(solution)/shard_map/ppermute | solution.py:24
  99.2 19.6 %collective-permute-start.41 = (bf16[72,2048]{1,0:T(8,128)(2,1)S(1)}, bf16[72,2048]{1,0:T(8,128)(2,1)S(1)}, u32[]{:S(2)}, u32[]{:S(2)}) collective-permute-start(bf16[72,2048]{1,0:T(8,128)(2,1)S(1)} %shard_map.138), channel_id=1, source_target_pairs={{0,1},{1,0},{2,3},{3,2},{4,5},{5,4},{6,7},{7,6},{8,9},{9,8},{10,11... | collective-permute-start | bytes 884744 | tf_op jit(solution)/shard_map/ppermute | solution.py:24
  101.6 11.2 %collective-permute-start.35 = (bf16[128,1024]{1,0:T(8,128)(2,1)S(1)}, bf16[128,1024]{1,0:T(8,128)(2,1)S(1)}, u32[]{:S(2)}, u32[]{:S(2)}) collective-permute-start(bf16[128,1024]{1,0:T(8,128)(2,1)S(1)} %collective-permute-done.28.left.refs_0_), channel_id=1, source_target_pairs={{0,2},{1,3},{2,0},{3,1},{4,6},{5,7},{6,4},{7,5},{8,10},{9,11},{10,... | collective-permute-start | bytes 786440 | tf_op jit(solution)/shard_map/ppermute | solution.py:24
  107.2 9.8 %collective-permute-start.34 = (bf16[128,1024]{1,0:T(8,128)(2,1)S(1)}, bf16[128,1024]{1,0:T(8,128)(2,1)S(1)}, u32[]{:S(2)}, u32[]{:S(2)}) collective-permute-start(bf16[128,1024]{1,0:T(8,128)(2,1)S(1)} %collective-permute-done.32.right.refs_1_), channel_id=1, source_target_pairs={{0,2},{1,3},{2,0},{3,1},{4,6},{5,7},{6,4},{7,5},{8,10},{9,11},{10,... | collective-permute-start | bytes 786440 | tf_op jit(solution)/shard_map/ppermute | solution.py:24
  107.6 12.2 %collective-permute-start.40 = (bf16[128,1024]{1,0:T(8,128)(2,1)S(1)}, bf16[128,1024]{1,0:T(8,128)(2,1)S(1)}, u32[]{:S(2)}, u32[]{:S(2)}) collective-permute-start(bf16[128,1024]{1,0:T(8,128)(2,1)S(1)} %collective-permute-done.36.right.refs_1_), channel_id=1, source_target_pairs={{0,2},{1,3},{2,0},{3,1},{4,6},{5,7},{6,4},{7,5},{8,10},{9,11},{10,... | collective-permute-start | bytes 786440 | tf_op jit(solution)/shard_map/ppermute | solution.py:24
  112.8 9.6 %collective-permute-start.39 = (bf16[72,2048]{1,0:T(8,128)(2,1)S(1)}, bf16[72,2048]{1,0:T(8,128)(2,1)S(1)}, u32[]{:S(2)}, u32[]{:S(2)}) collective-permute-start(bf16[72,2048]{1,0:T(8,128)(2,1)S(1)} %shard_map.139), channel_id=1, source_target_pairs={{0,1},{1,0},{2,3},{3,2},{4,5},{5,4},{6,7},{7,6},{8,9},{9,8},{10,11... | collective-permute-start | bytes 884744 | tf_op jit(solution)/shard_map/ppermute | solution.py:24
  117.2 10.0 %collective-permute-start.38 = (bf16[72,2048]{1,0:T(8,128)(2,1)S(1)}, bf16[72,2048]{1,0:T(8,128)(2,1)S(1)}, u32[]{:S(2)}, u32[]{:S(2)}) collective-permute-start(bf16[72,2048]{1,0:T(8,128)(2,1)S(1)} %shard_map.140), channel_id=1, source_target_pairs={{0,1},{1,0},{2,3},{3,2},{4,5},{5,4},{6,7},{7,6},{8,9},{9,8},{10,11... | collective-permute-start | bytes 884744 | tf_op jit(solution)/shard_map/ppermute | solution.py:24
  120.0 12.7 %collective-permute-start.43 = (bf16[72,2048]{1,0:T(8,128)(2,1)S(1)}, bf16[72,2048]{1,0:T(8,128)(2,1)S(1)}, u32[]{:S(2)}, u32[]{:S(2)}) collective-permute-start(bf16[72,2048]{1,0:T(8,128)(2,1)S(1)} %shard_map.141), channel_id=1, source_target_pairs={{0,1},{1,0},{2,3},{3,2},{4,5},{5,4},{6,7},{7,6},{8,9},{9,8},{10,11... | collective-permute-start | bytes 884744 | tf_op jit(solution)/shard_map/ppermute | solution.py:24
  121.8 15.0 %collective-permute-start.44 = (bf16[72,2048]{1,0:T(8,128)(2,1)S(1)}, bf16[72,2048]{1,0:T(8,128)(2,1)S(1)}, u32[]{:S(2)}, u32[]{:S(2)}) collective-permute-start(bf16[72,2048]{1,0:T(8,128)(2,1)S(1)} %shard_map.142), channel_id=1, source_target_pairs={{0,1},{1,0},{2,3},{3,2},{4,5},{5,4},{6,7},{7,6},{8,9},{9,8},{10,11... | collective-permute-start | bytes 884744 | tf_op jit(solution)/shard_map/ppermute | solution.py:24
  136.9 9.9 %collective-permute-start.45 = (bf16[72,2048]{1,0:T(8,128)(2,1)S(1)}, bf16[72,2048]{1,0:T(8,128)(2,1)S(1)}, u32[]{:S(2)}, u32[]{:S(2)}) collective-permute-start(bf16[72,2048]{1,0:T(8,128)(2,1)S(1)} %get-tuple-element.189), channel_id=1, source_target_pairs={{0,1},{1,0},{2,3},{3,2},{4,5},{5,4},{6,7},{7,6},{8,9},{9,8},{10,11... | collective-permute-start | bytes 884744 | tf_op jit(solution)/shard_map/ppermute | solution.py:24
  138.6 16.4 %collective-permute-start.48 = (bf16[72,2048]{1,0:T(8,128)(2,1)S(1)}, bf16[72,2048]{1,0:T(8,128)(2,1)S(1)}, u32[]{:S(2)}, u32[]{:S(2)}) collective-permute-start(bf16[72,2048]{1,0:T(8,128)(2,1)S(1)} %get-tuple-element.190), channel_id=1, source_target_pairs={{0,1},{1,0},{2,3},{3,2},{4,5},{5,4},{6,7},{7,6},{8,9},{9,8},{10,11... | collective-permute-start | bytes 884744 | tf_op jit(solution)/shard_map/ppermute | solution.py:24
  143.1 16.3 %collective-permute-start.51 = (bf16[72,2048]{1,0:T(8,128)(2,1)S(1)}, bf16[72,2048]{1,0:T(8,128)(2,1)S(1)}, u32[]{:S(2)}, u32[]{:S(2)}) collective-permute-start(bf16[72,2048]{1,0:T(8,128)(2,1)S(1)} %get-tuple-element.194), channel_id=1, source_target_pairs={{0,1},{1,0},{2,3},{3,2},{4,5},{5,4},{6,7},{7,6},{8,9},{9,8},{10,11... | collective-permute-start | bytes 884744 | tf_op jit(solution)/shard_map/ppermute | solution.py:24
  147.1 14.2 %collective-permute-start.50 = (bf16[128,1024]{1,0:T(8,128)(2,1)S(1)}, bf16[128,1024]{1,0:T(8,128)(2,1)S(1)}, u32[]{:S(2)}, u32[]{:S(2)}) collective-permute-start(bf16[128,1024]{1,0:T(8,128)(2,1)S(1)} %get-tuple-element.197), channel_id=1, source_target_pairs={{0,2},{1,3},{2,0},{3,1},{4,6},{5,7},{6,4},{7,5},{8,10},{9,11},{10,... | collective-permute-start | bytes 786440 | tf_op jit(solution)/shard_map/ppermute | solution.py:24
  148.8 14.3 %collective-permute-start.49 = (bf16[128,1024]{1,0:T(8,128)(2,1)S(1)}, bf16[128,1024]{1,0:T(8,128)(2,1)S(1)}, u32[]{:S(2)}, u32[]{:S(2)}) collective-permute-start(bf16[128,1024]{1,0:T(8,128)(2,1)S(1)} %get-tuple-element.207), channel_id=1, source_target_pairs={{0,2},{1,3},{2,0},{3,1},{4,6},{5,7},{6,4},{7,5},{8,10},{9,11},{10,... | collective-permute-start | bytes 786440 | tf_op jit(solution)/shard_map/ppermute | solution.py:24
  149.2 15.1 %collective-permute-start.47 = (bf16[72,2048]{1,0:T(8,128)(2,1)S(1)}, bf16[72,2048]{1,0:T(8,128)(2,1)S(1)}, u32[]{:S(2)}, u32[]{:S(2)}) collective-permute-start(bf16[72,2048]{1,0:T(8,128)(2,1)S(1)} %get-tuple-element.195), channel_id=1, source_target_pairs={{0,1},{1,0},{2,3},{3,2},{4,5},{5,4},{6,7},{7,6},{8,9},{9,8},{10,11... | collective-permute-start | bytes 884744 | tf_op jit(solution)/shard_map/ppermute | solution.py:24
  155.0 14.3 %collective-permute-start.54 = (bf16[72,2048]{1,0:T(8,128)(2,1)S(1)}, bf16[72,2048]{1,0:T(8,128)(2,1)S(1)}, u32[]{:S(2)}, u32[]{:S(2)}) collective-permute-start(bf16[72,2048]{1,0:T(8,128)(2,1)S(1)} %get-tuple-element.202), channel_id=1, source_target_pairs={{0,1},{1,0},{2,3},{3,2},{4,5},{5,4},{6,7},{7,6},{8,9},{9,8},{10,11... | collective-permute-start | bytes 884744 | tf_op jit(solution)/shard_map/ppermute | solution.py:24
  159.8 11.6 %collective-permute-start.53 = (bf16[128,1024]{1,0:T(8,128)(2,1)S(1)}, bf16[128,1024]{1,0:T(8,128)(2,1)S(1)}, u32[]{:S(2)}, u32[]{:S(2)}) collective-permute-start(bf16[128,1024]{1,0:T(8,128)(2,1)S(1)} %get-tuple-element.210), channel_id=1, source_target_pairs={{0,2},{1,3},{2,0},{3,1},{4,6},{5,7},{6,4},{7,5},{8,10},{9,11},{10,... | collective-permute-start | bytes 786440 | tf_op jit(solution)/shard_map/ppermute | solution.py:24
  161.5 10.5 %collective-permute-start.55 = (bf16[128,1024]{1,0:T(8,128)(2,1)S(1)}, bf16[128,1024]{1,0:T(8,128)(2,1)S(1)}, u32[]{:S(2)}, u32[]{:S(2)}) collective-permute-start(bf16[128,1024]{1,0:T(8,128)(2,1)S(1)} %add_convert_fusion.5), channel_id=1, source_target_pairs={{0,4},{1,5},{2,6},{3,7},{4,0},{5,1},{6,2},{7,3},{8,12},{9,13},{10,... | collective-permute-start | bytes 786440 | tf_op jit(solution)/shard_map/ppermute | solution.py:24
  163.1 10.5 %collective-permute-start.56 = (bf16[128,1024]{1,0:T(8,128)(2,1)S(1)}, bf16[128,1024]{1,0:T(8,128)(2,1)S(1)}, u32[]{:S(2)}, u32[]{:S(2)}) collective-permute-start(bf16[128,1024]{1,0:T(8,128)(2,1)S(1)} %add_convert_fusion.4), channel_id=1, source_target_pairs={{0,4},{1,5},{2,6},{3,7},{4,0},{5,1},{6,2},{7,3},{8,12},{9,13},{10,... | collective-permute-start | bytes 786440 | tf_op jit(solution)/shard_map/ppermute | solution.py:24
  164.3 12.0 %collective-permute-start.52 = (bf16[128,1024]{1,0:T(8,128)(2,1)S(1)}, bf16[128,1024]{1,0:T(8,128)(2,1)S(1)}, u32[]{:S(2)}, u32[]{:S(2)}) collective-permute-start(bf16[128,1024]{1,0:T(8,128)(2,1)S(1)} %get-tuple-element.215), channel_id=1, source_target_pairs={{0,2},{1,3},{2,0},{3,1},{4,6},{5,7},{6,4},{7,5},{8,10},{9,11},{10,... | collective-permute-start | bytes 786440 | tf_op jit(solution)/shard_map/ppermute | solution.py:24
  171.9 9.6 %collective-permute-start.63 = (bf16[128,1024]{1,0:T(8,128)(2,1)S(1)}, bf16[128,1024]{1,0:T(8,128)(2,1)S(1)}, u32[]{:S(2)}, u32[]{:S(2)}) collective-permute-start(bf16[128,1024]{1,0:T(8,128)(2,1)S(1)} %get-tuple-element.230), channel_id=1, source_target_pairs={{0,2},{1,3},{2,0},{3,1},{4,6},{5,7},{6,4},{7,5},{8,10},{9,11},{10,... | collective-permute-start | bytes 786440 | tf_op jit(solution)/shard_map/ppermute | solution.py:24
  173.6 15.1 %collective-permute-start.62 = (bf16[128,1024]{1,0:T(8,128)(2,1)S(1)}, bf16[128,1024]{1,0:T(8,128)(2,1)S(1)}, u32[]{:S(2)}, u32[]{:S(2)}) collective-permute-start(bf16[128,1024]{1,0:T(8,128)(2,1)S(1)} %add_convert_fusion.3), channel_id=1, source_target_pairs={{0,8},{1,9},{2,10},{3,11},{4,12},{5,13},{6,14},{7,15},{8,0},{9,1},... | collective-permute-start | bytes 786440 | tf_op jit(solution)/shard_map/ppermute | solution.py:24
  176.3 12.4 %collective-permute-start.61 = (bf16[72,2048]{1,0:T(8,128)(2,1)S(1)}, bf16[72,2048]{1,0:T(8,128)(2,1)S(1)}, u32[]{:S(2)}, u32[]{:S(2)}) collective-permute-start(bf16[72,2048]{1,0:T(8,128)(2,1)S(1)} %get-tuple-element.222), channel_id=1, source_target_pairs={{0,1},{1,0},{2,3},{3,2},{4,5},{5,4},{6,7},{7,6},{8,9},{9,8},{10,11... | collective-permute-start | bytes 884744 | tf_op jit(solution)/shard_map/ppermute | solution.py:24
  178.5 13.6 %collective-permute-start.60 = (bf16[128,1024]{1,0:T(8,128)(2,1)S(1)}, bf16[128,1024]{1,0:T(8,128)(2,1)S(1)}, u32[]{:S(2)}, u32[]{:S(2)}) collective-permute-start(bf16[128,1024]{1,0:T(8,128)(2,1)S(1)} %add_convert_fusion.2), channel_id=1, source_target_pairs={{0,8},{1,9},{2,10},{3,11},{4,12},{5,13},{6,14},{7,15},{8,0},{9,1},... | collective-permute-start | bytes 786440 | tf_op jit(solution)/shard_map/ppermute | solution.py:24
  180.3 15.1 %collective-permute-start.57 = (bf16[72,2048]{1,0:T(8,128)(2,1)S(1)}, bf16[72,2048]{1,0:T(8,128)(2,1)S(1)}, u32[]{:S(2)}, u32[]{:S(2)}) collective-permute-start(bf16[72,2048]{1,0:T(8,128)(2,1)S(1)} %get-tuple-element.227), channel_id=1, source_target_pairs={{0,1},{1,0},{2,3},{3,2},{4,5},{5,4},{6,7},{7,6},{8,9},{9,8},{10,11... | collective-permute-start | bytes 884744 | tf_op jit(solution)/shard_map/ppermute | solution.py:24
  181.6 13.9 %collective-permute-start.59 = (bf16[128,1024]{1,0:T(8,128)(2,1)S(1)}, bf16[128,1024]{1,0:T(8,128)(2,1)S(1)}, u32[]{:S(2)}, u32[]{:S(2)}) collective-permute-start(bf16[128,1024]{1,0:T(8,128)(2,1)S(1)} %add_convert_fusion.1), channel_id=1, source_target_pairs={{0,4},{1,5},{2,6},{3,7},{4,0},{5,1},{6,2},{7,3},{8,12},{9,13},{10,... | collective-permute-start | bytes 786440 | tf_op jit(solution)/shard_map/ppermute | solution.py:24
  188.7 9.5 %collective-permute-start.64 = (bf16[128,1024]{1,0:T(8,128)(2,1)S(1)}, bf16[128,1024]{1,0:T(8,128)(2,1)S(1)}, u32[]{:S(2)}, u32[]{:S(2)}) collective-permute-start(bf16[128,1024]{1,0:T(8,128)(2,1)S(1)} %add_convert_fusion), channel_id=1, source_target_pairs={{0,4},{1,5},{2,6},{3,7},{4,0},{5,1},{6,2},{7,3},{8,12},{9,13},{10,... | collective-permute-start | bytes 786440 | tf_op jit(solution)/shard_map/ppermute | solution.py:24
  (28 other events, 305.0 us)

commit v3 on v2

--- a/solution.py
+++ b/solution.py
@@ -141,12 +141,12 @@
     (5, 1),
     (3, 2),
     (None, 4),
+    (13, 1),
     (14, 2),
-    (13, 1),
     (None, 8),
+    (11, 1),
     (6, 2),
     (15, 1),
-    (11, 1),
     (7, 2),
 )
 
@@ -576,9 +576,9 @@
         sibling = swapped(given, "ctx", 1)
         planes, picks, masks = weight_planes(out_proj, picks, masks, given)
         given_sum, own_sum = product([sibling, kept], planes, rows)
-        picks, masks = doubled(picks, masks, 1)
-        heard_sum = after(swapped(given_sum, "ctx", 1), picks)
-        picks, masks = doubled(picks, masks, 2)
+        heard_sum = swapped(given_sum, "ctx", 1)
+        picks = jnp.concatenate([picks] + [swapped(picks, "ep", m) for m in (1, 2, 3)], axis=0)
+        masks = [mask | m for m in range(4) for mask in masks]
     else:
         picks, masks = all_picks(picks, masks, [1 << k for k in range(ep_count.bit_length() - 1)])
         full = lax.all_gather(out_proj, ("ctx", "ep"), axis=0, tiled=True)

time: 201 us -> 197 us (0.980)
  starting transfers between devices: 76.4 us -> 73.6 us
    ppermute x65 -> x66, starting transfers between devices: 76.3 us -> 73.4 us  [swapped(): return lax.ppermute(shard, axis, [(i, i ^ mask) for i in range(devices)])]
    ppermute x65 -> x66, waiting for transfers between devices: 86.5 us -> 86.2 us  [swapped(): return lax.ppermute(shard, axis, [(i, i ^ mask) for i in range(devices)])]
  transfers between devices with their start and end apart: 67 -> 68, of which waited for: 37 -> 39; matrix products, arithmetic and copies ran while one was open for 1% -> 1% of each run, Pallas kernels for 12% -> 12%
where the time goes in v3:
time: 197 us
  waiting for transfers between devices  88.8 us (45%)
  starting transfers between devices  73.6 us (37%)
  Pallas kernels  27.9 us (14%)
  local copies, waits for them, and re-layouts  3.8 us (2%)
  other arithmetic  2.05 us (1%)
    ppermute x66, waiting for transfers between devices, swapped(): return lax.ppermute(shard, axis, [(i, i ^ mask) for i in range(devices)])  86.2 us
    ppermute x66, starting transfers between devices, swapped(): return lax.ppermute(shard, axis, [(i, i ^ mask) for i in range(devices)])  73.4 us
    pallas_call x22, Pallas kernels, local(): pl.pallas_call(kernel, out_shape=out_shape, in_specs=[WHOLE] * len(operan...  22.1 us
  transfers between devices with their start and end apart: 68, of which 39 were waited for; matrix products, arithmetic and copies ran while one was open for 1% of the time, Pallas kernels for 12%

profile of v3, /device:TPU:0, one launch (start us, length us, event | category | flops | bytes accessed | tf_op | source)
XLA Modules:
  0.0 197.1 jit_solution(2795953589664172022)
XLA Ops:
  0.6 4.1 %collective-permute-start.5 = (bf16[64,2048]{1,0:T(8,128)(2,1)}, bf16[64,2048]{1,0:T(8,128)(2,1)S(1)}, u32[]{:S(2)}, u32[]{:S(2)}) collective-permute-start(bf16[64,2048]{1,0:T(8,128)(2,1)} %refs_2_.1), channel_id=1, source_target_pairs={{0,8},{1,9},{2,10},{3,11},{4,12},{5,13},{6,14},{7,15},{8,0},{9,1},... | collective-permute-start | bytes 786440 | tf_op jit(solution)/shard_map/ppermute | solution.py:24
  4.7 1.5 collective-permute-start.4
  6.3 1.5 collective-permute-start.3
  7.7 1.6 collective-permute-start.7
  15.0 3.4 %shard_map.131 = (bf16[128,2048]{1,0:T(8,128)(2,1)}, bf16[128,1024]{1,0:T(8,128)(2,1)S(1)}, bf16[128,1024]{1,0:T(8,128)(2,1)S(1)}) custom-call(s32[2]{0:T(128)S(1)} %pad_add_fusion.here, bf16[128,2048]{1,0:T(8,128)(2,1)S(1)} %copy-done.2, bf16[128,256]{1,0:T(8,128)(2,1)S(1)} %collective-permute-done.keys, ...), custom_call_target="tpu_custom_call" | custom-call | tf_op jit(solution)/shard_map/pallas_call | solution.py:123
  22.2 1.5 collective-permute-start.8
  24.4 3.2 %collective-permute-done.11.refs_11_ = bf16[64,2048]{1,0:T(8,128)(2,1)S(1)} collective-permute-done((bf16[64,2048]{1,0:T(8,128)(2,1)S(1)}, bf16[64,2048]{1,0:T(8,128)(2,1)S(1)}, u32[]{:S(2)}, u32[]{:S(2)}) %collective-permute-start.11) | collective-permute-done | bytes 262176 | tf_op jit(solution)/shard_map/ppermute | solution.py:24
  28.6 2.7 %collective-permute-done.14 = f32[1,16,128]{2,1,0:T(8,128)S(1)} collective-permute-done((f32[1,16,128]{2,1,0:T(8,128)S(1)}, f32[1,16,128]{2,1,0:T(8,128)S(1)}, u32[]{:S(2)}, u32[]{:S(2)}) %collective-permute-start.14) | collective-permute-done | bytes 8224 | tf_op jit(solution)/shard_map/ppermute | solution.py:24
  31.8 1.5 collective-permute-done.8.refs_7_
  33.2 1.8 collective-permute-done.6.refs_5_
  35.0 3.1 %collective-permute-start.15 = (f32[2,16,128]{2,1,0:T(8,128)S(1)}, f32[2,16,128]{2,1,0:T(8,128)S(1)}, u32[]{:S(2)}, u32[]{:S(2)}) collective-permute-start(f32[2,16,128]{2,1,0:T(8,128)S(1)} %pad_maximum_fusion.2), channel_id=1, source_target_pairs={{0,8},{1,9},{2,10},{3,11},{4,12},{5,13},{6,14},{7,15},{8,0},{9,1},... | collective-permute-start | bytes 49160 | tf_op jit(solution)/shard_map/ppermute | solution.py:24
  38.7 1.5 collective-permute-start.12
  40.6 1.5 collective-permute-start.19
  42.2 4.3 %collective-permute-done.13.refs_13_ = bf16[64,2048]{1,0:T(8,128)(2,1)S(1)} collective-permute-done((bf16[64,2048]{1,0:T(8,128)(2,1)S(1)}, bf16[64,2048]{1,0:T(8,128)(2,1)S(1)}, u32[]{:S(2)}, u32[]{:S(2)}) %collective-permute-start.13) | collective-permute-done | bytes 262176 | tf_op jit(solution)/shard_map/ppermute | solution.py:24
  47.6 1.7 collective-permute-done.19.refs_17_
  51.4 2.0 %shard_map.132 = (f32[128,2048]{1,0:T(8,128)S(1)}, f32[128,2048]{1,0:T(8,128)S(1)}) custom-call(bf16[128,1024]{1,0:T(8,128)(2,1)S(1)} %collective-permute-done.2.refs_0_, bf16[128,1024]{1,0:T(8,128)(2,1)S(1)} %get-tuple-element.122.refs_1_, bf16[64,2048]{1,0:T(8,128)(2,1)S(1)} %copy-done.4, bf16[64,2048]{1,0:T(8,128)(2,1)S(1)} %collective-permute-done.3.refs_3_, ...), custom_call_target="tpu_custom_call" | custom-call | tf_op jit(solution)/shard_map/pallas_call | solution.py:206
  53.5 1.5 collective-permute-start.23
  55.0 1.5 collective-permute-start.22
  58.9 1.5 collective-permute-done.21
  61.8 1.5 collective-permute-start.27
  63.3 1.6 collective-permute-start.25
  65.5 1.7 collective-permute-start.34
  67.3 3.2 %collective-permute-done.26.left.refs_2_ = bf16[128,1024]{1,0:T(8,128)(2,1)S(1)} collective-permute-done((bf16[128,1024]{1,0:T(8,128)(2,1)S(1)}, bf16[128,1024]{1,0:T(8,128)(2,1)S(1)}, u32[]{:S(2)}, u32[]{:S(2)}) %collective-permute-start.26) | collective-permute-done | bytes 262176 | tf_op jit(solution)/shard_map/ppermute | solution.py:24
  70.5 2.0 collective-permute-start.33
  74.1 5.3 %collective-permute-done.25.left.refs_0_ = bf16[128,1024]{1,0:T(8,128)(2,1)S(1)} collective-permute-done((bf16[128,1024]{1,0:T(8,128)(2,1)S(1)}, bf16[128,1024]{1,0:T(8,128)(2,1)S(1)}, u32[]{:S(2)}, u32[]{:S(2)}) %collective-permute-start.25) | collective-permute-done | bytes 262176 | tf_op jit(solution)/shard_map/ppermute | solution.py:24
  80.2 1.5 collective-permute-start.30
  83.1 5.8 %collective-permute-done.34.right.refs_1_ = bf16[128,1024]{1,0:T(8,128)(2,1)S(1)} collective-permute-done((bf16[128,1024]{1,0:T(8,128)(2,1)S(1)}, bf16[128,1024]{1,0:T(8,128)(2,1)S(1)}, u32[]{:S(2)}, u32[]{:S(2)}) %collective-permute-start.34) | collective-permute-done | bytes 262176 | tf_op jit(solution)/shard_map/ppermute | solution.py:24
  90.5 1.6 collective-permute-done.29.left.refs_0_
  92.9 1.6 collective-permute-start.37
  97.2 1.6 collective-permute-done.38.right.refs_3_
  99.7 4.8 %collective-permute-done.28.left.refs_2_ = bf16[128,1024]{1,0:T(8,128)(2,1)S(1)} collective-permute-done((bf16[128,1024]{1,0:T(8,128)(2,1)S(1)}, bf16[128,1024]{1,0:T(8,128)(2,1)S(1)}, u32[]{:S(2)}, u32[]{:S(2)}) %collective-permute-start.28) | collective-permute-done | bytes 262176 | tf_op jit(solution)/shard_map/ppermute | solution.py:24
  106.8 3.3 %collective-permute-done.36.left.refs_2_ = bf16[128,1024]{1,0:T(8,128)(2,1)S(1)} collective-permute-done((bf16[128,1024]{1,0:T(8,128)(2,1)S(1)}, bf16[128,1024]{1,0:T(8,128)(2,1)S(1)}, u32[]{:S(2)}, u32[]{:S(2)}) %collective-permute-start.36) | collective-permute-done | bytes 262176 | tf_op jit(solution)/shard_map/ppermute | solution.py:24
  111.3 3.7 %collective-permute-done.35.right.refs_3_ = bf16[128,1024]{1,0:T(8,128)(2,1)S(1)} collective-permute-done((bf16[128,1024]{1,0:T(8,128)(2,1)S(1)}, bf16[128,1024]{1,0:T(8,128)(2,1)S(1)}, u32[]{:S(2)}, u32[]{:S(2)}) %collective-permute-start.35) | collective-permute-done | bytes 262176 | tf_op jit(solution)/shard_map/ppermute | solution.py:24
  120.5 4.7 %collective-permute-done.39.refs_5_ = bf16[72,2048]{1,0:T(8,128)(2,1)S(1)} collective-permute-done((bf16[72,2048]{1,0:T(8,128)(2,1)S(1)}, bf16[72,2048]{1,0:T(8,128)(2,1)S(1)}, u32[]{:S(2)}, u32[]{:S(2)}) %collective-permute-start.39) | collective-permute-done | bytes 294944 | tf_op jit(solution)/shard_map/ppermute | solution.py:24
  125.2 4.0 %shard_map.143 = (f32[256,2048]{1,0:T(8,128)S(1)}, bf16[72,2048]{1,0:T(8,128)(2,1)S(1)}, bf16[72,2048]{1,0:T(8,128)(2,1)S(1)}) custom-call(bf16[128,1024]{1,0:T(8,128)(2,1)S(1)} %get-tuple-element.177.left.refs_0_, bf16[128,1024]{1,0:T(8,128)(2,1)S(1)} %get-tuple-element.150.right.refs_1_, bf16[128,1024]{1,0:T(8,128)(2,1)S(1)} %collective-permute-done.26.left.refs_2_, ...), custom_call_target="tpu_custom_call" | custom-call | tf_op jit(solution)/shard_map/pallas_call | solution.py:40
  130.6 4.0 %shard_map.144 = (f32[256,2048]{1,0:T(8,128)S(1)}, bf16[72,2048]{1,0:T(8,128)(2,1)S(1)}, bf16[72,2048]{1,0:T(8,128)(2,1)S(1)}) custom-call(bf16[128,1024]{1,0:T(8,128)(2,1)S(1)} %collective-permute-done.29.left.refs_0_, bf16[128,1024]{1,0:T(8,128)(2,1)S(1)} %collective-permute-done.37.right.refs_1_, ...), custom_call_target="tpu_custom_call" | custom-call | tf_op jit(solution)/shard_map/pallas_call | solution.py:40
  137.1 4.2 %shard_map.145 = (f32[256,2048]{1,0:T(8,128)S(1)}, bf16[72,2048]{1,0:T(8,128)(2,1)S(1)}, bf16[72,2048]{1,0:T(8,128)(2,1)S(1)}) custom-call(bf16[128,1024]{1,0:T(8,128)(2,1)S(1)} %collective-permute-done.24.left.refs_0_, bf16[128,1024]{1,0:T(8,128)(2,1)S(1)} %collective-permute-done.33.right.refs_1_, ...), custom_call_target="tpu_custom_call" | custom-call | tf_op jit(solution)/shard_map/pallas_call | solution.py:40
  142.6 2.5 %collective-permute-done.46.returned = bf16[72,2048]{1,0:T(8,128)(2,1)S(1)} collective-permute-done((bf16[72,2048]{1,0:T(8,128)(2,1)S(1)}, bf16[72,2048]{1,0:T(8,128)(2,1)S(1)}, u32[]{:S(2)}, u32[]{:S(2)}) %collective-permute-start.46) | collective-permute-done | bytes 294944 | tf_op jit(solution)/shard_map/ppermute | solution.py:24
  148.6 4.0 %shard_map.147 = (f32[256,2048]{1,0:T(8,128)S(1)}, bf16[72,2048]{1,0:T(8,128)(2,1)S(1)}, bf16[72,2048]{1,0:T(8,128)(2,1)S(1)}) custom-call(bf16[128,1024]{1,0:T(8,128)(2,1)S(1)} %collective-permute-done.25.left.refs_0_, bf16[128,1024]{1,0:T(8,128)(2,1)S(1)} %collective-permute-done.34.right.refs_1_, ...), custom_call_target="tpu_custom_call" | custom-call | tf_op jit(solution)/shard_map/pallas_call | solution.py:40
  153.9 3.8 %collective-permute-done.52.returned = bf16[72,2048]{1,0:T(8,128)(2,1)S(1)} collective-permute-done((bf16[72,2048]{1,0:T(8,128)(2,1)S(1)}, bf16[72,2048]{1,0:T(8,128)(2,1)S(1)}, u32[]{:S(2)}, u32[]{:S(2)}) %collective-permute-start.52) | collective-permute-done | bytes 294944 | tf_op jit(solution)/shard_map/ppermute | solution.py:24
  158.7 2.1 %collective-permute-start.56 = (bf16[128,1024]{1,0:T(8,128)(2,1)S(1)}, bf16[128,1024]{1,0:T(8,128)(2,1)S(1)}, u32[]{:S(2)}, u32[]{:S(2)}) collective-permute-start(bf16[128,1024]{1,0:T(8,128)(2,1)S(1)} %add_convert_fusion.5), channel_id=1, source_target_pairs={{0,4},{1,5},{2,6},{3,7},{4,0},{5,1},{6,2},{7,3},{8,12},{9,13},{10,... | collective-permute-start | bytes 786440 | tf_op jit(solution)/shard_map/ppermute | solution.py:24
  163.4 4.1 %collective-permute-done.55.returned = bf16[72,2048]{1,0:T(8,128)(2,1)S(1)} collective-permute-done((bf16[72,2048]{1,0:T(8,128)(2,1)S(1)}, bf16[72,2048]{1,0:T(8,128)(2,1)S(1)}, u32[]{:S(2)}, u32[]{:S(2)}) %collective-permute-start.55) | collective-permute-done | bytes 294944 | tf_op jit(solution)/shard_map/ppermute | solution.py:24
  171.2 4.0 %collective-permute-start.63 = (bf16[128,1024]{1,0:T(8,128)(2,1)S(1)}, bf16[128,1024]{1,0:T(8,128)(2,1)S(1)}, u32[]{:S(2)}, u32[]{:S(2)}) collective-permute-start(bf16[128,1024]{1,0:T(8,128)(2,1)S(1)} %add_convert_fusion.3), channel_id=1, source_target_pairs={{0,8},{1,9},{2,10},{3,11},{4,12},{5,13},{6,14},{7,15},{8,0},{9,1},... | collective-permute-start | bytes 786440 | tf_op jit(solution)/shard_map/ppermute | solution.py:24
  176.0 4.6 %collective-permute-start.61 = (bf16[128,1024]{1,0:T(8,128)(2,1)S(1)}, bf16[128,1024]{1,0:T(8,128)(2,1)S(1)}, u32[]{:S(2)}, u32[]{:S(2)}) collective-permute-start(bf16[128,1024]{1,0:T(8,128)(2,1)S(1)} %add_convert_fusion.2), channel_id=1, source_target_pairs={{0,8},{1,9},{2,10},{3,11},{4,12},{5,13},{6,14},{7,15},{8,0},{9,1},... | collective-permute-start | bytes 786440 | tf_op jit(solution)/shard_map/ppermute | solution.py:24
  181.3 5.1 %collective-permute-done.63.refs_2_ = bf16[128,1024]{1,0:T(8,128)(2,1)S(1)} collective-permute-done((bf16[128,1024]{1,0:T(8,128)(2,1)S(1)}, bf16[128,1024]{1,0:T(8,128)(2,1)S(1)}, u32[]{:S(2)}, u32[]{:S(2)}) %collective-permute-start.63) | collective-permute-done | bytes 262176 | tf_op jit(solution)/shard_map/ppermute | solution.py:24
  187.2 2.5 %collective-permute-done.61.refs_3_ = bf16[128,1024]{1,0:T(8,128)(2,1)S(1)} collective-permute-done((bf16[128,1024]{1,0:T(8,128)(2,1)S(1)}, bf16[128,1024]{1,0:T(8,128)(2,1)S(1)}, u32[]{:S(2)}, u32[]{:S(2)}) %collective-permute-start.61) | collective-permute-done | bytes 262176 | tf_op jit(solution)/shard_map/ppermute | solution.py:24
  192.0 2.5 %collective-permute-done.65.refs_5_ = bf16[128,1024]{1,0:T(8,128)(2,1)S(1)} collective-permute-done((bf16[128,1024]{1,0:T(8,128)(2,1)S(1)}, bf16[128,1024]{1,0:T(8,128)(2,1)S(1)}, u32[]{:S(2)}, u32[]{:S(2)}) %collective-permute-start.65) | collective-permute-done | bytes 262176 | tf_op jit(solution)/shard_map/ppermute | solution.py:24
  194.4 1.6 collective-permute-done.66.refs_6_
  (148 shorter events, 61.7 us)
Async XLA Ops:
  0.6 17.8 %collective-permute-start.5 = (bf16[64,2048]{1,0:T(8,128)(2,1)}, bf16[64,2048]{1,0:T(8,128)(2,1)S(1)}, u32[]{:S(2)}, u32[]{:S(2)}) collective-permute-start(bf16[64,2048]{1,0:T(8,128)(2,1)} %refs_2_.1), channel_id=1, source_target_pairs={{0,8},{1,9},{2,10},{3,11},{4,12},{5,13},{6,14},{7,15},{8,0},{9,1},... | collective-permute-start | bytes 786440 | tf_op jit(solution)/shard_map/ppermute | solution.py:24
  4.7 15.4 %collective-permute-start.4 = (bf16[64,2048]{1,0:T(8,128)(2,1)}, bf16[64,2048]{1,0:T(8,128)(2,1)S(1)}, u32[]{:S(2)}, u32[]{:S(2)}) collective-permute-start(bf16[64,2048]{1,0:T(8,128)(2,1)} %refs_2_.1), channel_id=1, source_target_pairs={{0,2},{1,3},{2,0},{3,1},{4,6},{5,7},{6,4},{7,5},{8,10},{9,11},{10,... | collective-permute-start | bytes 786440 | tf_op jit(solution)/shard_map/ppermute | solution.py:24
  6.3 15.1 %collective-permute-start.3 = (bf16[64,2048]{1,0:T(8,128)(2,1)}, bf16[64,2048]{1,0:T(8,128)(2,1)S(1)}, u32[]{:S(2)}, u32[]{:S(2)}) collective-permute-start(bf16[64,2048]{1,0:T(8,128)(2,1)} %refs_2_.1), channel_id=1, source_target_pairs={{0,1},{1,0},{2,3},{3,2},{4,5},{5,4},{6,7},{7,6},{8,9},{9,8},{10,11... | collective-permute-start | bytes 786440 | tf_op jit(solution)/shard_map/ppermute | solution.py:24
  7.7 14.4 %collective-permute-start.7 = (bf16[64,2048]{1,0:T(8,128)(2,1)}, bf16[64,2048]{1,0:T(8,128)(2,1)S(1)}, u32[]{:S(2)}, u32[]{:S(2)}) collective-permute-start(bf16[64,2048]{1,0:T(8,128)(2,1)} %refs_2_.1), channel_id=1, source_target_pairs={{0,4},{1,5},{2,6},{3,7},{4,0},{5,1},{6,2},{7,3},{8,12},{9,13},{10,... | collective-permute-start | bytes 786440 | tf_op jit(solution)/shard_map/ppermute | solution.py:24
  18.4 9.2 %collective-permute-start.11 = (bf16[64,2048]{1,0:T(8,128)(2,1)S(1)}, bf16[64,2048]{1,0:T(8,128)(2,1)S(1)}, u32[]{:S(2)}, u32[]{:S(2)}) collective-permute-start(bf16[64,2048]{1,0:T(8,128)(2,1)S(1)} %collective-permute-done.5.refs_10_), channel_id=1, source_target_pairs={{0,1},{1,0},{2,3},{3,2},{4,5},{5,4},{6,7},{7,6},{8,9},{9,8},{10,11... | collective-permute-start | bytes 786440 | tf_op jit(solution)/shard_map/ppermute | solution.py:24
  20.1 11.6 %collective-permute-start.9 = (bf16[64,2048]{1,0:T(8,128)(2,1)S(1)}, bf16[64,2048]{1,0:T(8,128)(2,1)S(1)}, u32[]{:S(2)}, u32[]{:S(2)}) collective-permute-start(bf16[64,2048]{1,0:T(8,128)(2,1)S(1)} %collective-permute-done.5.refs_10_), channel_id=1, source_target_pairs={{0,2},{1,3},{2,0},{3,1},{4,6},{5,7},{6,4},{7,5},{8,10},{9,11},{10,... | collective-permute-start | bytes 786440 | tf_op jit(solution)/shard_map/ppermute | solution.py:24
  21.4 13.6 %collective-permute-start.6 = (bf16[64,2048]{1,0:T(8,128)(2,1)S(1)}, bf16[64,2048]{1,0:T(8,128)(2,1)S(1)}, u32[]{:S(2)}, u32[]{:S(2)}) collective-permute-start(bf16[64,2048]{1,0:T(8,128)(2,1)S(1)} %collective-permute-done.3.refs_3_), channel_id=1, source_target_pairs={{0,2},{1,3},{2,0},{3,1},{4,6},{5,7},{6,4},{7,5},{8,10},{9,11},{10,... | collective-permute-start | bytes 786440 | tf_op jit(solution)/shard_map/ppermute | solution.py:24
  22.2 11.1 %collective-permute-start.8 = (bf16[64,2048]{1,0:T(8,128)(2,1)S(1)}, bf16[64,2048]{1,0:T(8,128)(2,1)S(1)}, u32[]{:S(2)}, u32[]{:S(2)}) collective-permute-start(bf16[64,2048]{1,0:T(8,128)(2,1)S(1)} %collective-permute-done.7.refs_6_), channel_id=1, source_target_pairs={{0,1},{1,0},{2,3},{3,2},{4,5},{5,4},{6,7},{7,6},{8,9},{9,8},{10,11... | collective-permute-start | bytes 786440 | tf_op jit(solution)/shard_map/ppermute | solution.py:24
  28.1 12.1 %collective-permute-start.17 = (bf16[64,2048]{1,0:T(8,128)(2,1)S(1)}, bf16[64,2048]{1,0:T(8,128)(2,1)S(1)}, u32[]{:S(2)}, u32[]{:S(2)}) collective-permute-start(bf16[64,2048]{1,0:T(8,128)(2,1)S(1)} %collective-permute-done.10.refs_14_), channel_id=1, source_target_pairs={{0,1},{1,0},{2,3},{3,2},{4,5},{5,4},{6,7},{7,6},{8,9},{9,8},{10,11... | collective-permute-start | bytes 786440 | tf_op jit(solution)/shard_map/ppermute | solution.py:24
  31.3 9.3 %collective-permute-start.16 = (bf16[64,2048]{1,0:T(8,128)(2,1)S(1)}, bf16[64,2048]{1,0:T(8,128)(2,1)S(1)}, u32[]{:S(2)}, u32[]{:S(2)}) collective-permute-start(bf16[64,2048]{1,0:T(8,128)(2,1)S(1)} %collective-permute-done.10.refs_14_), channel_id=1, source_target_pairs={{0,2},{1,3},{2,0},{3,1},{4,6},{5,7},{6,4},{7,5},{8,10},{9,11},{10,... | collective-permute-start | bytes 786440 | tf_op jit(solution)/shard_map/ppermute | solution.py:24
  61.2 9.3 %collective-permute-start.26 = (bf16[128,1024]{1,0:T(8,128)(2,1)S(1)}, bf16[128,1024]{1,0:T(8,128)(2,1)S(1)}, u32[]{:S(2)}, u32[]{:S(2)}) collective-permute-start(bf16[128,1024]{1,0:T(8,128)(2,1)S(1)} %get-tuple-element.177.left.refs_0_), channel_id=1, source_target_pairs={{0,2},{1,3},{2,0},{3,1},{4,6},{5,7},{6,4},{7,5},{8,10},{9,11},{10,... | collective-permute-start | bytes 786440 | tf_op jit(solution)/shard_map/ppermute | solution.py:24
  61.8 12.1 %collective-permute-start.27 = (bf16[128,1024]{1,0:T(8,128)(2,1)S(1)}, bf16[128,1024]{1,0:T(8,128)(2,1)S(1)}, u32[]{:S(2)}, u32[]{:S(2)}) collective-permute-start(bf16[128,1024]{1,0:T(8,128)(2,1)S(1)} %get-tuple-element.150.right.refs_1_), channel_id=1, source_target_pairs={{0,2},{1,3},{2,0},{3,1},{4,6},{5,7},{6,4},{7,5},{8,10},{9,11},{10,... | collective-permute-start | bytes 786440 | tf_op jit(solution)/shard_map/ppermute | solution.py:24
  63.3 16.1 %collective-permute-start.25 = (bf16[128,1024]{1,0:T(8,128)(2,1)S(1)}, bf16[128,1024]{1,0:T(8,128)(2,1)S(1)}, u32[]{:S(2)}, u32[]{:S(2)}) collective-permute-start(bf16[128,1024]{1,0:T(8,128)(2,1)S(1)} %get-tuple-element.177.left.refs_0_), channel_id=1, source_target_pairs={{0,4},{1,5},{2,6},{3,7},{4,0},{5,1},{6,2},{7,3},{8,12},{9,13},{10,... | collective-permute-start | bytes 786440 | tf_op jit(solution)/shard_map/ppermute | solution.py:24
  64.9 15.3 %collective-permute-start.24 = (bf16[128,1024]{1,0:T(8,128)(2,1)S(1)}, bf16[128,1024]{1,0:T(8,128)(2,1)S(1)}, u32[]{:S(2)}, u32[]{:S(2)}) collective-permute-start(bf16[128,1024]{1,0:T(8,128)(2,1)S(1)} %get-tuple-element.177.left.refs_0_), channel_id=1, source_target_pairs={{0,8},{1,9},{2,10},{3,11},{4,12},{5,13},{6,14},{7,15},{8,0},{9,1},... | collective-permute-start | bytes 786440 | tf_op jit(solution)/shard_map/ppermute | solution.py:24
  65.5 23.3 %collective-permute-start.34 = (bf16[128,1024]{1,0:T(8,128)(2,1)S(1)}, bf16[128,1024]{1,0:T(8,128)(2,1)S(1)}, u32[]{:S(2)}, u32[]{:S(2)}) collective-permute-start(bf16[128,1024]{1,0:T(8,128)(2,1)S(1)} %get-tuple-element.150.right.refs_1_), channel_id=1, source_target_pairs={{0,4},{1,5},{2,6},{3,7},{4,0},{5,1},{6,2},{7,3},{8,12},{9,13},{10,... | collective-permute-start | bytes 786440 | tf_op jit(solution)/shard_map/ppermute | solution.py:24
  70.5 19.2 %collective-permute-start.33 = (bf16[128,1024]{1,0:T(8,128)(2,1)S(1)}, bf16[128,1024]{1,0:T(8,128)(2,1)S(1)}, u32[]{:S(2)}, u32[]{:S(2)}) collective-permute-start(bf16[128,1024]{1,0:T(8,128)(2,1)S(1)} %get-tuple-element.150.right.refs_1_), channel_id=1, source_target_pairs={{0,8},{1,9},{2,10},{3,11},{4,12},{5,13},{6,14},{7,15},{8,0},{9,1},... | collective-permute-start | bytes 786440 | tf_op jit(solution)/shard_map/ppermute | solution.py:24
  80.2 12.0 %collective-permute-start.29 = (bf16[128,1024]{1,0:T(8,128)(2,1)S(1)}, bf16[128,1024]{1,0:T(8,128)(2,1)S(1)}, u32[]{:S(2)}, u32[]{:S(2)}) collective-permute-start(bf16[128,1024]{1,0:T(8,128)(2,1)S(1)} %collective-permute-done.24.left.refs_0_), channel_id=1, source_target_pairs={{0,4},{1,5},{2,6},{3,7},{4,0},{5,1},{6,2},{7,3},{8,12},{9,13},{10,... | collective-permute-start | bytes 786440 | tf_op jit(solution)/shard_map/ppermute | solution.py:24
  80.2 12.7 %collective-permute-start.30 = (bf16[128,1024]{1,0:T(8,128)(2,1)S(1)}, bf16[128,1024]{1,0:T(8,128)(2,1)S(1)}, u32[]{:S(2)}, u32[]{:S(2)}) collective-permute-start(bf16[128,1024]{1,0:T(8,128)(2,1)S(1)} %collective-permute-done.25.left.refs_0_), channel_id=1, source_target_pairs={{0,2},{1,3},{2,0},{3,1},{4,6},{5,7},{6,4},{7,5},{8,10},{9,11},{10,... | collective-permute-start | bytes 786440 | tf_op jit(solution)/shard_map/ppermute | solution.py:24
  81.6 12.9 %collective-permute-start.31 = (bf16[72,2048]{1,0:T(8,128)(2,1)S(1)}, bf16[72,2048]{1,0:T(8,128)(2,1)S(1)}, u32[]{:S(2)}, u32[]{:S(2)}) collective-permute-start(bf16[72,2048]{1,0:T(8,128)(2,1)S(1)} %shard_map.136), channel_id=1, source_target_pairs={{0,1},{1,0},{2,3},{3,2},{4,5},{5,4},{6,7},{7,6},{8,9},{9,8},{10,11... | collective-permute-start | bytes 884744 | tf_op jit(solution)/shard_map/ppermute | solution.py:24
  92.1 12.3 %collective-permute-start.28 = (bf16[128,1024]{1,0:T(8,128)(2,1)S(1)}, bf16[128,1024]{1,0:T(8,128)(2,1)S(1)}, u32[]{:S(2)}, u32[]{:S(2)}) collective-permute-start(bf16[128,1024]{1,0:T(8,128)(2,1)S(1)} %collective-permute-done.24.left.refs_0_), channel_id=1, source_target_pairs={{0,2},{1,3},{2,0},{3,1},{4,6},{5,7},{6,4},{7,5},{8,10},{9,11},{10,... | collective-permute-start | bytes 786440 | tf_op jit(solution)/shard_map/ppermute | solution.py:24
  92.9 12.4 %collective-permute-start.37 = (bf16[128,1024]{1,0:T(8,128)(2,1)S(1)}, bf16[128,1024]{1,0:T(8,128)(2,1)S(1)}, u32[]{:S(2)}, u32[]{:S(2)}) collective-permute-start(bf16[128,1024]{1,0:T(8,128)(2,1)S(1)} %collective-permute-done.33.right.refs_1_), channel_id=1, source_target_pairs={{0,4},{1,5},{2,6},{3,7},{4,0},{5,1},{6,2},{7,3},{8,12},{9,13},{10,... | collective-permute-start | bytes 786440 | tf_op jit(solution)/shard_map/ppermute | solution.py:24
  94.5 21.9 %collective-permute-start.43 = (bf16[72,2048]{1,0:T(8,128)(2,1)S(1)}, bf16[72,2048]{1,0:T(8,128)(2,1)S(1)}, u32[]{:S(2)}, u32[]{:S(2)}) collective-permute-start(bf16[72,2048]{1,0:T(8,128)(2,1)S(1)} %shard_map.137), channel_id=1, source_target_pairs={{0,1},{1,0},{2,3},{3,2},{4,5},{5,4},{6,7},{7,6},{8,9},{9,8},{10,11... | collective-permute-start | bytes 884744 | tf_op jit(solution)/shard_map/ppermute | solution.py:24
  97.2 19.2 %collective-permute-start.42 = (bf16[72,2048]{1,0:T(8,128)(2,1)S(1)}, bf16[72,2048]{1,0:T(8,128)(2,1)S(1)}, u32[]{:S(2)}, u32[]{:S(2)}) collective-permute-start(bf16[72,2048]{1,0:T(8,128)(2,1)S(1)} %shard_map.138), channel_id=1, source_target_pairs={{0,1},{1,0},{2,3},{3,2},{4,5},{5,4},{6,7},{7,6},{8,9},{9,8},{10,11... | collective-permute-start | bytes 884744 | tf_op jit(solution)/shard_map/ppermute | solution.py:24
  98.9 11.2 %collective-permute-start.36 = (bf16[128,1024]{1,0:T(8,128)(2,1)S(1)}, bf16[128,1024]{1,0:T(8,128)(2,1)S(1)}, u32[]{:S(2)}, u32[]{:S(2)}) collective-permute-start(bf16[128,1024]{1,0:T(8,128)(2,1)S(1)} %collective-permute-done.29.left.refs_0_), channel_id=1, source_target_pairs={{0,2},{1,3},{2,0},{3,1},{4,6},{5,7},{6,4},{7,5},{8,10},{9,11},{10,... | collective-permute-start | bytes 786440 | tf_op jit(solution)/shard_map/ppermute | solution.py:24
  104.5 10.5 %collective-permute-start.35 = (bf16[128,1024]{1,0:T(8,128)(2,1)S(1)}, bf16[128,1024]{1,0:T(8,128)(2,1)S(1)}, u32[]{:S(2)}, u32[]{:S(2)}) collective-permute-start(bf16[128,1024]{1,0:T(8,128)(2,1)S(1)} %collective-permute-done.33.right.refs_1_), channel_id=1, source_target_pairs={{0,2},{1,3},{2,0},{3,1},{4,6},{5,7},{6,4},{7,5},{8,10},{9,11},{10,... | collective-permute-start | bytes 786440 | tf_op jit(solution)/shard_map/ppermute | solution.py:24
  105.3 12.5 %collective-permute-start.41 = (bf16[128,1024]{1,0:T(8,128)(2,1)S(1)}, bf16[128,1024]{1,0:T(8,128)(2,1)S(1)}, u32[]{:S(2)}, u32[]{:S(2)}) collective-permute-start(bf16[128,1024]{1,0:T(8,128)(2,1)S(1)} %collective-permute-done.37.right.refs_1_), channel_id=1, source_target_pairs={{0,2},{1,3},{2,0},{3,1},{4,6},{5,7},{6,4},{7,5},{8,10},{9,11},{10,... | collective-permute-start | bytes 786440 | tf_op jit(solution)/shard_map/ppermute | solution.py:24
  110.1 10.4 %collective-permute-start.40 = (bf16[72,2048]{1,0:T(8,128)(2,1)S(1)}, bf16[72,2048]{1,0:T(8,128)(2,1)S(1)}, u32[]{:S(2)}, u32[]{:S(2)}) collective-permute-start(bf16[72,2048]{1,0:T(8,128)(2,1)S(1)} %shard_map.139), channel_id=1, source_target_pairs={{0,1},{1,0},{2,3},{3,2},{4,5},{5,4},{6,7},{7,6},{8,9},{9,8},{10,11... | collective-permute-start | bytes 884744 | tf_op jit(solution)/shard_map/ppermute | solution.py:24
  115.2 10.0 %collective-permute-start.39 = (bf16[72,2048]{1,0:T(8,128)(2,1)S(1)}, bf16[72,2048]{1,0:T(8,128)(2,1)S(1)}, u32[]{:S(2)}, u32[]{:S(2)}) collective-permute-start(bf16[72,2048]{1,0:T(8,128)(2,1)S(1)} %shard_map.140), channel_id=1, source_target_pairs={{0,1},{1,0},{2,3},{3,2},{4,5},{5,4},{6,7},{7,6},{8,9},{9,8},{10,11... | collective-permute-start | bytes 884744 | tf_op jit(solution)/shard_map/ppermute | solution.py:24
  118.0 12.6 %collective-permute-start.44 = (bf16[72,2048]{1,0:T(8,128)(2,1)S(1)}, bf16[72,2048]{1,0:T(8,128)(2,1)S(1)}, u32[]{:S(2)}, u32[]{:S(2)}) collective-permute-start(bf16[72,2048]{1,0:T(8,128)(2,1)S(1)} %shard_map.141), channel_id=1, source_target_pairs={{0,1},{1,0},{2,3},{3,2},{4,5},{5,4},{6,7},{7,6},{8,9},{9,8},{10,11... | collective-permute-start | bytes 884744 | tf_op jit(solution)/shard_map/ppermute | solution.py:24
  119.5 15.6 %collective-permute-start.45 = (bf16[72,2048]{1,0:T(8,128)(2,1)S(1)}, bf16[72,2048]{1,0:T(8,128)(2,1)S(1)}, u32[]{:S(2)}, u32[]{:S(2)}) collective-permute-start(bf16[72,2048]{1,0:T(8,128)(2,1)S(1)} %shard_map.142), channel_id=1, source_target_pairs={{0,1},{1,0},{2,3},{3,2},{4,5},{5,4},{6,7},{7,6},{8,9},{9,8},{10,11... | collective-permute-start | bytes 884744 | tf_op jit(solution)/shard_map/ppermute | solution.py:24
  135.1 9.9 %collective-permute-start.46 = (bf16[72,2048]{1,0:T(8,128)(2,1)S(1)}, bf16[72,2048]{1,0:T(8,128)(2,1)S(1)}, u32[]{:S(2)}, u32[]{:S(2)}) collective-permute-start(bf16[72,2048]{1,0:T(8,128)(2,1)S(1)} %get-tuple-element.187), channel_id=1, source_target_pairs={{0,1},{1,0},{2,3},{3,2},{4,5},{5,4},{6,7},{7,6},{8,9},{9,8},{10,11... | collective-permute-start | bytes 884744 | tf_op jit(solution)/shard_map/ppermute | solution.py:24
  136.2 16.4 %collective-permute-start.49 = (bf16[72,2048]{1,0:T(8,128)(2,1)S(1)}, bf16[72,2048]{1,0:T(8,128)(2,1)S(1)}, u32[]{:S(2)}, u32[]{:S(2)}) collective-permute-start(bf16[72,2048]{1,0:T(8,128)(2,1)S(1)} %get-tuple-element.188), channel_id=1, source_target_pairs={{0,1},{1,0},{2,3},{3,2},{4,5},{5,4},{6,7},{7,6},{8,9},{9,8},{10,11... | collective-permute-start | bytes 884744 | tf_op jit(solution)/shard_map/ppermute | solution.py:24
  141.4 16.3 %collective-permute-start.52 = (bf16[72,2048]{1,0:T(8,128)(2,1)S(1)}, bf16[72,2048]{1,0:T(8,128)(2,1)S(1)}, u32[]{:S(2)}, u32[]{:S(2)}) collective-permute-start(bf16[72,2048]{1,0:T(8,128)(2,1)S(1)} %get-tuple-element.192), channel_id=1, source_target_pairs={{0,1},{1,0},{2,3},{3,2},{4,5},{5,4},{6,7},{7,6},{8,9},{9,8},{10,11... | collective-permute-start | bytes 884744 | tf_op jit(solution)/shard_map/ppermute | solution.py:24
  145.4 13.3 %collective-permute-start.51 = (bf16[128,1024]{1,0:T(8,128)(2,1)S(1)}, bf16[128,1024]{1,0:T(8,128)(2,1)S(1)}, u32[]{:S(2)}, u32[]{:S(2)}) collective-permute-start(bf16[128,1024]{1,0:T(8,128)(2,1)S(1)} %get-tuple-element.195), channel_id=1, source_target_pairs={{0,2},{1,3},{2,0},{3,1},{4,6},{5,7},{6,4},{7,5},{8,10},{9,11},{10,... | collective-permute-start | bytes 786440 | tf_op jit(solution)/shard_map/ppermute | solution.py:24
  146.0 14.8 %collective-permute-start.50 = (bf16[128,1024]{1,0:T(8,128)(2,1)S(1)}, bf16[128,1024]{1,0:T(8,128)(2,1)S(1)}, u32[]{:S(2)}, u32[]{:S(2)}) collective-permute-start(bf16[128,1024]{1,0:T(8,128)(2,1)S(1)} %get-tuple-element.205), channel_id=1, source_target_pairs={{0,2},{1,3},{2,0},{3,1},{4,6},{5,7},{6,4},{7,5},{8,10},{9,11},{10,... | collective-permute-start | bytes 786440 | tf_op jit(solution)/shard_map/ppermute | solution.py:24
  147.5 14.7 %collective-permute-start.48 = (bf16[72,2048]{1,0:T(8,128)(2,1)S(1)}, bf16[72,2048]{1,0:T(8,128)(2,1)S(1)}, u32[]{:S(2)}, u32[]{:S(2)}) collective-permute-start(bf16[72,2048]{1,0:T(8,128)(2,1)S(1)} %get-tuple-element.193), channel_id=1, source_target_pairs={{0,1},{1,0},{2,3},{3,2},{4,5},{5,4},{6,7},{7,6},{8,9},{9,8},{10,11... | collective-permute-start | bytes 884744 | tf_op jit(solution)/shard_map/ppermute | solution.py:24
  152.6 14.9 %collective-permute-start.55 = (bf16[72,2048]{1,0:T(8,128)(2,1)S(1)}, bf16[72,2048]{1,0:T(8,128)(2,1)S(1)}, u32[]{:S(2)}, u32[]{:S(2)}) collective-permute-start(bf16[72,2048]{1,0:T(8,128)(2,1)S(1)} %get-tuple-element.200), channel_id=1, source_target_pairs={{0,1},{1,0},{2,3},{3,2},{4,5},{5,4},{6,7},{7,6},{8,9},{9,8},{10,11... | collective-permute-start | bytes 884744 | tf_op jit(solution)/shard_map/ppermute | solution.py:24
  158.0 11.0 %collective-permute-start.54 = (bf16[128,1024]{1,0:T(8,128)(2,1)S(1)}, bf16[128,1024]{1,0:T(8,128)(2,1)S(1)}, u32[]{:S(2)}, u32[]{:S(2)}) collective-permute-start(bf16[128,1024]{1,0:T(8,128)(2,1)S(1)} %get-tuple-element.208), channel_id=1, source_target_pairs={{0,2},{1,3},{2,0},{3,1},{4,6},{5,7},{6,4},{7,5},{8,10},{9,11},{10,... | collective-permute-start | bytes 786440 | tf_op jit(solution)/shard_map/ppermute | solution.py:24
  158.7 11.5 %collective-permute-start.56 = (bf16[128,1024]{1,0:T(8,128)(2,1)S(1)}, bf16[128,1024]{1,0:T(8,128)(2,1)S(1)}, u32[]{:S(2)}, u32[]{:S(2)}) collective-permute-start(bf16[128,1024]{1,0:T(8,128)(2,1)S(1)} %add_convert_fusion.5), channel_id=1, source_target_pairs={{0,4},{1,5},{2,6},{3,7},{4,0},{5,1},{6,2},{7,3},{8,12},{9,13},{10,... | collective-permute-start | bytes 786440 | tf_op jit(solution)/shard_map/ppermute | solution.py:24
  160.9 10.3 %collective-permute-start.57 = (bf16[128,1024]{1,0:T(8,128)(2,1)S(1)}, bf16[128,1024]{1,0:T(8,128)(2,1)S(1)}, u32[]{:S(2)}, u32[]{:S(2)}) collective-permute-start(bf16[128,1024]{1,0:T(8,128)(2,1)S(1)} %add_convert_fusion.4), channel_id=1, source_target_pairs={{0,4},{1,5},{2,6},{3,7},{4,0},{5,1},{6,2},{7,3},{8,12},{9,13},{10,... | collective-permute-start | bytes 786440 | tf_op jit(solution)/shard_map/ppermute | solution.py:24
  162.2 13.1 %collective-permute-start.53 = (bf16[128,1024]{1,0:T(8,128)(2,1)S(1)}, bf16[128,1024]{1,0:T(8,128)(2,1)S(1)}, u32[]{:S(2)}, u32[]{:S(2)}) collective-permute-start(bf16[128,1024]{1,0:T(8,128)(2,1)S(1)} %get-tuple-element.213), channel_id=1, source_target_pairs={{0,2},{1,3},{2,0},{3,1},{4,6},{5,7},{6,4},{7,5},{8,10},{9,11},{10,... | collective-permute-start | bytes 786440 | tf_op jit(solution)/shard_map/ppermute | solution.py:24
  169.0 11.9 %collective-permute-start.59 = (bf16[128,1024]{1,0:T(8,128)(2,1)S(1)}, bf16[128,1024]{1,0:T(8,128)(2,1)S(1)}, u32[]{:S(2)}, u32[]{:S(2)}) collective-permute-start(bf16[128,1024]{1,0:T(8,128)(2,1)S(1)} %get-tuple-element.217), channel_id=1, source_target_pairs={{0,2},{1,3},{2,0},{3,1},{4,6},{5,7},{6,4},{7,5},{8,10},{9,11},{10,... | collective-permute-start | bytes 786440 | tf_op jit(solution)/shard_map/ppermute | solution.py:24
  170.3 10.8 %collective-permute-start.64 = (bf16[128,1024]{1,0:T(8,128)(2,1)S(1)}, bf16[128,1024]{1,0:T(8,128)(2,1)S(1)}, u32[]{:S(2)}, u32[]{:S(2)}) collective-permute-start(bf16[128,1024]{1,0:T(8,128)(2,1)S(1)} %get-tuple-element.228), channel_id=1, source_target_pairs={{0,2},{1,3},{2,0},{3,1},{4,6},{5,7},{6,4},{7,5},{8,10},{9,11},{10,... | collective-permute-start | bytes 786440 | tf_op jit(solution)/shard_map/ppermute | solution.py:24
  171.2 15.1 %collective-permute-start.63 = (bf16[128,1024]{1,0:T(8,128)(2,1)S(1)}, bf16[128,1024]{1,0:T(8,128)(2,1)S(1)}, u32[]{:S(2)}, u32[]{:S(2)}) collective-permute-start(bf16[128,1024]{1,0:T(8,128)(2,1)S(1)} %add_convert_fusion.3), channel_id=1, source_target_pairs={{0,8},{1,9},{2,10},{3,11},{4,12},{5,13},{6,14},{7,15},{8,0},{9,1},... | collective-permute-start | bytes 786440 | tf_op jit(solution)/shard_map/ppermute | solution.py:24
  175.3 11.1 %collective-permute-start.62 = (bf16[72,2048]{1,0:T(8,128)(2,1)S(1)}, bf16[72,2048]{1,0:T(8,128)(2,1)S(1)}, u32[]{:S(2)}, u32[]{:S(2)}) collective-permute-start(bf16[72,2048]{1,0:T(8,128)(2,1)S(1)} %get-tuple-element.220), channel_id=1, source_target_pairs={{0,1},{1,0},{2,3},{3,2},{4,5},{5,4},{6,7},{7,6},{8,9},{9,8},{10,11... | collective-permute-start | bytes 884744 | tf_op jit(solution)/shard_map/ppermute | solution.py:24
  176.0 13.6 %collective-permute-start.61 = (bf16[128,1024]{1,0:T(8,128)(2,1)S(1)}, bf16[128,1024]{1,0:T(8,128)(2,1)S(1)}, u32[]{:S(2)}, u32[]{:S(2)}) collective-permute-start(bf16[128,1024]{1,0:T(8,128)(2,1)S(1)} %add_convert_fusion.2), channel_id=1, source_target_pairs={{0,8},{1,9},{2,10},{3,11},{4,12},{5,13},{6,14},{7,15},{8,0},{9,1},... | collective-permute-start | bytes 786440 | tf_op jit(solution)/shard_map/ppermute | solution.py:24
  181.0 10.7 %collective-permute-start.58 = (bf16[72,2048]{1,0:T(8,128)(2,1)S(1)}, bf16[72,2048]{1,0:T(8,128)(2,1)S(1)}, u32[]{:S(2)}, u32[]{:S(2)}) collective-permute-start(bf16[72,2048]{1,0:T(8,128)(2,1)S(1)} %get-tuple-element.225), channel_id=1, source_target_pairs={{0,1},{1,0},{2,3},{3,2},{4,5},{5,4},{6,7},{7,6},{8,9},{9,8},{10,11... | collective-permute-start | bytes 884744 | tf_op jit(solution)/shard_map/ppermute | solution.py:24
  181.1 10.5 %collective-permute-start.60 = (bf16[128,1024]{1,0:T(8,128)(2,1)S(1)}, bf16[128,1024]{1,0:T(8,128)(2,1)S(1)}, u32[]{:S(2)}, u32[]{:S(2)}) collective-permute-start(bf16[128,1024]{1,0:T(8,128)(2,1)S(1)} %add_convert_fusion.1), channel_id=1, source_target_pairs={{0,4},{1,5},{2,6},{3,7},{4,0},{5,1},{6,2},{7,3},{8,12},{9,13},{10,... | collective-permute-start | bytes 786440 | tf_op jit(solution)/shard_map/ppermute | solution.py:24
  (29 other events, 301.4 us)

commit v4 on v3

--- a/solution.py
+++ b/solution.py
@@ -364,12 +364,12 @@
 
 
 STEPS = (
+    ("block", 4, 0),
+    ("block", 8, 0),
     ("block", 2, 0),
     ("pack", 0),
     ("block", 2, 1),
     ("pack", 2),
-    ("block", 4, 0),
-    ("block", 8, 0),
     ("block", 4, 1),
     ("pack", 4),
     ("block", 8, 1),

time: 197 us -> 196 us (level)
  waiting for transfers between devices: 88.8 us -> 81.5 us
  starting transfers between devices: 73.6 us -> 78.9 us
    ppermute x66, waiting for transfers between devices: 86.2 us -> 78.9 us  [swapped(): return lax.ppermute(shard, axis, [(i, i ^ mask) for i in range(devices)])]
    ppermute x66, starting transfers between devices: 73.4 us -> 78.7 us  [swapped(): return lax.ppermute(shard, axis, [(i, i ^ mask) for i in range(devices)])]
  transfers between devices with their start and end apart: 68 -> 68, of which waited for: 39 -> 32; matrix products, arithmetic and copies ran while one was open for 1% -> 1% of each run, Pallas kernels for 12% -> 13%
where the time goes in v4:
time: 196 us; the launch traced here: 195 us
  waiting for transfers between devices  81.5 us (42%)
  starting transfers between devices  78.9 us (40%)
  Pallas kernels  28 us (14%)
  local copies, waits for them, and re-layouts  3.8 us (2%)
  other arithmetic  2.05 us (1%)
    ppermute x66, waiting for transfers between devices, swapped(): return lax.ppermute(shard, axis, [(i, i ^ mask) for i in range(devices)])  78.9 us
    ppermute x66, starting transfers between devices, swapped(): return lax.ppermute(shard, axis, [(i, i ^ mask) for i in range(devices)])  78.7 us
    pallas_call x22, Pallas kernels, local(): pl.pallas_call(kernel, out_shape=out_shape, in_specs=[WHOLE] * len(operan...  22.2 us
  transfers between devices with their start and end apart: 68, of which 32 were waited for; matrix products, arithmetic and copies ran while one was open for 1% of the time, Pallas kernels for 13%

profile of v4, /device:TPU:0, one launch (start us, length us, event | category | flops | bytes accessed | tf_op | source)
XLA Modules:
  0.0 195.2 jit_solution(10564497201886509295)
XLA Ops:
  0.6 4.1 %collective-permute-start.5 = (bf16[64,2048]{1,0:T(8,128)(2,1)}, bf16[64,2048]{1,0:T(8,128)(2,1)S(1)}, u32[]{:S(2)}, u32[]{:S(2)}) collective-permute-start(bf16[64,2048]{1,0:T(8,128)(2,1)} %refs_2_.1), channel_id=1, source_target_pairs={{0,8},{1,9},{2,10},{3,11},{4,12},{5,13},{6,14},{7,15},{8,0},{9,1},... | collective-permute-start | bytes 786440 | tf_op jit(solution)/shard_map/ppermute | solution.py:24
  4.7 1.5 collective-permute-start.4
  7.7 1.6 collective-permute-start.7
  15.0 3.4 %shard_map.131 = (bf16[128,2048]{1,0:T(8,128)(2,1)}, bf16[128,1024]{1,0:T(8,128)(2,1)S(1)}, bf16[128,1024]{1,0:T(8,128)(2,1)S(1)}) custom-call(s32[2]{0:T(128)S(1)} %pad_add_fusion.here, bf16[128,2048]{1,0:T(8,128)(2,1)S(1)} %copy-done.2, bf16[128,256]{1,0:T(8,128)(2,1)S(1)} %collective-permute-done.keys, ...), custom_call_target="tpu_custom_call" | custom-call | tf_op jit(solution)/shard_map/pallas_call | solution.py:123
  22.2 1.5 collective-permute-start.8
  24.4 3.2 %collective-permute-done.11.refs_11_ = bf16[64,2048]{1,0:T(8,128)(2,1)S(1)} collective-permute-done((bf16[64,2048]{1,0:T(8,128)(2,1)S(1)}, bf16[64,2048]{1,0:T(8,128)(2,1)S(1)}, u32[]{:S(2)}, u32[]{:S(2)}) %collective-permute-start.11) | collective-permute-done | bytes 262176 | tf_op jit(solution)/shard_map/ppermute | solution.py:24
  28.6 2.7 %collective-permute-done.14 = f32[1,16,128]{2,1,0:T(8,128)S(1)} collective-permute-done((f32[1,16,128]{2,1,0:T(8,128)S(1)}, f32[1,16,128]{2,1,0:T(8,128)S(1)}, u32[]{:S(2)}, u32[]{:S(2)}) %collective-permute-start.14) | collective-permute-done | bytes 8224 | tf_op jit(solution)/shard_map/ppermute | solution.py:24
  33.2 1.8 collective-permute-done.6.refs_5_
  35.0 3.1 %collective-permute-start.15 = (f32[2,16,128]{2,1,0:T(8,128)S(1)}, f32[2,16,128]{2,1,0:T(8,128)S(1)}, u32[]{:S(2)}, u32[]{:S(2)}) collective-permute-start(f32[2,16,128]{2,1,0:T(8,128)S(1)} %pad_maximum_fusion.2), channel_id=1, source_target_pairs={{0,8},{1,9},{2,10},{3,11},{4,12},{5,13},{6,14},{7,15},{8,0},{9,1},... | collective-permute-start | bytes 49160 | tf_op jit(solution)/shard_map/ppermute | solution.py:24
  38.7 1.5 collective-permute-start.12
  42.2 4.3 %collective-permute-done.13.refs_13_ = bf16[64,2048]{1,0:T(8,128)(2,1)S(1)} collective-permute-done((bf16[64,2048]{1,0:T(8,128)(2,1)S(1)}, bf16[64,2048]{1,0:T(8,128)(2,1)S(1)}, u32[]{:S(2)}, u32[]{:S(2)}) %collective-permute-start.13) | collective-permute-done | bytes 262176 | tf_op jit(solution)/shard_map/ppermute | solution.py:24
  47.6 1.7 collective-permute-done.19.refs_17_
  51.4 2.0 %shard_map.132 = (f32[128,2048]{1,0:T(8,128)S(1)}, f32[128,2048]{1,0:T(8,128)S(1)}) custom-call(bf16[128,1024]{1,0:T(8,128)(2,1)S(1)} %collective-permute-done.2.refs_0_, bf16[128,1024]{1,0:T(8,128)(2,1)S(1)} %get-tuple-element.122.refs_1_, bf16[64,2048]{1,0:T(8,128)(2,1)S(1)} %copy-done.4, bf16[64,2048]{1,0:T(8,128)(2,1)S(1)} %collective-permute-done.3.refs_3_, ...), custom_call_target="tpu_custom_call" | custom-call | tf_op jit(solution)/shard_map/pallas_call | solution.py:206
  53.5 1.5 collective-permute-start.23
  55.0 1.5 collective-permute-start.22
  57.4 1.6 collective-permute-start.25
  59.1 1.6 collective-permute-start.24
  61.1 1.5 collective-permute-start.29
  63.2 1.7 collective-permute-start.34
  64.9 7.4 %collective-permute-done.25.left.refs_0_ = bf16[128,1024]{1,0:T(8,128)(2,1)S(1)} collective-permute-done((bf16[128,1024]{1,0:T(8,128)(2,1)S(1)}, bf16[128,1024]{1,0:T(8,128)(2,1)S(1)}, u32[]{:S(2)}, u32[]{:S(2)}) %collective-permute-start.25) | collective-permute-done | bytes 262176 | tf_op jit(solution)/shard_map/ppermute | solution.py:24
  73.6 3.2 %collective-permute-start.27 = (bf16[128,1024]{1,0:T(8,128)(2,1)S(1)}, bf16[128,1024]{1,0:T(8,128)(2,1)S(1)}, u32[]{:S(2)}, u32[]{:S(2)}) collective-permute-start(bf16[128,1024]{1,0:T(8,128)(2,1)S(1)} %collective-permute-done.24.left.refs_0_), channel_id=1, source_target_pairs={{0,4},{1,5},{2,6},{3,7},{4,0},{5,1},{6,2},{7,3},{8,12},{9,13},{10,... | collective-permute-start | bytes 786440 | tf_op jit(solution)/shard_map/ppermute | solution.py:24
  77.9 5.1 %collective-permute-done.34.right.refs_1_ = bf16[128,1024]{1,0:T(8,128)(2,1)S(1)} collective-permute-done((bf16[128,1024]{1,0:T(8,128)(2,1)S(1)}, bf16[128,1024]{1,0:T(8,128)(2,1)S(1)}, u32[]{:S(2)}, u32[]{:S(2)}) %collective-permute-start.34) | collective-permute-done | bytes 262176 | tf_op jit(solution)/shard_map/ppermute | solution.py:24
  87.8 1.7 collective-permute-start.37
  92.7 3.8 %collective-permute-done.38.right.refs_3_ = bf16[128,1024]{1,0:T(8,128)(2,1)S(1)} collective-permute-done((bf16[128,1024]{1,0:T(8,128)(2,1)S(1)}, bf16[128,1024]{1,0:T(8,128)(2,1)S(1)}, u32[]{:S(2)}, u32[]{:S(2)}) %collective-permute-start.38) | collective-permute-done | bytes 262176 | tf_op jit(solution)/shard_map/ppermute | solution.py:24
  96.6 1.6 collective-permute-start.35
  98.9 3.3 %collective-permute-done.36.left.refs_2_ = bf16[128,1024]{1,0:T(8,128)(2,1)S(1)} collective-permute-done((bf16[128,1024]{1,0:T(8,128)(2,1)S(1)}, bf16[128,1024]{1,0:T(8,128)(2,1)S(1)}, u32[]{:S(2)}, u32[]{:S(2)}) %collective-permute-start.36) | collective-permute-done | bytes 262176 | tf_op jit(solution)/shard_map/ppermute | solution.py:24
  103.1 4.7 %collective-permute-done.35.right.refs_3_ = bf16[128,1024]{1,0:T(8,128)(2,1)S(1)} collective-permute-done((bf16[128,1024]{1,0:T(8,128)(2,1)S(1)}, bf16[128,1024]{1,0:T(8,128)(2,1)S(1)}, u32[]{:S(2)}, u32[]{:S(2)}) %collective-permute-start.35) | collective-permute-done | bytes 262176 | tf_op jit(solution)/shard_map/ppermute | solution.py:24
  109.0 2.3 %collective-permute-done.41.right.refs_3_ = bf16[128,1024]{1,0:T(8,128)(2,1)S(1)} collective-permute-done((bf16[128,1024]{1,0:T(8,128)(2,1)S(1)}, bf16[128,1024]{1,0:T(8,128)(2,1)S(1)}, u32[]{:S(2)}, u32[]{:S(2)}) %collective-permute-start.41) | collective-permute-done | bytes 262176 | tf_op jit(solution)/shard_map/ppermute | solution.py:24
  114.0 4.4 %collective-permute-done.39.refs_5_ = bf16[72,2048]{1,0:T(8,128)(2,1)S(1)} collective-permute-done((bf16[72,2048]{1,0:T(8,128)(2,1)S(1)}, bf16[72,2048]{1,0:T(8,128)(2,1)S(1)}, u32[]{:S(2)}, u32[]{:S(2)}) %collective-permute-start.39) | collective-permute-done | bytes 294944 | tf_op jit(solution)/shard_map/ppermute | solution.py:24
  118.5 4.0 %shard_map.143 = (f32[256,2048]{1,0:T(8,128)S(1)}, bf16[72,2048]{1,0:T(8,128)(2,1)S(1)}, bf16[72,2048]{1,0:T(8,128)(2,1)S(1)}) custom-call(bf16[128,1024]{1,0:T(8,128)(2,1)S(1)} %get-tuple-element.177.left.refs_0_, bf16[128,1024]{1,0:T(8,128)(2,1)S(1)} %get-tuple-element.152.right.refs_1_, bf16[128,1024]{1,0:T(8,128)(2,1)S(1)} %collective-permute-done.29.left.refs_2_, ...), custom_call_target="tpu_custom_call" | custom-call | tf_op jit(solution)/shard_map/pallas_call | solution.py:40
  122.5 2.3 %collective-permute-done.44.refs_5_ = bf16[72,2048]{1,0:T(8,128)(2,1)S(1)} collective-permute-done((bf16[72,2048]{1,0:T(8,128)(2,1)S(1)}, bf16[72,2048]{1,0:T(8,128)(2,1)S(1)}, u32[]{:S(2)}, u32[]{:S(2)}) %collective-permute-start.44) | collective-permute-done | bytes 294944 | tf_op jit(solution)/shard_map/ppermute | solution.py:24
  124.8 4.0 %shard_map.144 = (f32[256,2048]{1,0:T(8,128)S(1)}, bf16[72,2048]{1,0:T(8,128)(2,1)S(1)}, bf16[72,2048]{1,0:T(8,128)(2,1)S(1)}) custom-call(bf16[128,1024]{1,0:T(8,128)(2,1)S(1)} %collective-permute-done.27.left.refs_0_, bf16[128,1024]{1,0:T(8,128)(2,1)S(1)} %collective-permute-done.37.right.refs_1_, ...), custom_call_target="tpu_custom_call" | custom-call | tf_op jit(solution)/shard_map/pallas_call | solution.py:40
  130.9 4.2 %shard_map.145 = (f32[256,2048]{1,0:T(8,128)S(1)}, bf16[72,2048]{1,0:T(8,128)(2,1)S(1)}, bf16[72,2048]{1,0:T(8,128)(2,1)S(1)}) custom-call(bf16[128,1024]{1,0:T(8,128)(2,1)S(1)} %collective-permute-done.24.left.refs_0_, bf16[128,1024]{1,0:T(8,128)(2,1)S(1)} %collective-permute-done.33.right.refs_1_, ...), custom_call_target="tpu_custom_call" | custom-call | tf_op jit(solution)/shard_map/pallas_call | solution.py:40
  136.4 2.4 %collective-permute-done.46.returned = bf16[72,2048]{1,0:T(8,128)(2,1)S(1)} collective-permute-done((bf16[72,2048]{1,0:T(8,128)(2,1)S(1)}, bf16[72,2048]{1,0:T(8,128)(2,1)S(1)}, u32[]{:S(2)}, u32[]{:S(2)}) %collective-permute-start.46) | collective-permute-done | bytes 294944 | tf_op jit(solution)/shard_map/ppermute | solution.py:24
  142.4 4.0 %shard_map.147 = (f32[256,2048]{1,0:T(8,128)S(1)}, bf16[72,2048]{1,0:T(8,128)(2,1)S(1)}, bf16[72,2048]{1,0:T(8,128)(2,1)S(1)}) custom-call(bf16[128,1024]{1,0:T(8,128)(2,1)S(1)} %collective-permute-done.25.left.refs_0_, bf16[128,1024]{1,0:T(8,128)(2,1)S(1)} %collective-permute-done.34.right.refs_1_, ...), custom_call_target="tpu_custom_call" | custom-call | tf_op jit(solution)/shard_map/pallas_call | solution.py:40
  147.7 3.8 %collective-permute-done.52.returned = bf16[72,2048]{1,0:T(8,128)(2,1)S(1)} collective-permute-done((bf16[72,2048]{1,0:T(8,128)(2,1)S(1)}, bf16[72,2048]{1,0:T(8,128)(2,1)S(1)}, u32[]{:S(2)}, u32[]{:S(2)}) %collective-permute-start.52) | collective-permute-done | bytes 294944 | tf_op jit(solution)/shard_map/ppermute | solution.py:24
  153.2 3.3 %collective-permute-start.56 = (bf16[128,1024]{1,0:T(8,128)(2,1)S(1)}, bf16[128,1024]{1,0:T(8,128)(2,1)S(1)}, u32[]{:S(2)}, u32[]{:S(2)}) collective-permute-start(bf16[128,1024]{1,0:T(8,128)(2,1)S(1)} %add_convert_fusion.5), channel_id=1, source_target_pairs={{0,4},{1,5},{2,6},{3,7},{4,0},{5,1},{6,2},{7,3},{8,12},{9,13},{10,... | collective-permute-start | bytes 786440 | tf_op jit(solution)/shard_map/ppermute | solution.py:24
  158.0 2.8 %collective-permute-done.55.returned = bf16[72,2048]{1,0:T(8,128)(2,1)S(1)} collective-permute-done((bf16[72,2048]{1,0:T(8,128)(2,1)S(1)}, bf16[72,2048]{1,0:T(8,128)(2,1)S(1)}, u32[]{:S(2)}, u32[]{:S(2)}) %collective-permute-start.55) | collective-permute-done | bytes 294944 | tf_op jit(solution)/shard_map/ppermute | solution.py:24
  160.8 1.7 collective-permute-start.47
  165.6 2.9 %collective-permute-start.63 = (bf16[128,1024]{1,0:T(8,128)(2,1)S(1)}, bf16[128,1024]{1,0:T(8,128)(2,1)S(1)}, u32[]{:S(2)}, u32[]{:S(2)}) collective-permute-start(bf16[128,1024]{1,0:T(8,128)(2,1)S(1)} %add_convert_fusion.3), channel_id=1, source_target_pairs={{0,8},{1,9},{2,10},{3,11},{4,12},{5,13},{6,14},{7,15},{8,0},{9,1},... | collective-permute-start | bytes 786440 | tf_op jit(solution)/shard_map/ppermute | solution.py:24
  168.7 1.6 collective-permute-done.47.returned
  170.2 3.6 %collective-permute-start.61 = (bf16[128,1024]{1,0:T(8,128)(2,1)S(1)}, bf16[128,1024]{1,0:T(8,128)(2,1)S(1)}, u32[]{:S(2)}, u32[]{:S(2)}) collective-permute-start(bf16[128,1024]{1,0:T(8,128)(2,1)S(1)} %add_convert_fusion.2), channel_id=1, source_target_pairs={{0,8},{1,9},{2,10},{3,11},{4,12},{5,13},{6,14},{7,15},{8,0},{9,1},... | collective-permute-start | bytes 786440 | tf_op jit(solution)/shard_map/ppermute | solution.py:24
  174.6 1.9 collective-permute-start.60
  176.7 5.3 %collective-permute-done.63.refs_2_ = bf16[128,1024]{1,0:T(8,128)(2,1)S(1)} collective-permute-done((bf16[128,1024]{1,0:T(8,128)(2,1)S(1)}, bf16[128,1024]{1,0:T(8,128)(2,1)S(1)}, u32[]{:S(2)}, u32[]{:S(2)}) %collective-permute-start.63) | collective-permute-done | bytes 262176 | tf_op jit(solution)/shard_map/ppermute | solution.py:24
  183.4 2.1 %collective-permute-done.61.refs_3_ = bf16[128,1024]{1,0:T(8,128)(2,1)S(1)} collective-permute-done((bf16[128,1024]{1,0:T(8,128)(2,1)S(1)}, bf16[128,1024]{1,0:T(8,128)(2,1)S(1)}, u32[]{:S(2)}, u32[]{:S(2)}) %collective-permute-start.61) | collective-permute-done | bytes 262176 | tf_op jit(solution)/shard_map/ppermute | solution.py:24
  186.6 2.4 %collective-permute-done.60.refs_4_ = bf16[128,1024]{1,0:T(8,128)(2,1)S(1)} collective-permute-done((bf16[128,1024]{1,0:T(8,128)(2,1)S(1)}, bf16[128,1024]{1,0:T(8,128)(2,1)S(1)}, u32[]{:S(2)}, u32[]{:S(2)}) %collective-permute-start.60) | collective-permute-done | bytes 262176 | tf_op jit(solution)/shard_map/ppermute | solution.py:24
  189.3 3.2 %collective-permute-done.65.refs_5_ = bf16[128,1024]{1,0:T(8,128)(2,1)S(1)} collective-permute-done((bf16[128,1024]{1,0:T(8,128)(2,1)S(1)}, bf16[128,1024]{1,0:T(8,128)(2,1)S(1)}, u32[]{:S(2)}, u32[]{:S(2)}) %collective-permute-start.65) | collective-permute-done | bytes 262176 | tf_op jit(solution)/shard_map/ppermute | solution.py:24
  192.5 1.6 collective-permute-done.66.refs_6_
  (148 shorter events, 57.5 us)
Async XLA Ops:
  0.6 17.8 %collective-permute-start.5 = (bf16[64,2048]{1,0:T(8,128)(2,1)}, bf16[64,2048]{1,0:T(8,128)(2,1)S(1)}, u32[]{:S(2)}, u32[]{:S(2)}) collective-permute-start(bf16[64,2048]{1,0:T(8,128)(2,1)} %refs_2_.1), channel_id=1, source_target_pairs={{0,8},{1,9},{2,10},{3,11},{4,12},{5,13},{6,14},{7,15},{8,0},{9,1},... | collective-permute-start | bytes 786440 | tf_op jit(solution)/shard_map/ppermute | solution.py:24
  4.7 15.4 %collective-permute-start.4 = (bf16[64,2048]{1,0:T(8,128)(2,1)}, bf16[64,2048]{1,0:T(8,128)(2,1)S(1)}, u32[]{:S(2)}, u32[]{:S(2)}) collective-permute-start(bf16[64,2048]{1,0:T(8,128)(2,1)} %refs_2_.1), channel_id=1, source_target_pairs={{0,2},{1,3},{2,0},{3,1},{4,6},{5,7},{6,4},{7,5},{8,10},{9,11},{10,... | collective-permute-start | bytes 786440 | tf_op jit(solution)/shard_map/ppermute | solution.py:24
  6.3 15.1 %collective-permute-start.3 = (bf16[64,2048]{1,0:T(8,128)(2,1)}, bf16[64,2048]{1,0:T(8,128)(2,1)S(1)}, u32[]{:S(2)}, u32[]{:S(2)}) collective-permute-start(bf16[64,2048]{1,0:T(8,128)(2,1)} %refs_2_.1), channel_id=1, source_target_pairs={{0,1},{1,0},{2,3},{3,2},{4,5},{5,4},{6,7},{7,6},{8,9},{9,8},{10,11... | collective-permute-start | bytes 786440 | tf_op jit(solution)/shard_map/ppermute | solution.py:24
  7.7 14.4 %collective-permute-start.7 = (bf16[64,2048]{1,0:T(8,128)(2,1)}, bf16[64,2048]{1,0:T(8,128)(2,1)S(1)}, u32[]{:S(2)}, u32[]{:S(2)}) collective-permute-start(bf16[64,2048]{1,0:T(8,128)(2,1)} %refs_2_.1), channel_id=1, source_target_pairs={{0,4},{1,5},{2,6},{3,7},{4,0},{5,1},{6,2},{7,3},{8,12},{9,13},{10,... | collective-permute-start | bytes 786440 | tf_op jit(solution)/shard_map/ppermute | solution.py:24
  20.1 11.6 %collective-permute-start.9 = (bf16[64,2048]{1,0:T(8,128)(2,1)S(1)}, bf16[64,2048]{1,0:T(8,128)(2,1)S(1)}, u32[]{:S(2)}, u32[]{:S(2)}) collective-permute-start(bf16[64,2048]{1,0:T(8,128)(2,1)S(1)} %collective-permute-done.5.refs_10_), channel_id=1, source_target_pairs={{0,2},{1,3},{2,0},{3,1},{4,6},{5,7},{6,4},{7,5},{8,10},{9,11},{10,... | collective-permute-start | bytes 786440 | tf_op jit(solution)/shard_map/ppermute | solution.py:24
  21.4 13.6 %collective-permute-start.6 = (bf16[64,2048]{1,0:T(8,128)(2,1)S(1)}, bf16[64,2048]{1,0:T(8,128)(2,1)S(1)}, u32[]{:S(2)}, u32[]{:S(2)}) collective-permute-start(bf16[64,2048]{1,0:T(8,128)(2,1)S(1)} %collective-permute-done.3.refs_3_), channel_id=1, source_target_pairs={{0,2},{1,3},{2,0},{3,1},{4,6},{5,7},{6,4},{7,5},{8,10},{9,11},{10,... | collective-permute-start | bytes 786440 | tf_op jit(solution)/shard_map/ppermute | solution.py:24
  22.2 11.1 %collective-permute-start.8 = (bf16[64,2048]{1,0:T(8,128)(2,1)S(1)}, bf16[64,2048]{1,0:T(8,128)(2,1)S(1)}, u32[]{:S(2)}, u32[]{:S(2)}) collective-permute-start(bf16[64,2048]{1,0:T(8,128)(2,1)S(1)} %collective-permute-done.7.refs_6_), channel_id=1, source_target_pairs={{0,1},{1,0},{2,3},{3,2},{4,5},{5,4},{6,7},{7,6},{8,9},{9,8},{10,11... | collective-permute-start | bytes 786440 | tf_op jit(solution)/shard_map/ppermute | solution.py:24
  28.1 12.1 %collective-permute-start.17 = (bf16[64,2048]{1,0:T(8,128)(2,1)S(1)}, bf16[64,2048]{1,0:T(8,128)(2,1)S(1)}, u32[]{:S(2)}, u32[]{:S(2)}) collective-permute-start(bf16[64,2048]{1,0:T(8,128)(2,1)S(1)} %collective-permute-done.10.refs_14_), channel_id=1, source_target_pairs={{0,1},{1,0},{2,3},{3,2},{4,5},{5,4},{6,7},{7,6},{8,9},{9,8},{10,11... | collective-permute-start | bytes 786440 | tf_op jit(solution)/shard_map/ppermute | solution.py:24
  57.4 14.9 %collective-permute-start.25 = (bf16[128,1024]{1,0:T(8,128)(2,1)S(1)}, bf16[128,1024]{1,0:T(8,128)(2,1)S(1)}, u32[]{:S(2)}, u32[]{:S(2)}) collective-permute-start(bf16[128,1024]{1,0:T(8,128)(2,1)S(1)} %get-tuple-element.177.left.refs_0_), channel_id=1, source_target_pairs={{0,4},{1,5},{2,6},{3,7},{4,0},{5,1},{6,2},{7,3},{8,12},{9,13},{10,... | collective-permute-start | bytes 786440 | tf_op jit(solution)/shard_map/ppermute | solution.py:24
  59.1 13.3 %collective-permute-start.24 = (bf16[128,1024]{1,0:T(8,128)(2,1)S(1)}, bf16[128,1024]{1,0:T(8,128)(2,1)S(1)}, u32[]{:S(2)}, u32[]{:S(2)}) collective-permute-start(bf16[128,1024]{1,0:T(8,128)(2,1)S(1)} %get-tuple-element.177.left.refs_0_), channel_id=1, source_target_pairs={{0,8},{1,9},{2,10},{3,11},{4,12},{5,13},{6,14},{7,15},{8,0},{9,1},... | collective-permute-start | bytes 786440 | tf_op jit(solution)/shard_map/ppermute | solution.py:24
  61.1 12.5 %collective-permute-start.29 = (bf16[128,1024]{1,0:T(8,128)(2,1)S(1)}, bf16[128,1024]{1,0:T(8,128)(2,1)S(1)}, u32[]{:S(2)}, u32[]{:S(2)}) collective-permute-start(bf16[128,1024]{1,0:T(8,128)(2,1)S(1)} %get-tuple-element.177.left.refs_0_), channel_id=1, source_target_pairs={{0,2},{1,3},{2,0},{3,1},{4,6},{5,7},{6,4},{7,5},{8,10},{9,11},{10,... | collective-permute-start | bytes 786440 | tf_op jit(solution)/shard_map/ppermute | solution.py:24
  62.6 14.4 %collective-permute-start.30 = (bf16[128,1024]{1,0:T(8,128)(2,1)S(1)}, bf16[128,1024]{1,0:T(8,128)(2,1)S(1)}, u32[]{:S(2)}, u32[]{:S(2)}) collective-permute-start(bf16[128,1024]{1,0:T(8,128)(2,1)S(1)} %get-tuple-element.152.right.refs_1_), channel_id=1, source_target_pairs={{0,2},{1,3},{2,0},{3,1},{4,6},{5,7},{6,4},{7,5},{8,10},{9,11},{10,... | collective-permute-start | bytes 786440 | tf_op jit(solution)/shard_map/ppermute | solution.py:24
  63.2 19.8 %collective-permute-start.34 = (bf16[128,1024]{1,0:T(8,128)(2,1)S(1)}, bf16[128,1024]{1,0:T(8,128)(2,1)S(1)}, u32[]{:S(2)}, u32[]{:S(2)}) collective-permute-start(bf16[128,1024]{1,0:T(8,128)(2,1)S(1)} %get-tuple-element.152.right.refs_1_), channel_id=1, source_target_pairs={{0,4},{1,5},{2,6},{3,7},{4,0},{5,1},{6,2},{7,3},{8,12},{9,13},{10,... | collective-permute-start | bytes 786440 | tf_op jit(solution)/shard_map/ppermute | solution.py:24
  72.4 12.1 %collective-permute-start.33 = (bf16[128,1024]{1,0:T(8,128)(2,1)S(1)}, bf16[128,1024]{1,0:T(8,128)(2,1)S(1)}, u32[]{:S(2)}, u32[]{:S(2)}) collective-permute-start(bf16[128,1024]{1,0:T(8,128)(2,1)S(1)} %get-tuple-element.152.right.refs_1_), channel_id=1, source_target_pairs={{0,8},{1,9},{2,10},{3,11},{4,12},{5,13},{6,14},{7,15},{8,0},{9,1},... | collective-permute-start | bytes 786440 | tf_op jit(solution)/shard_map/ppermute | solution.py:24
  72.4 13.2 %collective-permute-start.28 = (bf16[128,1024]{1,0:T(8,128)(2,1)S(1)}, bf16[128,1024]{1,0:T(8,128)(2,1)S(1)}, u32[]{:S(2)}, u32[]{:S(2)}) collective-permute-start(bf16[128,1024]{1,0:T(8,128)(2,1)S(1)} %collective-permute-done.25.left.refs_0_), channel_id=1, source_target_pairs={{0,2},{1,3},{2,0},{3,1},{4,6},{5,7},{6,4},{7,5},{8,10},{9,11},{10,... | collective-permute-start | bytes 786440 | tf_op jit(solution)/shard_map/ppermute | solution.py:24
  73.6 14.2 %collective-permute-start.27 = (bf16[128,1024]{1,0:T(8,128)(2,1)S(1)}, bf16[128,1024]{1,0:T(8,128)(2,1)S(1)}, u32[]{:S(2)}, u32[]{:S(2)}) collective-permute-start(bf16[128,1024]{1,0:T(8,128)(2,1)S(1)} %collective-permute-done.24.left.refs_0_), channel_id=1, source_target_pairs={{0,4},{1,5},{2,6},{3,7},{4,0},{5,1},{6,2},{7,3},{8,12},{9,13},{10,... | collective-permute-start | bytes 786440 | tf_op jit(solution)/shard_map/ppermute | solution.py:24
  77.3 12.2 %collective-permute-start.31 = (bf16[72,2048]{1,0:T(8,128)(2,1)S(1)}, bf16[72,2048]{1,0:T(8,128)(2,1)S(1)}, u32[]{:S(2)}, u32[]{:S(2)}) collective-permute-start(bf16[72,2048]{1,0:T(8,128)(2,1)S(1)} %shard_map.136), channel_id=1, source_target_pairs={{0,1},{1,0},{2,3},{3,2},{4,5},{5,4},{6,7},{7,6},{8,9},{9,8},{10,11... | collective-permute-start | bytes 884744 | tf_op jit(solution)/shard_map/ppermute | solution.py:24
  85.5 11.0 %collective-permute-start.38 = (bf16[128,1024]{1,0:T(8,128)(2,1)S(1)}, bf16[128,1024]{1,0:T(8,128)(2,1)S(1)}, u32[]{:S(2)}, u32[]{:S(2)}) collective-permute-start(bf16[128,1024]{1,0:T(8,128)(2,1)S(1)} %collective-permute-done.34.right.refs_1_), channel_id=1, source_target_pairs={{0,2},{1,3},{2,0},{3,1},{4,6},{5,7},{6,4},{7,5},{8,10},{9,11},{10,... | collective-permute-start | bytes 786440 | tf_op jit(solution)/shard_map/ppermute | solution.py:24
  87.8 10.4 %collective-permute-start.37 = (bf16[128,1024]{1,0:T(8,128)(2,1)S(1)}, bf16[128,1024]{1,0:T(8,128)(2,1)S(1)}, u32[]{:S(2)}, u32[]{:S(2)}) collective-permute-start(bf16[128,1024]{1,0:T(8,128)(2,1)S(1)} %collective-permute-done.33.right.refs_1_), channel_id=1, source_target_pairs={{0,4},{1,5},{2,6},{3,7},{4,0},{5,1},{6,2},{7,3},{8,12},{9,13},{10,... | collective-permute-start | bytes 786440 | tf_op jit(solution)/shard_map/ppermute | solution.py:24
  89.5 19.6 %collective-permute-start.43 = (bf16[72,2048]{1,0:T(8,128)(2,1)S(1)}, bf16[72,2048]{1,0:T(8,128)(2,1)S(1)}, u32[]{:S(2)}, u32[]{:S(2)}) collective-permute-start(bf16[72,2048]{1,0:T(8,128)(2,1)S(1)} %shard_map.137), channel_id=1, source_target_pairs={{0,1},{1,0},{2,3},{3,2},{4,5},{5,4},{6,7},{7,6},{8,9},{9,8},{10,11... | collective-permute-start | bytes 884744 | tf_op jit(solution)/shard_map/ppermute | solution.py:24
  91.2 17.8 %collective-permute-start.42 = (bf16[72,2048]{1,0:T(8,128)(2,1)S(1)}, bf16[72,2048]{1,0:T(8,128)(2,1)S(1)}, u32[]{:S(2)}, u32[]{:S(2)}) collective-permute-start(bf16[72,2048]{1,0:T(8,128)(2,1)S(1)} %shard_map.138), channel_id=1, source_target_pairs={{0,1},{1,0},{2,3},{3,2},{4,5},{5,4},{6,7},{7,6},{8,9},{9,8},{10,11... | collective-permute-start | bytes 884744 | tf_op jit(solution)/shard_map/ppermute | solution.py:24
  91.8 10.4 %collective-permute-start.36 = (bf16[128,1024]{1,0:T(8,128)(2,1)S(1)}, bf16[128,1024]{1,0:T(8,128)(2,1)S(1)}, u32[]{:S(2)}, u32[]{:S(2)}) collective-permute-start(bf16[128,1024]{1,0:T(8,128)(2,1)S(1)} %collective-permute-done.27.left.refs_0_), channel_id=1, source_target_pairs={{0,2},{1,3},{2,0},{3,1},{4,6},{5,7},{6,4},{7,5},{8,10},{9,11},{10,... | collective-permute-start | bytes 786440 | tf_op jit(solution)/shard_map/ppermute | solution.py:24
  96.6 11.2 %collective-permute-start.35 = (bf16[128,1024]{1,0:T(8,128)(2,1)S(1)}, bf16[128,1024]{1,0:T(8,128)(2,1)S(1)}, u32[]{:S(2)}, u32[]{:S(2)}) collective-permute-start(bf16[128,1024]{1,0:T(8,128)(2,1)S(1)} %collective-permute-done.33.right.refs_1_), channel_id=1, source_target_pairs={{0,2},{1,3},{2,0},{3,1},{4,6},{5,7},{6,4},{7,5},{8,10},{9,11},{10,... | collective-permute-start | bytes 786440 | tf_op jit(solution)/shard_map/ppermute | solution.py:24
  98.2 13.1 %collective-permute-start.41 = (bf16[128,1024]{1,0:T(8,128)(2,1)S(1)}, bf16[128,1024]{1,0:T(8,128)(2,1)S(1)}, u32[]{:S(2)}, u32[]{:S(2)}) collective-permute-start(bf16[128,1024]{1,0:T(8,128)(2,1)S(1)} %collective-permute-done.37.right.refs_1_), channel_id=1, source_target_pairs={{0,2},{1,3},{2,0},{3,1},{4,6},{5,7},{6,4},{7,5},{8,10},{9,11},{10,... | collective-permute-start | bytes 786440 | tf_op jit(solution)/shard_map/ppermute | solution.py:24
  102.2 11.8 %collective-permute-start.40 = (bf16[72,2048]{1,0:T(8,128)(2,1)S(1)}, bf16[72,2048]{1,0:T(8,128)(2,1)S(1)}, u32[]{:S(2)}, u32[]{:S(2)}) collective-permute-start(bf16[72,2048]{1,0:T(8,128)(2,1)S(1)} %shard_map.139), channel_id=1, source_target_pairs={{0,1},{1,0},{2,3},{3,2},{4,5},{5,4},{6,7},{7,6},{8,9},{9,8},{10,11... | collective-permute-start | bytes 884744 | tf_op jit(solution)/shard_map/ppermute | solution.py:24
  108.0 10.4 %collective-permute-start.39 = (bf16[72,2048]{1,0:T(8,128)(2,1)S(1)}, bf16[72,2048]{1,0:T(8,128)(2,1)S(1)}, u32[]{:S(2)}, u32[]{:S(2)}) collective-permute-start(bf16[72,2048]{1,0:T(8,128)(2,1)S(1)} %shard_map.140), channel_id=1, source_target_pairs={{0,1},{1,0},{2,3},{3,2},{4,5},{5,4},{6,7},{7,6},{8,9},{9,8},{10,11... | collective-permute-start | bytes 884744 | tf_op jit(solution)/shard_map/ppermute | solution.py:24
  111.6 13.2 %collective-permute-start.44 = (bf16[72,2048]{1,0:T(8,128)(2,1)S(1)}, bf16[72,2048]{1,0:T(8,128)(2,1)S(1)}, u32[]{:S(2)}, u32[]{:S(2)}) collective-permute-start(bf16[72,2048]{1,0:T(8,128)(2,1)S(1)} %shard_map.141), channel_id=1, source_target_pairs={{0,1},{1,0},{2,3},{3,2},{4,5},{5,4},{6,7},{7,6},{8,9},{9,8},{10,11... | collective-permute-start | bytes 884744 | tf_op jit(solution)/shard_map/ppermute | solution.py:24
  113.1 15.7 %collective-permute-start.45 = (bf16[72,2048]{1,0:T(8,128)(2,1)S(1)}, bf16[72,2048]{1,0:T(8,128)(2,1)S(1)}, u32[]{:S(2)}, u32[]{:S(2)}) collective-permute-start(bf16[72,2048]{1,0:T(8,128)(2,1)S(1)} %shard_map.142), channel_id=1, source_target_pairs={{0,1},{1,0},{2,3},{3,2},{4,5},{5,4},{6,7},{7,6},{8,9},{9,8},{10,11... | collective-permute-start | bytes 884744 | tf_op jit(solution)/shard_map/ppermute | solution.py:24
  128.8 10.0 %collective-permute-start.46 = (bf16[72,2048]{1,0:T(8,128)(2,1)S(1)}, bf16[72,2048]{1,0:T(8,128)(2,1)S(1)}, u32[]{:S(2)}, u32[]{:S(2)}) collective-permute-start(bf16[72,2048]{1,0:T(8,128)(2,1)S(1)} %get-tuple-element.187), channel_id=1, source_target_pairs={{0,1},{1,0},{2,3},{3,2},{4,5},{5,4},{6,7},{7,6},{8,9},{9,8},{10,11... | collective-permute-start | bytes 884744 | tf_op jit(solution)/shard_map/ppermute | solution.py:24
  130.0 16.4 %collective-permute-start.49 = (bf16[72,2048]{1,0:T(8,128)(2,1)S(1)}, bf16[72,2048]{1,0:T(8,128)(2,1)S(1)}, u32[]{:S(2)}, u32[]{:S(2)}) collective-permute-start(bf16[72,2048]{1,0:T(8,128)(2,1)S(1)} %get-tuple-element.188), channel_id=1, source_target_pairs={{0,1},{1,0},{2,3},{3,2},{4,5},{5,4},{6,7},{7,6},{8,9},{9,8},{10,11... | collective-permute-start | bytes 884744 | tf_op jit(solution)/shard_map/ppermute | solution.py:24
  135.1 16.3 %collective-permute-start.52 = (bf16[72,2048]{1,0:T(8,128)(2,1)S(1)}, bf16[72,2048]{1,0:T(8,128)(2,1)S(1)}, u32[]{:S(2)}, u32[]{:S(2)}) collective-permute-start(bf16[72,2048]{1,0:T(8,128)(2,1)S(1)} %get-tuple-element.192), channel_id=1, source_target_pairs={{0,1},{1,0},{2,3},{3,2},{4,5},{5,4},{6,7},{7,6},{8,9},{9,8},{10,11... | collective-permute-start | bytes 884744 | tf_op jit(solution)/shard_map/ppermute | solution.py:24
  139.1 14.0 %collective-permute-start.51 = (bf16[128,1024]{1,0:T(8,128)(2,1)S(1)}, bf16[128,1024]{1,0:T(8,128)(2,1)S(1)}, u32[]{:S(2)}, u32[]{:S(2)}) collective-permute-start(bf16[128,1024]{1,0:T(8,128)(2,1)S(1)} %get-tuple-element.195), channel_id=1, source_target_pairs={{0,2},{1,3},{2,0},{3,1},{4,6},{5,7},{6,4},{7,5},{8,10},{9,11},{10,... | collective-permute-start | bytes 786440 | tf_op jit(solution)/shard_map/ppermute | solution.py:24
  140.5 16.0 %collective-permute-start.50 = (bf16[128,1024]{1,0:T(8,128)(2,1)S(1)}, bf16[128,1024]{1,0:T(8,128)(2,1)S(1)}, u32[]{:S(2)}, u32[]{:S(2)}) collective-permute-start(bf16[128,1024]{1,0:T(8,128)(2,1)S(1)} %get-tuple-element.205), channel_id=1, source_target_pairs={{0,2},{1,3},{2,0},{3,1},{4,6},{5,7},{6,4},{7,5},{8,10},{9,11},{10,... | collective-permute-start | bytes 786440 | tf_op jit(solution)/shard_map/ppermute | solution.py:24
  141.2 15.7 %collective-permute-start.48 = (bf16[72,2048]{1,0:T(8,128)(2,1)S(1)}, bf16[72,2048]{1,0:T(8,128)(2,1)S(1)}, u32[]{:S(2)}, u32[]{:S(2)}) collective-permute-start(bf16[72,2048]{1,0:T(8,128)(2,1)S(1)} %get-tuple-element.193), channel_id=1, source_target_pairs={{0,1},{1,0},{2,3},{3,2},{4,5},{5,4},{6,7},{7,6},{8,9},{9,8},{10,11... | collective-permute-start | bytes 884744 | tf_op jit(solution)/shard_map/ppermute | solution.py:24
  146.4 14.3 %collective-permute-start.55 = (bf16[72,2048]{1,0:T(8,128)(2,1)S(1)}, bf16[72,2048]{1,0:T(8,128)(2,1)S(1)}, u32[]{:S(2)}, u32[]{:S(2)}) collective-permute-start(bf16[72,2048]{1,0:T(8,128)(2,1)S(1)} %get-tuple-element.200), channel_id=1, source_target_pairs={{0,1},{1,0},{2,3},{3,2},{4,5},{5,4},{6,7},{7,6},{8,9},{9,8},{10,11... | collective-permute-start | bytes 884744 | tf_op jit(solution)/shard_map/ppermute | solution.py:24
  151.8 11.1 %collective-permute-start.54 = (bf16[128,1024]{1,0:T(8,128)(2,1)S(1)}, bf16[128,1024]{1,0:T(8,128)(2,1)S(1)}, u32[]{:S(2)}, u32[]{:S(2)}) collective-permute-start(bf16[128,1024]{1,0:T(8,128)(2,1)S(1)} %get-tuple-element.208), channel_id=1, source_target_pairs={{0,2},{1,3},{2,0},{3,1},{4,6},{5,7},{6,4},{7,5},{8,10},{9,11},{10,... | collective-permute-start | bytes 786440 | tf_op jit(solution)/shard_map/ppermute | solution.py:24
  153.2 10.7 %collective-permute-start.56 = (bf16[128,1024]{1,0:T(8,128)(2,1)S(1)}, bf16[128,1024]{1,0:T(8,128)(2,1)S(1)}, u32[]{:S(2)}, u32[]{:S(2)}) collective-permute-start(bf16[128,1024]{1,0:T(8,128)(2,1)S(1)} %add_convert_fusion.5), channel_id=1, source_target_pairs={{0,4},{1,5},{2,6},{3,7},{4,0},{5,1},{6,2},{7,3},{8,12},{9,13},{10,... | collective-permute-start | bytes 786440 | tf_op jit(solution)/shard_map/ppermute | solution.py:24
  156.9 11.7 %collective-permute-start.53 = (bf16[128,1024]{1,0:T(8,128)(2,1)S(1)}, bf16[128,1024]{1,0:T(8,128)(2,1)S(1)}, u32[]{:S(2)}, u32[]{:S(2)}) collective-permute-start(bf16[128,1024]{1,0:T(8,128)(2,1)S(1)} %get-tuple-element.213), channel_id=1, source_target_pairs={{0,2},{1,3},{2,0},{3,1},{4,6},{5,7},{6,4},{7,5},{8,10},{9,11},{10,... | collective-permute-start | bytes 786440 | tf_op jit(solution)/shard_map/ppermute | solution.py:24
  160.8 9.5 %collective-permute-start.47 = (bf16[72,2048]{1,0:T(8,128)(2,1)S(1)}, bf16[72,2048]{1,0:T(8,128)(2,1)S(1)}, u32[]{:S(2)}, u32[]{:S(2)}) collective-permute-start(bf16[72,2048]{1,0:T(8,128)(2,1)S(1)} %get-tuple-element.201), channel_id=1, source_target_pairs={{0,1},{1,0},{2,3},{3,2},{4,5},{5,4},{6,7},{7,6},{8,9},{9,8},{10,11... | collective-permute-start | bytes 884744 | tf_op jit(solution)/shard_map/ppermute | solution.py:24
  162.8 11.3 %collective-permute-start.59 = (bf16[128,1024]{1,0:T(8,128)(2,1)S(1)}, bf16[128,1024]{1,0:T(8,128)(2,1)S(1)}, u32[]{:S(2)}, u32[]{:S(2)}) collective-permute-start(bf16[128,1024]{1,0:T(8,128)(2,1)S(1)} %get-tuple-element.217), channel_id=1, source_target_pairs={{0,2},{1,3},{2,0},{3,1},{4,6},{5,7},{6,4},{7,5},{8,10},{9,11},{10,... | collective-permute-start | bytes 786440 | tf_op jit(solution)/shard_map/ppermute | solution.py:24
  163.9 10.8 %collective-permute-start.64 = (bf16[128,1024]{1,0:T(8,128)(2,1)S(1)}, bf16[128,1024]{1,0:T(8,128)(2,1)S(1)}, u32[]{:S(2)}, u32[]{:S(2)}) collective-permute-start(bf16[128,1024]{1,0:T(8,128)(2,1)S(1)} %get-tuple-element.228), channel_id=1, source_target_pairs={{0,2},{1,3},{2,0},{3,1},{4,6},{5,7},{6,4},{7,5},{8,10},{9,11},{10,... | collective-permute-start | bytes 786440 | tf_op jit(solution)/shard_map/ppermute | solution.py:24
  165.6 16.3 %collective-permute-start.63 = (bf16[128,1024]{1,0:T(8,128)(2,1)S(1)}, bf16[128,1024]{1,0:T(8,128)(2,1)S(1)}, u32[]{:S(2)}, u32[]{:S(2)}) collective-permute-start(bf16[128,1024]{1,0:T(8,128)(2,1)S(1)} %add_convert_fusion.3), channel_id=1, source_target_pairs={{0,8},{1,9},{2,10},{3,11},{4,12},{5,13},{6,14},{7,15},{8,0},{9,1},... | collective-permute-start | bytes 786440 | tf_op jit(solution)/shard_map/ppermute | solution.py:24
  168.6 13.4 %collective-permute-start.62 = (bf16[72,2048]{1,0:T(8,128)(2,1)S(1)}, bf16[72,2048]{1,0:T(8,128)(2,1)S(1)}, u32[]{:S(2)}, u32[]{:S(2)}) collective-permute-start(bf16[72,2048]{1,0:T(8,128)(2,1)S(1)} %get-tuple-element.220), channel_id=1, source_target_pairs={{0,1},{1,0},{2,3},{3,2},{4,5},{5,4},{6,7},{7,6},{8,9},{9,8},{10,11... | collective-permute-start | bytes 884744 | tf_op jit(solution)/shard_map/ppermute | solution.py:24
  170.2 15.3 %collective-permute-start.61 = (bf16[128,1024]{1,0:T(8,128)(2,1)S(1)}, bf16[128,1024]{1,0:T(8,128)(2,1)S(1)}, u32[]{:S(2)}, u32[]{:S(2)}) collective-permute-start(bf16[128,1024]{1,0:T(8,128)(2,1)S(1)} %add_convert_fusion.2), channel_id=1, source_target_pairs={{0,8},{1,9},{2,10},{3,11},{4,12},{5,13},{6,14},{7,15},{8,0},{9,1},... | collective-permute-start | bytes 786440 | tf_op jit(solution)/shard_map/ppermute | solution.py:24
  174.2 14.8 %collective-permute-start.58 = (bf16[72,2048]{1,0:T(8,128)(2,1)S(1)}, bf16[72,2048]{1,0:T(8,128)(2,1)S(1)}, u32[]{:S(2)}, u32[]{:S(2)}) collective-permute-start(bf16[72,2048]{1,0:T(8,128)(2,1)S(1)} %get-tuple-element.225), channel_id=1, source_target_pairs={{0,1},{1,0},{2,3},{3,2},{4,5},{5,4},{6,7},{7,6},{8,9},{9,8},{10,11... | collective-permute-start | bytes 884744 | tf_op jit(solution)/shard_map/ppermute | solution.py:24
  174.6 14.3 %collective-permute-start.60 = (bf16[128,1024]{1,0:T(8,128)(2,1)S(1)}, bf16[128,1024]{1,0:T(8,128)(2,1)S(1)}, u32[]{:S(2)}, u32[]{:S(2)}) collective-permute-start(bf16[128,1024]{1,0:T(8,128)(2,1)S(1)} %add_convert_fusion.1), channel_id=1, source_target_pairs={{0,4},{1,5},{2,6},{3,7},{4,0},{5,1},{6,2},{7,3},{8,12},{9,13},{10,... | collective-permute-start | bytes 786440 | tf_op jit(solution)/shard_map/ppermute | solution.py:24
  182.0 10.5 %collective-permute-start.65 = (bf16[128,1024]{1,0:T(8,128)(2,1)S(1)}, bf16[128,1024]{1,0:T(8,128)(2,1)S(1)}, u32[]{:S(2)}, u32[]{:S(2)}) collective-permute-start(bf16[128,1024]{1,0:T(8,128)(2,1)S(1)} %add_convert_fusion), channel_id=1, source_target_pairs={{0,4},{1,5},{2,6},{3,7},{4,0},{5,1},{6,2},{7,3},{8,12},{9,13},{10,... | collective-permute-start | bytes 786440 | tf_op jit(solution)/shard_map/ppermute | solution.py:24
  182.3 10.2 %collective-permute-start.67 = (bf16[128,1024]{1,0:T(8,128)(2,1)S(1)}, bf16[128,1024]{1,0:T(8,128)(2,1)S(1)}, u32[]{:S(2)}, u32[]{:S(2)}) collective-permute-start(bf16[128,1024]{1,0:T(8,128)(2,1)S(1)} %get-tuple-element.238), channel_id=1, source_target_pairs={{0,2},{1,3},{2,0},{3,1},{4,6},{5,7},{6,4},{7,5},{8,10},{9,11},{10,... | collective-permute-start | bytes 786440 | tf_op jit(solution)/shard_map/ppermute | solution.py:24
  (29 other events, 295.0 us)
